TPU v7x, 512 devices: a whole 4x4x16 slice. The times are simulated.
512 devices in a mesh: dp: 32 (over y_lo, z), owner: 16 (over y_hi, x, core).
Axes of the slice: x: 4, y: 4 (y_hi: 2, y_lo: 2; y = y_hi * 2 + y_lo), z: 16, core: 2. Of those that a mesh axis runs over, the one named last changes fastest.
Arguments:
- tokens: bfloat16 [4096, 4096], P('dp'), may hold values from -6 to 6
- act_basis: bfloat16 [2, 4096, 4096], P(None, 'dp', 'owner'), may hold values from -0.09375 to 0.09375
- grad_basis: bfloat16 [2, 8192, 8192], P(None, 'owner', 'dp'), may hold values from -0.0625 to 0.0625
- grads: bfloat16 [2, 4096, 8192], P(None, 'dp', 'owner'), may hold values from -6 to 6
- expert_ids: int32 [4096, 2], P('dp'), may hold values from 0 to 7, all different within a row; in each aligned block of 128 rows (0 to 127, 128 to 255, ...) at most 64 rows name the same one
Outputs:
- corrected: float32 [2, 8192, 4096], P(None, 'dp', 'owner')
Inputs may be any that keep to these rules, and one draw needn't show every extreme that they name: `expert_ids`: among the 128 rows of one device no expert is named by more than 64 rows, a bound that some block reaches; the two experts of a row differ.
All inputs are finite; a program needn't handle non-finite values.
Results may differ from a plain program's by a relative error of at most 0.0013.
Values may be sent and summed in bfloat16 or wider, within the bound.
No kernel may reach another device: no remote copies, remote signals or barrier semaphores. Data moves between devices by JAX's collectives and lax.ppermute only.
A program may use at most 64 MiB of HBM per device.

v0:
```python
import jax
import jax.numpy as jnp
from jax import lax
from jax.sharding import PartitionSpec as P


def compact(expert_ids, tokens, grads, capacity):
    slot_order = jnp.arange(capacity, dtype=jnp.int32)[:, None]
    choosers = []
    for expert in range(grads.shape[0]):
        routed = jnp.any(expert_ids == expert, axis=1)
        slot_index = jnp.cumsum(routed.astype(jnp.int32)) - 1
        chosen = jnp.logical_and(routed[None, :], slot_index[None, :] == slot_order)
        choosers.append(chosen.astype(jnp.bfloat16))
    chooser = jnp.stack(choosers)
    picked_act = jnp.einsum(
        "ect,td->ecd", chooser, tokens, preferred_element_type=jnp.float32
    ).astype(jnp.bfloat16)
    picked_grad = jnp.einsum(
        "ect,etf->ecf", chooser, grads, preferred_element_type=jnp.float32
    ).astype(jnp.bfloat16)
    return (picked_act, picked_grad)


def correct(picked_act, picked_grad, act_basis, grad_basis, token_total):
    projected = jnp.einsum(
        "ecn,ena->eca",
        picked_act,
        lax.all_gather(act_basis, "dp", axis=1, tiled=True),
        preferred_element_type=jnp.float32,
    )
    act_all = lax.all_gather(projected.astype(jnp.bfloat16), "dp", axis=1, tiled=True)
    act_sq = jnp.square(act_all.astype(jnp.float32)).astype(jnp.bfloat16)
    grad_part = jnp.einsum(
        "erf,efk->erk",
        lax.all_gather(picked_grad, "dp", axis=1, tiled=True),
        grad_basis,
        preferred_element_type=jnp.float32,
    )
    grad_all = lax.psum(grad_part, "owner")
    grad_sq = jnp.square(grad_all).astype(jnp.bfloat16)
    return (
        jnp.einsum("erk,era->eka", grad_sq, act_sq, preferred_element_type=jnp.float32)
        / token_total
    )


def per_device(tokens, act_basis, grad_basis, grads, expert_ids):
    tok_rows = tokens.shape[0]
    capacity = tok_rows // 2
    token_total = tok_rows * lax.axis_size("dp")
    picked_act, picked_grad = compact(expert_ids, tokens, grads, capacity)
    results = []
    for expert in range(grads.shape[0]):
        results.append(
            correct(
                picked_act[expert : expert + 1],
                picked_grad[expert : expert + 1],
                act_basis[expert : expert + 1],
                grad_basis[expert : expert + 1],
                token_total,
            )
        )
    return jnp.concatenate(results, axis=0)


def solution(mesh):
    placed = (
        P("dp", None),
        P(None, "dp", "owner"),
        P(None, "owner", "dp"),
        P(None, "dp", "owner"),
        P("dp", None),
    )
    return jax.shard_map(
        per_device, mesh=mesh, in_specs=placed, out_specs=P(None, "dp", "owner"), check_vma=False
    )
```

profile of v0, /device:TPU:6, one launch (start us, length us, event | category | flops | bytes accessed | tf_op | source)
XLA Modules:
  0.0 967.6 jit_solution(10477772346757692174)
XLA Ops:
  6.5 1.6 fusion.27
  8.2 0.7 compare_reduce_fusion.1
  8.9 0.1 copy.9
  9.2 0.2 reduce-window.17
  9.3 0.2 reduce-window.16
  9.8 1.1 convolution_convert_fusion.1
  10.9 0.6 fusion.28
  11.6 0.7 all-gather.9.cloned.1.call-update
  12.3 0.5 all-gather.15.cloned.1.call-update
  12.9 0.4 convolution_convert_fusion
  13.4 134.1 %all-gather.11.cloned.1.call-done = bf16[1,4096,256]{2,1,0:T(8,128)(2,1)} async-done(((bf16[1,128,256]{2,1,0:T(8,128)(2,1)}), bf16[1,4096,256]{2,1,0:T(8,128)(2,1)}) %all-gather.11.cloned.1.call-update) | async-done | bytes 2097168 | tf_op jit(solution)/shard_map/all_gather | solution.py:29
  147.5 2.7 fusion.8
  150.2 126.3 %all-gather.13.cloned.1.call-done = bf16[1,2048,512]{2,1,0:T(8,128)(2,1)} async-done(((bf16[1,64,512]{2,1,0:T(8,128)(2,1)}), bf16[1,2048,512]{2,1,0:T(8,128)(2,1)}) %all-gather.13.cloned.1.call-update) | async-done | bytes 2097168 | tf_op jit(solution)/shard_map/all_gather | solution.py:36
  276.5 3.6 convolution_bitcast_fusion
  280.1 125.4 %all-gather.9.cloned.1.call-done = bf16[1,2048,512]{2,1,0:T(8,128)(2,1)} async-done(((bf16[1,64,512]{2,1,0:T(8,128)(2,1)}), bf16[1,2048,512]{2,1,0:T(8,128)(2,1)}) %all-gather.9.cloned.1.call-update) | async-done | bytes 2097168 | tf_op jit(solution)/shard_map/all_gather | solution.py:36
  405.6 3.7 convolution_bitcast_fusion.1
  409.3 125.2 %all-gather.15.cloned.1.call-done = bf16[1,4096,256]{2,1,0:T(8,128)(2,1)} async-done(((bf16[1,128,256]{2,1,0:T(8,128)(2,1)}), bf16[1,4096,256]{2,1,0:T(8,128)(2,1)}) %all-gather.15.cloned.1.call-update) | async-done | bytes 2097168 | tf_op jit(solution)/shard_map/all_gather | solution.py:29
  534.5 2.7 fusion.11
  537.2 124.4 %all-gather.17.cloned.1.call-done = bf16[2048,256]{1,0:T(8,128)(2,1)} async-done(((bf16[64,256]{1,0:T(8,128)(2,1)}), bf16[2048,256]{1,0:T(8,128)(2,1)}) %all-gather.17.cloned.1.call-update) | async-done | bytes 1048592 | tf_op jit(solution)/shard_map/all_gather | solution.py:32
  661.6 158.6 %all-reduce.3.cloned.1.call-done = (f32[1,2048,256]{2,1,0:T(8,128)}, f32[1,2048,256]{2,1,0:T(8,128)}) async-done(((f32[1,2048,256]{2,1,0:T(8,128)}, f32[1,2048,256]{2,1,0:T(8,128)}), (f32[1,2048,256]{2,1,0:T(8,128)}, f32[1,2048,256]{2,1,0:T(8,128)})) %all-reduce.3.cloned.1.call-update) | async-done | bytes 4194320 | tf_op jit(solution)/shard_map/psum | solution.py:40
  820.2 2.5 fusion.7
  822.7 135.5 %all-gather.19.cloned.1.call-done = bf16[2048,256]{1,0:T(8,128)(2,1)} async-done(((bf16[64,256]{1,0:T(8,128)(2,1)}), bf16[2048,256]{1,0:T(8,128)(2,1)}) %all-gather.19.cloned.1.call-update) | async-done | bytes 1048592 | tf_op jit(solution)/shard_map/all_gather | solution.py:32
  958.2 1.7 fusion.6
  959.9 0.8 pad_maximum_fusion
  (24 shorter events, 0.7 us)
Async XLA Ops:
  6.5 6.4 copy-start
  6.5 140.9 %all-gather.11.cloned.1.call-start = ((), (), s32[]{:S(2)}) async-start(), calls=%async_computation.1 | async-start | bytes 2162688 | tf_op jit(solution)/shard_map/all_gather | solution.py:29
  8.2 268.4 %all-gather.13.cloned.1.call-start = ((), (), s32[]{:S(2)}) async-start(), calls=%async_computation.2 | async-start | bytes 2162688 | tf_op jit(solution)/shard_map/all_gather | solution.py:36
  11.6 394.0 %all-gather.9.cloned.1.call-start = ((), (), s32[]{:S(2)}) async-start(), calls=%async_computation | async-start | bytes 2162688 | tf_op jit(solution)/shard_map/all_gather | solution.py:36
  12.3 522.2 %all-gather.15.cloned.1.call-start = ((), (), s32[]{:S(2)}) async-start(), calls=%async_computation.3 | async-start | bytes 2162688 | tf_op jit(solution)/shard_map/all_gather | solution.py:29
  12.9 263.6 %copy-start.2 = (bf16[2,512,256]{2,1,0:T(8,128)(2,1)S(1)}, bf16[2,512,256]{2,1,0:T(8,128)(2,1)}, u32[]{:S(2)}) copy-start(bf16[2,512,256]{2,1,0:T(8,128)(2,1)} %param.7) | copy-start | bytes 1572868
  12.9 648.7 %all-gather.17.cloned.1.call-start = ((), (), s32[]{:S(2)}) async-start(), calls=%async_computation.4 | async-start | bytes 1081344 | tf_op jit(solution)/shard_map/all_gather | solution.py:32
  150.2 670.1 %all-reduce.3.cloned.1.call-start = ((), (), s32[]{:S(2)}) async-start(), calls=%async_computation.6 | async-start | bytes 8388608 | tf_op jit(solution)/shard_map/psum | solution.py:40
  409.3 549.0 %all-gather.19.cloned.1.call-start = ((), (), s32[]{:S(2)}) async-start(), calls=%async_computation.5 | async-start | bytes 1081344 | tf_op jit(solution)/shard_map/all_gather | solution.py:32
  820.2 138.0 %copy-start.1 = (f32[1,2048,256]{2,1,0:T(8,128)S(1)}, f32[1,2048,256]{2,1,0:T(8,128)}, u32[]{:S(2)}) copy-start(f32[1,2048,256]{2,1,0:T(8,128)} %get-tuple-element.7) | copy-start | bytes 6291460
Sparse Core Ops, SparseCore 0:
  9.4 137.9 all-gather.10
  149.6 126.9 all-gather.12
  278.6 126.9 all-gather.8
  407.5 126.9 all-gather.14
  536.4 125.1 all-gather.16
  664.4 155.7 all-reduce.2
  822.3 135.8 all-gather.18
where the time goes:
time: 968 us
  waiting for transfers between devices  931 us (96%)
  matrix products  18.3 us (2%)
  between operations  13.6 us (1%)
    all_gather x2, waiting for transfers between devices, correct(): lax.all_gather(projected.astype(jnp.bfloat16), 'dp', axis=1, tiled=True)  260 us
    all_gather x2, waiting for transfers between devices, correct(): lax.all_gather(act_basis, 'dp', axis=1, tiled=True)  259 us
    all_gather x2, waiting for transfers between devices, correct(): lax.all_gather(picked_grad, 'dp', axis=1, tiled=True)  252 us
    psum x1, waiting for transfers between devices, correct(): grad_all = lax.psum(grad_part, 'owner')  159 us
  transfers between devices with their start and end apart: 7, of which 7 were waited for; matrix products, arithmetic and copies ran while one was open for 2% of the time, Pallas kernels for 0%

commit v1 on v0

v1 whole, which is shorter than its diff:
```python
import jax
import jax.numpy as jnp
from jax import lax
from jax.sharding import Mesh, PartitionSpec as P

F32, BF16 = jnp.float32, jnp.bfloat16
PLANE = ("yh", "x")


def choosers(expert_ids, experts, capacity):
    slot_order = jnp.arange(capacity, dtype=jnp.int32)[:, None]
    rows = expert_ids.shape[0]
    before = jnp.tril(jnp.ones((rows, rows), BF16))
    out = []
    for expert in range(experts):
        routed = jnp.any(expert_ids == expert, axis=1)
        count = jnp.dot(before, routed.astype(BF16)[:, None], preferred_element_type=F32)[:, 0]
        slot_index = count.astype(jnp.int32) - 1
        chosen = jnp.logical_and(routed[None, :], slot_index[None, :] == slot_order)
        out.append(chosen.astype(BF16))
    return out


def pick(chooser, rows):
    return jnp.dot(chooser, rows, preferred_element_type=F32).astype(BF16)


def swap(x, axis):
    return lax.ppermute(x, axis, [(0, 1), (1, 0)])


def dot(a, b):
    return jnp.dot(a, b, preferred_element_type=F32)


def per_device(tokens, act_basis, grad_basis, grads, expert_ids):
    tok_rows, width = tokens.shape
    capacity = tok_rows // 2
    nz = lax.axis_size("z")
    token_total = tok_rows * lax.axis_size("yl") * nz
    planes = lax.axis_size("yh") * lax.axis_size("x")
    yl, core = lax.axis_index("yl"), lax.axis_index("c")
    basis_rows, cols = act_basis.shape[1:]
    hidden = grads.shape[2]

    def mine(x):
        return lax.dynamic_index_in_dim(x, yl, 0, keepdims=False)

    def theirs(x):
        return lax.dynamic_index_in_dim(x, 1 - yl, 0, keepdims=False)

    act_other = swap(theirs(act_basis), "yl")
    choose = choosers(expert_ids, 2, capacity)
    picked_grad = jnp.stack([pick(choose[e], grads[e]) for e in range(2)])
    straight = [(2 * y + c, 2 * c + y) for y in range(2) for c in range(2)]
    crossed = [(2 * y + c, 2 * (1 - c) + y) for y in range(2) for c in range(2)]
    grad_a = lax.ppermute(
        lax.dynamic_index_in_dim(picked_grad, core, 0, keepdims=False), ("yl", "c"), straight
    )
    grad_b = lax.ppermute(
        lax.dynamic_index_in_dim(picked_grad, 1 - core, 0, keepdims=False), ("yl", "c"), crossed
    )
    act_rows = jnp.concatenate([mine(act_basis), act_other], axis=1)
    payload = jnp.concatenate([act_rows, grad_a, grad_b], axis=0)
    gathered = lax.all_gather(payload, "z", axis=0, tiled=False)

    picked_act = jnp.stack([pick(choose[e], tokens) for e in range(2)])
    act_in, act_in_other = mine(picked_act), swap(theirs(picked_act), "yl")
    first = jnp.where(yl == core, act_in, act_in_other)
    second = jnp.where(yl == core, act_in_other, act_in)
    rows = jnp.concatenate([first, second], axis=0)
    low, high = rows[:, : width // 2], rows[:, width // 2 :]
    rows_own = jnp.where(yl == 0, low, high)
    rows_other = jnp.where(yl == 0, high, low)
    basis_half = jnp.concatenate([mine(grad_basis), swap(theirs(grad_basis), "yl")], axis=1)
    basis_peer = swap(basis_half, "c")
    basis_a = jnp.where(yl == core, basis_half, basis_peer)
    basis_b = jnp.where(yl == core, basis_peer, basis_half)

    own_basis = gathered[:, :basis_rows, :cols].reshape(nz * basis_rows, cols)
    other_basis = gathered[:, :basis_rows, cols:].reshape(nz * basis_rows, cols)
    act_proj = (dot(rows_own, own_basis) + dot(rows_other, other_basis)).astype(BF16)
    act_all = lax.all_gather(act_proj, "z", axis=0, tiled=False)

    got_a = gathered[:, basis_rows : basis_rows + capacity].reshape(nz * capacity, hidden)
    got_b = gathered[:, basis_rows + capacity :].reshape(nz * capacity, hidden)
    part = dot(got_a, basis_a) + dot(got_b, basis_b)
    share = part.shape[0] // planes
    parts = lax.all_to_all(part.reshape(planes, share, -1), PLANE, 0, 0, tiled=True)
    grad_sq = jnp.square(jnp.sum(parts, axis=0)).astype(BF16)
    copies = jnp.broadcast_to(grad_sq[None], (planes,) + grad_sq.shape)
    grad_sq = lax.all_to_all(copies, PLANE, 0, 0, tiled=True).reshape(nz * capacity, -1)
    grad_sq_other = swap(grad_sq, "c")

    act_sq = jnp.square(act_all.astype(F32)).astype(BF16)
    act_first = act_sq[:, :capacity].reshape(nz * capacity, cols)
    act_second = act_sq[:, capacity:].reshape(nz * capacity, cols)

    def outer(g, a):
        return lax.dot_general(g, a, (((0,), (0,)), ((), ())), preferred_element_type=F32)

    block = (outer(grad_sq, act_first) + outer(grad_sq_other, act_second)) / token_total
    half = block.shape[0] // 2
    kept, got = block[:half], swap(block[half:], "yl")
    return jnp.stack([jnp.where(yl == 0, kept, got), jnp.where(yl == 0, got, kept)])


def solution(mesh):
    dp, owner = mesh.devices.shape
    split = Mesh(mesh.devices.reshape(2, dp // 2, 2, owner // 4, 2), ("yl", "z", "yh", "x", "c"))
    rows, cols = ("yl", "z"), ("yh", "x", "c")
    placed = (
        P(rows, None),
        P(None, rows, cols),
        P(None, cols, rows),
        P(None, rows, cols),
        P(rows, None),
    )
    return jax.shard_map(
        per_device, mesh=split, in_specs=placed, out_specs=P(None, rows, cols), check_vma=False
    )
```

time: 968 us -> 210 us (0.22)
  waiting for transfers between devices: 931 us -> 131 us
  starting transfers between devices: 0.25 us -> 27.2 us
  blocking collectives: 0 us -> 17.3 us
  matrix products: 18.3 us -> 8.1 us
    all_gather x6 -> x2, waiting for transfers between devices: 771 us -> 101 us  [the longest x1 67.5 us: per_device(): gathered = lax.all_gather(payload, 'z', axis=0, tiled=False)]
    psum x1 -> x0, waiting for transfers between devices: 159 us -> none  [correct(): grad_all = lax.psum(grad_part, 'owner')]
    ppermute x0 -> x8, starting transfers between devices: none -> 20 us  [the longest x6 14.6 us: swap(): return lax.ppermute(x, axis, [(0, 1), (1, 0)])]
    all_to_all x0 -> x1, blocking collectives: none -> 17.3 us  [per_device(): lax.all_to_all(copies, PLANE, 0, 0, tiled=True).reshape(nz * capacity, -1)]
    ppermute x0 -> x8, waiting for transfers between devices: none -> 15.7 us  [the longest x6 15.7 us: swap(): return lax.ppermute(x, axis, [(0, 1), (1, 0)])]
    all_to_all x0 -> x1, waiting for transfers between devices: none -> 14.3 us  [per_device(): lax.all_to_all(part.reshape(planes, share, -1), PLANE, 0, 0, tiled=True)]
    dot_general x8 -> x12, matrix products: 18.3 us -> 8.1 us  [the longest x4 4.13 us: dot(): return jnp.dot(a, b, preferred_element_type=F32)]
  transfers between devices with their start and end apart: 7 -> 11, of which waited for: 7 -> 6; matrix products, arithmetic and copies ran while one was open for 2% -> 7% of each run, Pallas kernels for 0% -> 0%
where the time goes in v1:
time: 210 us; the launch traced here: 209 us
  waiting for transfers between devices  131 us (62%)
  starting transfers between devices  27.2 us (13%)
  blocking collectives  17.3 us (8%)
  between operations  13.7 us (7%)
  matrix products  8.1 us (4%)
  other arithmetic  6.97 us (3%)
  local copies, waits for them, and re-layouts  4.64 us (2%)
    all_gather x1, waiting for transfers between devices, per_device(): gathered = lax.all_gather(payload, 'z', axis=0, tiled=False)  67.5 us
    all_gather x1, waiting for transfers between devices, per_device(): act_all = lax.all_gather(act_proj, 'z', axis=0, tiled=False)  33.9 us
    all_to_all x1, blocking collectives, per_device(): lax.all_to_all(copies, PLANE, 0, 0, tiled=True).reshape(nz * capacity, -1)  17.3 us
    ppermute x6, waiting for transfers between devices, swap(): return lax.ppermute(x, axis, [(0, 1), (1, 0)])  15.7 us
    ppermute x6, starting transfers between devices, swap(): return lax.ppermute(x, axis, [(0, 1), (1, 0)])  14.6 us
    all_to_all x1, waiting for transfers between devices, per_device(): lax.all_to_all(part.reshape(planes, share, -1), PLANE, 0, 0, tiled=True)  14.3 us
    all_to_all x1, starting transfers between devices, per_device(): lax.all_to_all(part.reshape(planes, share, -1), PLANE, 0, 0, tiled=True)  7.25 us
    ppermute x1, starting transfers between devices, per_device(): lax.ppermute(lax.dynamic_index_in_dim(picked_grad, 1 - core, 0, keepdims=...  4.74 us
  transfers between devices with their start and end apart: 11, of which 6 were waited for; matrix products, arithmetic and copies ran while one was open for 7% of the time, Pallas kernels for 0%

profile of v1, /device:TPU:6, one launch (start us, length us, event | category | flops | bytes accessed | tf_op | source)
XLA Modules:
  0.0 209.3 jit_solution(10135935943564768892)
XLA Ops:
  7.6 1.1 fusion.4
  8.7 1.1 fusion.5
  10.5 4.7 %collective-permute-start.2 = (bf16[64,512]{1,0:T(8,128)(2,1)S(1)}, bf16[64,512]{1,0:T(8,128)(2,1)S(1)}, u32[]{:S(2)}, u32[]{:S(2)}) collective-permute-start(bf16[64,512]{1,0:T(8,128)(2,1)S(1)} %get-tuple-element.22), channel_id=1, source_target_pairs={{0,256},{1,0},{256,257},{257,1},{2,258},{3,2},{258,259},{259,3},{4... | collective-permute-start | bytes 196616 | tf_op jit(solution)/shard_map/ppermute | solution.py:60
  16.2 1.9 collective-permute-start
  18.1 4.2 %collective-permute-done = bf16[128,256]{1,0:T(8,128)(2,1)S(1)} collective-permute-done((bf16[128,256]{1,0:T(8,128)(2,1)S(1)}, bf16[128,256]{1,0:T(8,128)(2,1)S(1)}, u32[]{:S(2)}, u32[]{:S(2)}) %collective-permute-start) | collective-permute-done | bytes 65568 | tf_op jit(solution)/shard_map/ppermute | solution.py:29
  23.2 1.9 collective-permute-start.3
  25.7 6.5 %collective-permute-done.3 = bf16[512,256]{1,0:T(8,128)(2,1)S(1)} collective-permute-done((bf16[512,256]{1,0:T(8,128)(2,1)S(1)}, bf16[512,256]{1,0:T(8,128)(2,1)S(1)}, u32[]{:S(2)}, u32[]{:S(2)}) %collective-permute-start.3) | collective-permute-done | bytes 262176 | tf_op jit(solution)/shard_map/ppermute | solution.py:29
  32.3 1.9 collective-permute-start.4
  34.2 1.0 fusion.12
  35.2 3.6 %collective-permute-start.5 = (bf16[64,4096]{1,0:T(8,128)(2,1)}, bf16[64,4096]{1,0:T(8,128)(2,1)}, u32[]{:S(2)}, u32[]{:S(2)}) collective-permute-start(bf16[64,4096]{1,0:T(8,128)(2,1)} %fusion.12), channel_id=1, source_target_pairs={{0,256},{256,0},{1,257},{257,1},{2,258},{258,2},{3,259},{259,3},{4... | collective-permute-start | bytes 1572872 | tf_op jit(solution)/shard_map/ppermute | solution.py:29
  38.9 67.5 %all-gather.5.cloned.1.call-done = bf16[4096,512]{1,0:T(8,128)(2,1)} async-done(((bf16[256,512]{1,0:T(8,128)(2,1)}), bf16[4096,512]{1,0:T(8,128)(2,1)}) %all-gather.5.cloned.1.call-update) | async-done | bytes 4194320 | tf_op jit(solution)/shard_map/all_gather | solution.py:65
  106.3 1.8 fusion.65
  108.9 2.1 %convolution_add_fusion = f32[1024,512]{1,0:T(8,128)} fusion(f32[1024,512]{1,0:T(8,128)S(1)} %fusion.18, bf16[1024,512]{1,0:T(8,128)(2,1)S(1)} %bitcast.78, bf16[512,512]{1,0:T(8,128)(2,1)S(1)} %collective-permute-done.4, pred[]{:T(512)S(6)} %eq.61, bf16[512,256]{1,0:T(8,128)(2,1)S(1)} %collective-permute-done.3, bf16[512,256]{1,0:T(8,128)(2,1)S(1)} %get-tuple-element.17), kind=kOutput, calls=%fused_computation.5 | convolution fusion | flops 538705920 | bytes 6291457 | tf_op jit(solution)/shard_map/dot_general | solution.py:33
  111.0 7.2 %all-to-all-start = ((f32[8,128,512]{2,1,0:T(8,128)}), f32[8,128,512]{2,1,0:T(8,128)S(1)}, u32[]{:S(2)}, u32[]{:S(2)}) async-start(f32[8,128,512]{2,1,0:T(8,128)} %bitcast.17), calls=%async_computation | async-start | bytes 4194304 | tf_op jit(solution)/shard_map/all_to_all | solution.py:89
  118.2 1.8 broadcast_select_fusion.1
  120.0 1.7 fusion.64
  122.1 1.0 fusion.3
  123.0 14.3 %all-to-all-done = f32[8,128,512]{2,1,0:T(8,128)S(1)} async-done(((f32[8,128,512]{2,1,0:T(8,128)}), f32[8,128,512]{2,1,0:T(8,128)S(1)}, u32[]{:S(2)}, u32[]{:S(2)}) %all-to-all-start) | async-done | bytes 2097184 | tf_op jit(solution)/shard_map/all_to_all | solution.py:89
  137.7 17.3 %all_to_all.10 = bf16[8,128,512]{2,1,0:T(8,128)(2,1)S(1)} all-to-all(bf16[8,128,512]{2,1,0:T(8,128)(2,1)S(1)} %broadcast_in_dim.10), channel_id=1, replica_groups=mesh['yl'=2,'z'=16,'yh'=2,'x'=4,'c'=2] {'yh','x'}, dimensions={0} | all-to-all | bytes 2097152 | tf_op jit(solution)/shard_map/all_to_all | solution.py:92
  155.0 1.9 collective-permute-start.6
  156.9 33.9 %all-gather.7.cloned.1.call-done = bf16[2048,256]{1,0:T(8,128)(2,1)} async-done(((bf16[128,256]{1,0:T(8,128)(2,1)}), bf16[2048,256]{1,0:T(8,128)(2,1)}) %all-gather.7.cloned.1.call-update) | async-done | bytes 1048592 | tf_op jit(solution)/shard_map/all_gather | solution.py:83
  190.8 1.4 multiply_convert_fusion
  193.3 3.3 %collective-permute-start.7 = (f32[256,256]{1,0:T(8,128)S(1)}, f32[256,256]{1,0:T(8,128)S(1)}, u32[]{:S(2)}, u32[]{:S(2)}) collective-permute-start(f32[256,256]{1,0:T(8,128)S(1)} %slice.57), channel_id=1, source_target_pairs={{0,256},{256,0},{1,257},{257,1},{2,258},{258,2},{3,259},{259,3},{4... | collective-permute-start | bytes 786440 | tf_op jit(solution)/shard_map/ppermute | solution.py:29
  196.6 5.0 %collective-permute-done.7 = f32[256,256]{1,0:T(8,128)S(1)} collective-permute-done((f32[256,256]{1,0:T(8,128)S(1)}, f32[256,256]{1,0:T(8,128)S(1)}, u32[]{:S(2)}, u32[]{:S(2)}) %collective-permute-start.7) | collective-permute-done | bytes 262176 | tf_op jit(solution)/shard_map/ppermute | solution.py:29
  (39 shorter events, 7.5 us)
Async XLA Ops:
  6.5 18.6 %copy-start = (bf16[128,4096]{1,0:T(8,128)(2,1)S(1)}, bf16[128,4096]{1,0:T(8,128)(2,1)}, u32[]{:S(2)}) copy-start(bf16[128,4096]{1,0:T(8,128)(2,1)} %param.5) | copy-start | bytes 3145732
  6.5 16.6 %copy-start.3 = (bf16[2,512,256]{2,1,0:T(8,128)(2,1)S(1)}, bf16[2,512,256]{2,1,0:T(8,128)(2,1)}, u32[]{:S(2)}) copy-start(bf16[2,512,256]{2,1,0:T(8,128)(2,1)} %param.7) | copy-start | bytes 1572868
  6.5 99.8 %all-gather.5.cloned.1.call-start = ((), (), s32[]{:S(2)}) async-start(), calls=%async_computation.2 | async-start | bytes 4456448 | tf_op jit(solution)/shard_map/all_gather | solution.py:65
  9.9 8.2 %collective-permute-start.1 = (bf16[64,512]{1,0:T(8,128)(2,1)S(1)}, bf16[64,512]{1,0:T(8,128)(2,1)S(1)}, u32[]{:S(2)}, u32[]{:S(2)}) collective-permute-start(bf16[64,512]{1,0:T(8,128)(2,1)S(1)} %get-tuple-element.21), channel_id=1, source_target_pairs={{0,0},{1,256},{256,1},{257,257},{2,2},{3,258},{258,3},{259,259},{4... | collective-permute-start | bytes 196616 | tf_op jit(solution)/shard_map/ppermute | solution.py:57
  10.5 7.6 %collective-permute-start.2 = (bf16[64,512]{1,0:T(8,128)(2,1)S(1)}, bf16[64,512]{1,0:T(8,128)(2,1)S(1)}, u32[]{:S(2)}, u32[]{:S(2)}) collective-permute-start(bf16[64,512]{1,0:T(8,128)(2,1)S(1)} %get-tuple-element.22), channel_id=1, source_target_pairs={{0,256},{1,0},{256,257},{257,1},{2,258},{3,2},{258,259},{259,3},{4... | collective-permute-start | bytes 196616 | tf_op jit(solution)/shard_map/ppermute | solution.py:60
  16.2 6.2 %collective-permute-start = (bf16[128,256]{1,0:T(8,128)(2,1)S(1)}, bf16[128,256]{1,0:T(8,128)(2,1)S(1)}, u32[]{:S(2)}, u32[]{:S(2)}) collective-permute-start(bf16[128,256]{1,0:T(8,128)(2,1)S(1)} %get-tuple-element.20), channel_id=1, source_target_pairs={{0,256},{256,0},{1,257},{257,1},{2,258},{258,2},{3,259},{259,3},{4... | collective-permute-start | bytes 196616 | tf_op jit(solution)/shard_map/ppermute | solution.py:29
  23.2 9.1 %collective-permute-start.3 = (bf16[512,256]{1,0:T(8,128)(2,1)S(1)}, bf16[512,256]{1,0:T(8,128)(2,1)S(1)}, u32[]{:S(2)}, u32[]{:S(2)}) collective-permute-start(bf16[512,256]{1,0:T(8,128)(2,1)S(1)} %get-tuple-element.18), channel_id=1, source_target_pairs={{0,256},{256,0},{1,257},{257,1},{2,258},{258,2},{3,259},{259,3},{4... | collective-permute-start | bytes 786440 | tf_op jit(solution)/shard_map/ppermute | solution.py:29
  25.4 9.8 %copy-start.1 = (bf16[1,64,4096]{2,1,0:T(8,128)(2,1)}, bf16[1,64,4096]{2,1,0:T(8,128)(2,1)S(1)}, u32[]{:S(2)}) copy-start(bf16[1,64,4096]{2,1,0:T(8,128)(2,1)S(1)} %fusion) | copy-start | bytes 1572868
  25.7 8.5 %copy-start.2 = (bf16[1,64,4096]{2,1,0:T(8,128)(2,1)}, bf16[1,64,4096]{2,1,0:T(8,128)(2,1)S(1)}, u32[]{:S(2)}) copy-start(bf16[1,64,4096]{2,1,0:T(8,128)(2,1)S(1)} %fusion.1) | copy-start | bytes 1572868
  32.3 75.8 %collective-permute-start.4 = (bf16[512,512]{1,0:T(8,128)(2,1)S(1)}, bf16[512,512]{1,0:T(8,128)(2,1)S(1)}, u32[]{:S(2)}, u32[]{:S(2)}) collective-permute-start(bf16[512,512]{1,0:T(8,128)(2,1)S(1)} %pad_maximum_fusion.1), channel_id=1, source_target_pairs={{0,1},{1,0},{2,3},{3,2},{4,5},{5,4},{6,7},{7,6},{8,9},{9,8},{10,11... | collective-permute-start | bytes 1572872 | tf_op jit(solution)/shard_map/ppermute | solution.py:29
  35.2 83.0 %collective-permute-start.5 = (bf16[64,4096]{1,0:T(8,128)(2,1)}, bf16[64,4096]{1,0:T(8,128)(2,1)}, u32[]{:S(2)}, u32[]{:S(2)}) collective-permute-start(bf16[64,4096]{1,0:T(8,128)(2,1)} %fusion.12), channel_id=1, source_target_pairs={{0,256},{256,0},{1,257},{257,1},{2,258},{258,2},{3,259},{259,3},{4... | collective-permute-start | bytes 1572872 | tf_op jit(solution)/shard_map/ppermute | solution.py:29
  111.0 26.4 %all-to-all-start = ((f32[8,128,512]{2,1,0:T(8,128)}), f32[8,128,512]{2,1,0:T(8,128)S(1)}, u32[]{:S(2)}, u32[]{:S(2)}) async-start(f32[8,128,512]{2,1,0:T(8,128)} %bitcast.17), calls=%async_computation | async-start | bytes 4194304 | tf_op jit(solution)/shard_map/all_to_all | solution.py:89
  118.2 72.5 %all-gather.7.cloned.1.call-start = ((), (), s32[]{:S(2)}) async-start(), calls=%async_computation.3 | async-start | bytes 1114112 | tf_op jit(solution)/shard_map/all_gather | solution.py:83
  155.0 37.8 %collective-permute-start.6 = (bf16[1024,512]{1,0:T(8,128)(2,1)S(1)}, bf16[1024,512]{1,0:T(8,128)(2,1)S(1)}, u32[]{:S(2)}, u32[]{:S(2)}) collective-permute-start(bf16[1024,512]{1,0:T(8,128)(2,1)S(1)} %bitcast.82), channel_id=1, source_target_pairs={{0,1},{1,0},{2,3},{3,2},{4,5},{5,4},{6,7},{7,6},{8,9},{9,8},{10,11... | collective-permute-start | bytes 3145736 | tf_op jit(solution)/shard_map/ppermute | solution.py:29
  193.3 8.3 %collective-permute-start.7 = (f32[256,256]{1,0:T(8,128)S(1)}, f32[256,256]{1,0:T(8,128)S(1)}, u32[]{:S(2)}, u32[]{:S(2)}) collective-permute-start(f32[256,256]{1,0:T(8,128)S(1)} %slice.57), channel_id=1, source_target_pairs={{0,256},{256,0},{1,257},{257,1},{2,258},{258,2},{3,259},{259,3},{4... | collective-permute-start | bytes 786440 | tf_op jit(solution)/shard_map/ppermute | solution.py:29
Sparse Core Ops, SparseCore 0:
  23.2 83.0 all-gather.4
  123.2 67.5 all-gather.6

commit v2 on v1

--- a/solution.py
+++ b/solution.py
@@ -36,7 +36,8 @@
 def per_device(tokens, act_basis, grad_basis, grads, expert_ids):
     tok_rows, width = tokens.shape
     capacity = tok_rows // 2
-    nz = lax.axis_size("z")
+    nl = lax.axis_size("zl")
+    nz = lax.axis_size("zh") * nl
     token_total = tok_rows * lax.axis_size("yl") * nz
     planes = lax.axis_size("yh") * lax.axis_size("x")
     yl, core = lax.axis_index("yl"), lax.axis_index("c")
@@ -62,16 +63,23 @@
     )
     act_rows = jnp.concatenate([mine(act_basis), act_other], axis=1)
     payload = jnp.concatenate([act_rows, grad_a, grad_b], axis=0)
-    gathered = lax.all_gather(payload, "z", axis=0, tiled=False)
+    gathered = lax.all_gather(payload, ("zh", "zl"), axis=0, tiled=False)
 
-    picked_act = jnp.stack([pick(choose[e], tokens) for e in range(2)])
+    plane = lax.axis_index("yh") * lax.axis_size("x") + lax.axis_index("x")
+    share = width // (2 * planes)
+    piece = lax.dynamic_slice_in_dim(tokens, core * (width // 2) + plane * share, share, 1)
+    picked_act = jnp.stack([pick(choose[e], piece) for e in range(2)])
     act_in, act_in_other = mine(picked_act), swap(theirs(picked_act), "yl")
-    first = jnp.where(yl == core, act_in, act_in_other)
-    second = jnp.where(yl == core, act_in_other, act_in)
-    rows = jnp.concatenate([first, second], axis=0)
-    low, high = rows[:, : width // 2], rows[:, width // 2 :]
-    rows_own = jnp.where(yl == 0, low, high)
-    rows_other = jnp.where(yl == 0, high, low)
+    rows = jnp.concatenate(
+        [jnp.where(yl == 0, act_in, act_in_other), jnp.where(yl == 0, act_in_other, act_in)], axis=0
+    )
+    rows = lax.all_gather(rows, "zh", axis=0, tiled=True)
+    copies = jnp.broadcast_to(rows[None], (planes,) + rows.shape)
+    rows = lax.all_to_all(copies, PLANE, 0, 0, tiled=True)
+    rows = rows.transpose(1, 0, 2).reshape(rows.shape[1], planes * share)
+    rows_peer = swap(rows, "c")
+    rows_own = jnp.where(yl == core, rows, rows_peer)
+    rows_other = jnp.where(yl == core, rows_peer, rows)
     basis_half = jnp.concatenate([mine(grad_basis), swap(theirs(grad_basis), "yl")], axis=1)
     basis_peer = swap(basis_half, "c")
     basis_a = jnp.where(yl == core, basis_half, basis_peer)
@@ -80,21 +88,23 @@
     own_basis = gathered[:, :basis_rows, :cols].reshape(nz * basis_rows, cols)
     other_basis = gathered[:, :basis_rows, cols:].reshape(nz * basis_rows, cols)
     act_proj = (dot(rows_own, own_basis) + dot(rows_other, other_basis)).astype(BF16)
-    act_all = lax.all_gather(act_proj, "z", axis=0, tiled=False)
-
     got_a = gathered[:, basis_rows : basis_rows + capacity].reshape(nz * capacity, hidden)
     got_b = gathered[:, basis_rows + capacity :].reshape(nz * capacity, hidden)
+    act_proj, got_a, got_b = lax.optimization_barrier((act_proj, got_a, got_b))
+    act_all = lax.all_gather(act_proj, "zl", axis=0, tiled=False)
+
     part = dot(got_a, basis_a) + dot(got_b, basis_b)
-    share = part.shape[0] // planes
-    parts = lax.all_to_all(part.reshape(planes, share, -1), PLANE, 0, 0, tiled=True)
+    parts = lax.all_to_all(part.reshape(planes, part.shape[0] // planes, -1), PLANE, 0, 0, tiled=True)
     grad_sq = jnp.square(jnp.sum(parts, axis=0)).astype(BF16)
     copies = jnp.broadcast_to(grad_sq[None], (planes,) + grad_sq.shape)
     grad_sq = lax.all_to_all(copies, PLANE, 0, 0, tiled=True).reshape(nz * capacity, -1)
     grad_sq_other = swap(grad_sq, "c")
 
     act_sq = jnp.square(act_all.astype(F32)).astype(BF16)
-    act_first = act_sq[:, :capacity].reshape(nz * capacity, cols)
-    act_second = act_sq[:, capacity:].reshape(nz * capacity, cols)
+    act_sq = act_sq.reshape(nl, nz // nl, 2, capacity, cols).transpose(2, 1, 0, 3, 4)
+    act_sq = act_sq.reshape(2, nz * capacity, cols)
+    act_first = lax.dynamic_index_in_dim(act_sq, core, 0, keepdims=False)
+    act_second = lax.dynamic_index_in_dim(act_sq, 1 - core, 0, keepdims=False)
 
     def outer(g, a):
         return lax.dot_general(g, a, (((0,), (0,)), ((), ())), preferred_element_type=F32)
@@ -107,8 +117,10 @@
 
 def solution(mesh):
     dp, owner = mesh.devices.shape
-    split = Mesh(mesh.devices.reshape(2, dp // 2, 2, owner // 4, 2), ("yl", "z", "yh", "x", "c"))
-    rows, cols = ("yl", "z"), ("yh", "x", "c")
+    split = Mesh(
+        mesh.devices.reshape(2, dp // 8, 4, 2, owner // 4, 2), ("yl", "zh", "zl", "yh", "x", "c")
+    )
+    rows, cols = ("yl", "zh", "zl"), ("yh", "x", "c")
     placed = (
         P(rows, None),
         P(None, rows, cols),

time: 210 us -> 198 us (0.943)
  waiting for transfers between devices: 131 us -> 52.8 us
  blocking collectives: 17.3 us -> 78.1 us
  matrix products: 8.1 us -> 12.1 us
  local copies, waits for them, and re-layouts: 4.64 us -> 7.32 us
    all_gather x2, waiting for transfers between devices: 101 us -> 2.01 us  [the longest x1 1.99 us: per_device(): gathered = lax.all_gather(payload, ('zh', 'zl'), axis=0, tiled=False)]
    all_gather x0 -> x1, blocking collectives: none -> 28.9 us  [per_device(): rows = lax.all_gather(rows, 'zh', axis=0, tiled=True)]
    all_to_all x0 -> x1, blocking collectives: none -> 28.7 us  [per_device(): rows = lax.all_to_all(copies, PLANE, 0, 0, tiled=True)]
    all_to_all x1, waiting for transfers between devices: 14.3 us -> 25 us  [per_device(): lax.all_to_all(part.reshape(planes, part.shape[0] // planes, -1), PLANE,...]
    ppermute x6 -> x7, waiting for transfers between devices: 15.7 us -> 25 us  [swap(): return lax.ppermute(x, axis, [(0, 1), (1, 0)])]
    dot_general x4, matrix products: 4.13 us -> 8.45 us  [dot(): return jnp.dot(a, b, preferred_element_type=F32)]
    all_to_all x1, blocking collectives: 17.3 us -> 20.5 us  [per_device(): lax.all_to_all(copies, PLANE, 0, 0, tiled=True).reshape(nz * capacity, -1)]
    all_to_all x0 -> x1, local copies, waits for them, and re-layouts: none -> 2.45 us  [per_device(): rows = lax.all_to_all(copies, PLANE, 0, 0, tiled=True)]
  transfers between devices with their start and end apart: 11 -> 12, of which waited for: 6 -> 7; matrix products, arithmetic and copies ran while one was open for 7% -> 7% of each run, Pallas kernels for 0% -> 0%
where the time goes in v2:
time: 198 us; the launch traced here: 195 us
  blocking collectives  78.1 us (39%)
  waiting for transfers between devices  52.8 us (27%)
  starting transfers between devices  26.2 us (13%)
  between operations  13.7 us (7%)
  matrix products  12.1 us (6%)
  local copies, waits for them, and re-layouts  7.32 us (4%)
  other arithmetic  5.03 us (3%)
    all_gather x1, blocking collectives, per_device(): rows = lax.all_gather(rows, 'zh', axis=0, tiled=True)  28.9 us
    all_to_all x1, blocking collectives, per_device(): rows = lax.all_to_all(copies, PLANE, 0, 0, tiled=True)  28.7 us
    all_to_all x1, waiting for transfers between devices, per_device(): lax.all_to_all(part.reshape(planes, part.shape[0] // planes, -1), PLANE,...  25 us
    ppermute x7, waiting for transfers between devices, swap(): return lax.ppermute(x, axis, [(0, 1), (1, 0)])  25 us
    all_to_all x1, blocking collectives, per_device(): lax.all_to_all(copies, PLANE, 0, 0, tiled=True).reshape(nz * capacity, -1)  20.5 us
    ppermute x7, starting transfers between devices, swap(): return lax.ppermute(x, axis, [(0, 1), (1, 0)])  14.1 us
    dot_general x4, matrix products, dot(): return jnp.dot(a, b, preferred_element_type=F32)  8.45 us
    all_to_all x1, starting transfers between devices, per_device(): lax.all_to_all(part.reshape(planes, part.shape[0] // planes, -1), PLANE,...  6.77 us
  transfers between devices with their start and end apart: 12, of which 7 were waited for; matrix products, arithmetic and copies ran while one was open for 7% of the time, Pallas kernels for 0%

profile of v2, /device:TPU:6, one launch (start us, length us, event | category | flops | bytes accessed | tf_op | source)
XLA Modules:
  0.0 195.3 jit_solution(15065543036265567578)
XLA Ops:
  10.5 4.7 %collective-permute-start.4 = (bf16[64,512]{1,0:T(8,128)(2,1)S(1)}, bf16[64,512]{1,0:T(8,128)(2,1)S(1)}, u32[]{:S(2)}, u32[]{:S(2)}) collective-permute-start(bf16[64,512]{1,0:T(8,128)(2,1)S(1)} %get-tuple-element.24), channel_id=1, source_target_pairs={{0,256},{1,0},{256,257},{257,1},{2,258},{3,2},{258,259},{259,3},{4... | collective-permute-start | bytes 196616 | tf_op jit(solution)/shard_map/ppermute | solution.py:61
  16.1 1.9 collective-permute-start.2
  18.1 4.2 %collective-permute-done.2 = bf16[128,256]{1,0:T(8,128)(2,1)S(1)} collective-permute-done((bf16[128,256]{1,0:T(8,128)(2,1)S(1)}, bf16[128,256]{1,0:T(8,128)(2,1)S(1)}, u32[]{:S(2)}, u32[]{:S(2)}) %collective-permute-start.2) | collective-permute-done | bytes 65568 | tf_op jit(solution)/shard_map/ppermute | solution.py:29
  23.4 1.9 collective-permute-start
  25.3 3.9 %collective-permute-done = bf16[64,256]{1,0:T(8,128)(2,1)S(1)} collective-permute-done((bf16[64,256]{1,0:T(8,128)(2,1)S(1)}, bf16[64,256]{1,0:T(8,128)(2,1)S(1)}, u32[]{:S(2)}, u32[]{:S(2)}) %collective-permute-start) | collective-permute-done | bytes 32800 | tf_op jit(solution)/shard_map/ppermute | solution.py:29
  29.2 28.9 %all_gather.15 = bf16[512,256]{1,0:T(8,128)(2,1)S(1)} all-gather(bf16[128,256]{1,0:T(8,128)(2,1)S(1)} %pad_maximum_fusion.3), channel_id=1, replica_groups=mesh['yl'=2,'zh'=4,'zl'=4,'yh'=2,'x'=4,'c'=2] {'zh'}, dimensions={0}, use_global_device_ids=true | all-gather | bytes 327680 | tf_op jit(solution)/shard_map/all_gather | solution.py:76
  58.3 28.7 %all_to_all.15 = bf16[8,512,256]{2,1,0:T(8,128)(2,1)S(1)} all-to-all(bf16[8,512,256]{2,1,0:T(8,128)(2,1)S(1)} %broadcast_in_dim.12), channel_id=1, replica_groups=mesh['yl'=2,'zh'=4,'zl'=4,'yh'=2,'x'=4,'c'=2] {'yh','x'}, dimensions={0} | all-to-all | bytes 4194304 | tf_op jit(solution)/shard_map/all_to_all | solution.py:78
  87.0 2.5 %copy.8 = bf16[8,512,256]{1,2,0:T(8,128)(2,1)} copy(bf16[8,512,256]{2,1,0:T(8,128)(2,1)S(1)} %all_to_all.15) | data formatting | bytes 4194304 | tf_op jit(solution)/shard_map/all_to_all | solution.py:78
  89.4 1.9 collective-permute-start.1
  92.4 2.6 %collective-permute-start.5 = (bf16[512,256]{1,0:T(8,128)(2,1)S(1)}, bf16[512,256]{1,0:T(8,128)(2,1)S(1)}, u32[]{:S(2)}, u32[]{:S(2)}) collective-permute-start(bf16[512,256]{1,0:T(8,128)(2,1)S(1)} %get-tuple-element.20), channel_id=1, source_target_pairs={{0,256},{256,0},{1,257},{257,1},{2,258},{258,2},{3,259},{259,3},{4... | collective-permute-start | bytes 786440 | tf_op jit(solution)/shard_map/ppermute | solution.py:29
  95.0 8.0 %collective-permute-done.5 = bf16[512,256]{1,0:T(8,128)(2,1)S(1)} collective-permute-done((bf16[512,256]{1,0:T(8,128)(2,1)S(1)}, bf16[512,256]{1,0:T(8,128)(2,1)S(1)}, u32[]{:S(2)}, u32[]{:S(2)}) %collective-permute-start.5) | collective-permute-done | bytes 262176 | tf_op jit(solution)/shard_map/ppermute | solution.py:29
  103.9 1.9 collective-permute-start.6
  105.8 2.0 %all-gather.5.cloned.1.call-done = bf16[4096,512]{1,0:T(8,128)(2,1)} async-done(((bf16[256,512]{1,0:T(8,128)(2,1)}), bf16[4096,512]{1,0:T(8,128)(2,1)}) %all-gather.5.cloned.1.call-update) | async-done | bytes 4194320 | tf_op jit(solution)/shard_map/all_gather | solution.py:66
  107.8 1.9 fusion.77
  110.1 2.7 %fusion = f32[512,256]{1,0:T(8,128)S(1)} fusion(bf16[2048,256]{1,0:T(8,128)(2,1)S(1)} %bitcast.95, bf16[512,2048]{0,1:T(8,128)(2,1)} %collective-permute-done.1, bf16[512,2048]{0,1:T(8,128)(2,1)S(1)} %bitcast.90, pred[]{:T(512)S(6)} %eq.25), kind=kOutput, calls=%fused_computation.1 | convolution fusion | flops 537919488 | bytes 5767169 | tf_op jit(solution)/shard_map/dot_general | solution.py:33
  113.1 1.7 fusion.10
  114.9 1.9 fusion.26
  116.8 2.1 %convolution_add_fusion = f32[1024,512]{1,0:T(8,128)} fusion(f32[1024,512]{1,0:T(8,128)S(1)} %fusion.26, bf16[1024,512]{1,0:T(8,128)(2,1)S(1)} %bitcast.84, bf16[512,512]{1,0:T(8,128)(2,1)} %collective-permute-done.6, pred[]{:T(512)S(6)} %eq.25, bf16[512,256]{1,0:T(8,128)(2,1)S(1)} %copy-done.3, bf16[512,256]{1,0:T(8,128)(2,1)S(1)} %get-tuple-element.19), kind=kOutput, calls=%fused_computation.7 | convolution fusion | flops 538705920 | bytes 6291457 | tf_op jit(solution)/shard_map/dot_general | solution.py:33
  118.9 6.8 %all-to-all-start.1 = ((f32[8,128,512]{2,1,0:T(8,128)}), f32[8,128,512]{2,1,0:T(8,128)S(1)}, u32[]{:S(2)}, u32[]{:S(2)}) async-start(f32[8,128,512]{2,1,0:T(8,128)} %bitcast.26), calls=%async_computation.1 | async-start | bytes 4194304 | tf_op jit(solution)/shard_map/all_to_all | solution.py:97
  126.4 25.0 %all-to-all-done.1 = f32[8,128,512]{2,1,0:T(8,128)S(1)} async-done(((f32[8,128,512]{2,1,0:T(8,128)}), f32[8,128,512]{2,1,0:T(8,128)S(1)}, u32[]{:S(2)}, u32[]{:S(2)}) %all-to-all-start.1) | async-done | bytes 2097184 | tf_op jit(solution)/shard_map/all_to_all | solution.py:97
  151.8 20.5 %all_to_all.16 = bf16[8,128,512]{2,1,0:T(8,128)(2,1)S(1)} all-to-all(bf16[8,128,512]{2,1,0:T(8,128)(2,1)S(1)} %broadcast_in_dim.13), channel_id=1, replica_groups=mesh['yl'=2,'zh'=4,'zl'=4,'yh'=2,'x'=4,'c'=2] {'yh','x'}, dimensions={0} | all-to-all | bytes 2097152 | tf_op jit(solution)/shard_map/all_to_all | solution.py:100
  172.3 1.9 collective-permute-start.7
  177.3 1.9 collective-permute-start.8
  179.2 8.3 %collective-permute-done.8 = f32[256,256]{1,0:T(8,128)S(1)} collective-permute-done((f32[256,256]{1,0:T(8,128)S(1)}, f32[256,256]{1,0:T(8,128)S(1)}, u32[]{:S(2)}, u32[]{:S(2)}) %collective-permute-start.8) | collective-permute-done | bytes 262176 | tf_op jit(solution)/shard_map/ppermute | solution.py:29
  (48 shorter events, 13.7 us)
Async XLA Ops:
  6.5 16.5 %copy-start = (bf16[128,4096]{1,0:T(8,128)(2,1)S(1)}, bf16[128,4096]{1,0:T(8,128)(2,1)}, u32[]{:S(2)}) copy-start(bf16[128,4096]{1,0:T(8,128)(2,1)} %param.5) | copy-start | bytes 3145732
  6.5 101.3 %all-gather.5.cloned.1.call-start = ((), (), s32[]{:S(2)}) async-start(), calls=%async_computation.3 | async-start | bytes 4456448 | tf_op jit(solution)/shard_map/all_gather | solution.py:66
  9.8 8.2 %collective-permute-start.3 = (bf16[64,512]{1,0:T(8,128)(2,1)S(1)}, bf16[64,512]{1,0:T(8,128)(2,1)S(1)}, u32[]{:S(2)}, u32[]{:S(2)}) collective-permute-start(bf16[64,512]{1,0:T(8,128)(2,1)S(1)} %get-tuple-element.23), channel_id=1, source_target_pairs={{0,0},{1,256},{256,1},{257,257},{2,2},{3,258},{258,3},{259,259},{4... | collective-permute-start | bytes 196616 | tf_op jit(solution)/shard_map/ppermute | solution.py:58
  10.5 7.6 %collective-permute-start.4 = (bf16[64,512]{1,0:T(8,128)(2,1)S(1)}, bf16[64,512]{1,0:T(8,128)(2,1)S(1)}, u32[]{:S(2)}, u32[]{:S(2)}) collective-permute-start(bf16[64,512]{1,0:T(8,128)(2,1)S(1)} %get-tuple-element.24), channel_id=1, source_target_pairs={{0,256},{1,0},{256,257},{257,1},{2,258},{3,2},{258,259},{259,3},{4... | collective-permute-start | bytes 196616 | tf_op jit(solution)/shard_map/ppermute | solution.py:61
  16.1 6.2 %collective-permute-start.2 = (bf16[128,256]{1,0:T(8,128)(2,1)S(1)}, bf16[128,256]{1,0:T(8,128)(2,1)S(1)}, u32[]{:S(2)}, u32[]{:S(2)}) collective-permute-start(bf16[128,256]{1,0:T(8,128)(2,1)S(1)} %get-tuple-element.22), channel_id=1, source_target_pairs={{0,256},{256,0},{1,257},{257,1},{2,258},{258,2},{3,259},{259,3},{4... | collective-permute-start | bytes 196616 | tf_op jit(solution)/shard_map/ppermute | solution.py:29
  23.4 5.8 %collective-permute-start = (bf16[64,256]{1,0:T(8,128)(2,1)S(1)}, bf16[64,256]{1,0:T(8,128)(2,1)S(1)}, u32[]{:S(2)}, u32[]{:S(2)}) collective-permute-start(bf16[64,256]{1,0:T(8,128)(2,1)S(1)} %fusion.45), channel_id=1, source_target_pairs={{0,256},{256,0},{1,257},{257,1},{2,258},{258,2},{3,259},{259,3},{4... | collective-permute-start | bytes 98312 | tf_op jit(solution)/shard_map/ppermute | solution.py:29
  89.4 20.3 %collective-permute-start.1 = (bf16[512,2048]{0,1:T(8,128)(2,1)}, bf16[512,2048]{0,1:T(8,128)(2,1)}, u32[]{:S(2)}, u32[]{:S(2)}) collective-permute-start(bf16[512,2048]{0,1:T(8,128)(2,1)} %bitcast.89), channel_id=1, source_target_pairs={{0,1},{1,0},{2,3},{3,2},{4,5},{5,4},{6,7},{7,6},{8,9},{9,8},{10,11... | collective-permute-start | bytes 6291464 | tf_op jit(solution)/shard_map/ppermute | solution.py:29
  92.4 10.6 %collective-permute-start.5 = (bf16[512,256]{1,0:T(8,128)(2,1)S(1)}, bf16[512,256]{1,0:T(8,128)(2,1)S(1)}, u32[]{:S(2)}, u32[]{:S(2)}) collective-permute-start(bf16[512,256]{1,0:T(8,128)(2,1)S(1)} %get-tuple-element.20), channel_id=1, source_target_pairs={{0,256},{256,0},{1,257},{257,1},{2,258},{258,2},{3,259},{259,3},{4... | collective-permute-start | bytes 786440 | tf_op jit(solution)/shard_map/ppermute | solution.py:29
  103.0 6.7 %copy-start.2 = (bf16[512,256]{1,0:T(8,128)(2,1)}, bf16[512,256]{1,0:T(8,128)(2,1)S(1)}, u32[]{:S(2)}) copy-start(bf16[512,256]{1,0:T(8,128)(2,1)S(1)} %collective-permute-done.5) | copy-start | bytes 786436
  103.9 11.0 %collective-permute-start.6 = (bf16[512,512]{1,0:T(8,128)(2,1)}, bf16[512,512]{1,0:T(8,128)(2,1)}, u32[]{:S(2)}, u32[]{:S(2)}) collective-permute-start(bf16[512,512]{1,0:T(8,128)(2,1)} %pad_maximum_fusion), channel_id=1, source_target_pairs={{0,1},{1,0},{2,3},{3,2},{4,5},{5,4},{6,7},{7,6},{8,9},{9,8},{10,11... | collective-permute-start | bytes 1572872 | tf_op jit(solution)/shard_map/ppermute | solution.py:29
  107.8 2.3 %copy-start.4 = (bf16[8,512,256]{1,2,0:T(8,128)(2,1)S(1)}, bf16[8,512,256]{1,2,0:T(8,128)(2,1)}, u32[]{:S(2)}) copy-start(bf16[8,512,256]{1,2,0:T(8,128)(2,1)} %copy.8) | copy-start | bytes 6291460
  110.1 2.8 %copy-start.1 = (bf16[4096,512]{1,0:T(8,128)(2,1)S(1)}, bf16[4096,512]{1,0:T(8,128)(2,1)}, u32[]{:S(2)}) copy-start(bf16[4096,512]{1,0:T(8,128)(2,1)} %all-gather.5.cloned.1.call-done) | copy-start | bytes 12582916
  114.9 1.9 copy-start.3
  118.9 32.5 %all-to-all-start.1 = ((f32[8,128,512]{2,1,0:T(8,128)}), f32[8,128,512]{2,1,0:T(8,128)S(1)}, u32[]{:S(2)}, u32[]{:S(2)}) async-start(f32[8,128,512]{2,1,0:T(8,128)} %bitcast.26), calls=%async_computation.1 | async-start | bytes 4194304 | tf_op jit(solution)/shard_map/all_to_all | solution.py:97
  125.7 48.5 %all-gather.7.cloned.1.call-start = ((), (), s32[]{:S(2)}) async-start(), calls=%async_computation.4 | async-start | bytes 1310720 | tf_op jit(solution)/shard_map/all_gather | solution.py:94
  172.3 4.5 %collective-permute-start.7 = (bf16[1024,512]{1,0:T(8,128)(2,1)S(1)}, bf16[1024,512]{1,0:T(8,128)(2,1)S(1)}, u32[]{:S(2)}, u32[]{:S(2)}) collective-permute-start(bf16[1024,512]{1,0:T(8,128)(2,1)S(1)} %bitcast.92), channel_id=1, source_target_pairs={{0,1},{1,0},{2,3},{3,2},{4,5},{5,4},{6,7},{7,6},{8,9},{9,8},{10,11... | collective-permute-start | bytes 3145736 | tf_op jit(solution)/shard_map/ppermute | solution.py:29
  177.3 10.2 %collective-permute-start.8 = (f32[256,256]{1,0:T(8,128)S(1)}, f32[256,256]{1,0:T(8,128)S(1)}, u32[]{:S(2)}, u32[]{:S(2)}) collective-permute-start(f32[256,256]{1,0:T(8,128)S(1)} %slice.37), channel_id=1, source_target_pairs={{0,256},{256,0},{1,257},{257,1},{2,258},{258,2},{3,259},{259,3},{4... | collective-permute-start | bytes 786440 | tf_op jit(solution)/shard_map/ppermute | solution.py:29
Sparse Core Ops, SparseCore 0:
  23.2 84.6 all-gather.4
  128.6 36.5 all-gather.6

commit v3 on v2

--- a/solution.py
+++ b/solution.py
@@ -90,7 +90,6 @@
     act_proj = (dot(rows_own, own_basis) + dot(rows_other, other_basis)).astype(BF16)
     got_a = gathered[:, basis_rows : basis_rows + capacity].reshape(nz * capacity, hidden)
     got_b = gathered[:, basis_rows + capacity :].reshape(nz * capacity, hidden)
-    act_proj, got_a, got_b = lax.optimization_barrier((act_proj, got_a, got_b))
     act_all = lax.all_gather(act_proj, "zl", axis=0, tiled=False)
 
     part = dot(got_a, basis_a) + dot(got_b, basis_b)
@@ -109,9 +108,13 @@
     def outer(g, a):
         return lax.dot_general(g, a, (((0,), (0,)), ((), ())), preferred_element_type=F32)
 
-    block = (outer(grad_sq, act_first) + outer(grad_sq_other, act_second)) / token_total
-    half = block.shape[0] // 2
-    kept, got = block[:half], swap(block[half:], "yl")
+    def block(lo, hi):
+        own, other = grad_sq[:, lo:hi], grad_sq_other[:, lo:hi]
+        return (outer(own, act_first) + outer(other, act_second)) / token_total
+
+    keys = grad_sq.shape[1]
+    got = swap(block(keys // 2, keys), "yl")
+    kept = block(0, keys // 2)
     return jnp.stack([jnp.where(yl == 0, kept, got), jnp.where(yl == 0, got, kept)])
 
 

time: 198 us -> 184 us (0.929)
  blocking collectives: 78.1 us -> 46 us
  starting transfers between devices: 26.2 us -> 38.3 us
  local copies, waits for them, and re-layouts: 7.32 us -> 10.8 us
  waiting for transfers between devices: 52.8 us -> 55.4 us
    all_to_all x1 -> x0, blocking collectives: 28.7 us -> none  [per_device(): rows = lax.all_to_all(copies, PLANE, 0, 0, tiled=True)]
    all_to_all x0 -> x1, waiting for transfers between devices: none -> 19.5 us  [per_device(): rows = lax.all_to_all(copies, PLANE, 0, 0, tiled=True)]
    ppermute x7, waiting for transfers between devices: 25 us -> 11.2 us  [swap(): return lax.ppermute(x, axis, [(0, 1), (1, 0)])]
    all_to_all x1, waiting for transfers between devices: 25 us -> 12.6 us  [per_device(): lax.all_to_all(part.reshape(planes, part.shape[0] // planes, -1), PLANE,...]
    all_gather x1, waiting for transfers between devices: 1.99 us -> 9.17 us  [per_device(): gathered = lax.all_gather(payload, ('zh', 'zl'), axis=0, tiled=False)]
    all_to_all x0 -> x1, starting transfers between devices: none -> 7.13 us  [per_device(): rows = lax.all_to_all(copies, PLANE, 0, 0, tiled=True)]
    ppermute x7, starting transfers between devices: 14.1 us -> 19.8 us  [swap(): return lax.ppermute(x, axis, [(0, 1), (1, 0)])]
    all_to_all x1, blocking collectives: 20.5 us -> 17.3 us  [per_device(): lax.all_to_all(copies, PLANE, 0, 0, tiled=True).reshape(nz * capacity, -1)]
  transfers between devices with their start and end apart: 12 -> 13, of which waited for: 7 -> 7; matrix products, arithmetic and copies ran while one was open for 7% -> 13% of each run, Pallas kernels for 0% -> 0%
where the time goes in v3:
time: 184 us; the launch traced here: 182 us
  waiting for transfers between devices  55.4 us (30%)
  blocking collectives  46 us (25%)
  starting transfers between devices  38.3 us (21%)
  between operations  13.7 us (7%)
  matrix products  13.2 us (7%)
  local copies, waits for them, and re-layouts  10.8 us (6%)
  other arithmetic  5.11 us (3%)
    all_gather x1, blocking collectives, per_device(): rows = lax.all_gather(rows, 'zh', axis=0, tiled=True)  28.7 us
    ppermute x7, starting transfers between devices, swap(): return lax.ppermute(x, axis, [(0, 1), (1, 0)])  19.8 us
    all_to_all x1, waiting for transfers between devices, per_device(): rows = lax.all_to_all(copies, PLANE, 0, 0, tiled=True)  19.5 us
    all_to_all x1, blocking collectives, per_device(): lax.all_to_all(copies, PLANE, 0, 0, tiled=True).reshape(nz * capacity, -1)  17.3 us
    all_to_all x1, waiting for transfers between devices, per_device(): lax.all_to_all(part.reshape(planes, part.shape[0] // planes, -1), PLANE,...  12.6 us
    ppermute x7, waiting for transfers between devices, swap(): return lax.ppermute(x, axis, [(0, 1), (1, 0)])  11.2 us
    all_gather x1, waiting for transfers between devices, per_device(): gathered = lax.all_gather(payload, ('zh', 'zl'), axis=0, tiled=False)  9.17 us
    dot_general x4, matrix products, dot(): return jnp.dot(a, b, preferred_element_type=F32)  9.06 us
  transfers between devices with their start and end apart: 13, of which 7 were waited for; matrix products, arithmetic and copies ran while one was open for 13% of the time, Pallas kernels for 0%

profile of v3, /device:TPU:6, one launch (start us, length us, event | category | flops | bytes accessed | tf_op | source)
XLA Modules:
  0.0 182.5 jit_solution(12394067993871902624)
XLA Ops:
  9.8 3.5 %collective-permute-start.2 = (bf16[64,512]{1,0:T(8,128)(2,1)S(1)}, bf16[64,512]{1,0:T(8,128)(2,1)S(1)}, u32[]{:S(2)}, u32[]{:S(2)}) collective-permute-start(bf16[64,512]{1,0:T(8,128)(2,1)S(1)} %get-tuple-element.18), channel_id=1, source_target_pairs={{0,256},{1,0},{256,257},{257,1},{2,258},{3,2},{258,259},{259,3},{4... | collective-permute-start | bytes 196616 | tf_op jit(solution)/shard_map/ppermute | solution.py:61
  14.9 3.7 %collective-permute-start = (bf16[128,256]{1,0:T(8,128)(2,1)S(1)}, bf16[128,256]{1,0:T(8,128)(2,1)S(1)}, u32[]{:S(2)}, u32[]{:S(2)}) collective-permute-start(bf16[128,256]{1,0:T(8,128)(2,1)S(1)} %get-tuple-element.16), channel_id=1, source_target_pairs={{0,256},{256,0},{1,257},{257,1},{2,258},{258,2},{3,259},{259,3},{4... | collective-permute-start | bytes 196616 | tf_op jit(solution)/shard_map/ppermute | solution.py:29
  18.6 2.8 %collective-permute-done = bf16[128,256]{1,0:T(8,128)(2,1)S(1)} collective-permute-done((bf16[128,256]{1,0:T(8,128)(2,1)S(1)}, bf16[128,256]{1,0:T(8,128)(2,1)S(1)}, u32[]{:S(2)}, u32[]{:S(2)}) %collective-permute-start) | collective-permute-done | bytes 65568 | tf_op jit(solution)/shard_map/ppermute | solution.py:29
  22.5 3.3 %collective-permute-start.5 = (bf16[64,256]{1,0:T(8,128)(2,1)S(1)}, bf16[64,256]{1,0:T(8,128)(2,1)S(1)}, u32[]{:S(2)}, u32[]{:S(2)}) collective-permute-start(bf16[64,256]{1,0:T(8,128)(2,1)S(1)} %fusion.55), channel_id=1, source_target_pairs={{0,256},{256,0},{1,257},{257,1},{2,258},{258,2},{3,259},{259,3},{4... | collective-permute-start | bytes 98312 | tf_op jit(solution)/shard_map/ppermute | solution.py:29
  25.9 2.5 %collective-permute-done.5 = bf16[64,256]{1,0:T(8,128)(2,1)S(1)} collective-permute-done((bf16[64,256]{1,0:T(8,128)(2,1)S(1)}, bf16[64,256]{1,0:T(8,128)(2,1)S(1)}, u32[]{:S(2)}, u32[]{:S(2)}) %collective-permute-start.5) | collective-permute-done | bytes 32800 | tf_op jit(solution)/shard_map/ppermute | solution.py:29
  28.4 28.7 %all_gather.17 = bf16[512,256]{1,0:T(8,128)(2,1)S(1)} all-gather(bf16[128,256]{1,0:T(8,128)(2,1)S(1)} %pad_maximum_fusion.3), channel_id=1, replica_groups=mesh['yl'=2,'zh'=4,'zl'=4,'yh'=2,'x'=4,'c'=2] {'zh'}, dimensions={0}, use_global_device_ids=true | all-gather | bytes 327680 | tf_op jit(solution)/shard_map/all_gather | solution.py:76
  58.6 7.1 %all-to-all-start.2 = ((bf16[8,512,256]{2,1,0:T(8,128)(2,1)}), bf16[8,512,256]{2,1,0:T(8,128)(2,1)S(1)}, u32[]{:S(2)}, u32[]{:S(2)}) async-start(bf16[8,512,256]{2,1,0:T(8,128)(2,1)} %broadcast_in_dim.13), calls=%async_computation.2 | async-start | bytes 4194304 | tf_op jit(solution)/shard_map/all_to_all | solution.py:78
  65.7 1.8 dynamic-slice_bitcast_fusion.1
  67.5 3.1 %collective-permute-start.3 = (bf16[512,256]{1,0:T(8,128)(2,1)}, bf16[512,256]{1,0:T(8,128)(2,1)}, u32[]{:S(2)}, u32[]{:S(2)}) collective-permute-start(bf16[512,256]{1,0:T(8,128)(2,1)} %get-tuple-element.14), channel_id=1, source_target_pairs={{0,256},{256,0},{1,257},{257,1},{2,258},{258,2},{3,259},{259,3},{4... | collective-permute-start | bytes 786440 | tf_op jit(solution)/shard_map/ppermute | solution.py:29
  70.6 19.5 %all-to-all-done.2 = bf16[8,512,256]{2,1,0:T(8,128)(2,1)S(1)} async-done(((bf16[8,512,256]{2,1,0:T(8,128)(2,1)}), bf16[8,512,256]{2,1,0:T(8,128)(2,1)S(1)}, u32[]{:S(2)}, u32[]{:S(2)}) %all-to-all-start.2) | async-done | bytes 2097184 | tf_op jit(solution)/shard_map/all_to_all | solution.py:78
  90.2 2.4 %copy.8 = bf16[8,512,256]{1,2,0:T(8,128)(2,1)} copy(bf16[8,512,256]{2,1,0:T(8,128)(2,1)S(1)} %all-to-all-done.2) | data formatting | bytes 4194304 | tf_op jit(solution)/shard_map/all_to_all | solution.py:78
  92.6 1.9 %collective-permute-start.6 = (bf16[512,2048]{0,1:T(8,128)(2,1)}, bf16[512,2048]{0,1:T(8,128)(2,1)}, u32[]{:S(2)}, u32[]{:S(2)}) collective-permute-start(bf16[512,2048]{0,1:T(8,128)(2,1)} %bitcast.95), channel_id=1, source_target_pairs={{0,1},{1,0},{2,3},{3,2},{4,5},{5,4},{6,7},{7,6},{8,9},{9,8},{10,11... | collective-permute-start | bytes 6291464 | tf_op jit(solution)/shard_map/ppermute | solution.py:29
  95.5 2.4 %collective-permute-start.4 = (bf16[512,512]{1,0:T(8,128)(2,1)S(1)}, bf16[512,512]{1,0:T(8,128)(2,1)S(1)}, u32[]{:S(2)}, u32[]{:S(2)}) collective-permute-start(bf16[512,512]{1,0:T(8,128)(2,1)S(1)} %pad_maximum_fusion), channel_id=1, source_target_pairs={{0,1},{1,0},{2,3},{3,2},{4,5},{5,4},{6,7},{7,6},{8,9},{9,8},{10,11... | collective-permute-start | bytes 1572872 | tf_op jit(solution)/shard_map/ppermute | solution.py:29
  97.9 9.2 %all-gather.5.cloned.1.call-done = bf16[4096,512]{1,0:T(8,128)(2,1)} async-done(((bf16[256,512]{1,0:T(8,128)(2,1)}), bf16[4096,512]{1,0:T(8,128)(2,1)}) %all-gather.5.cloned.1.call-update) | async-done | bytes 4194320 | tf_op jit(solution)/shard_map/all_gather | solution.py:66
  110.6 3.1 %convolution_add_fusion = f32[1024,512]{1,0:T(8,128)} fusion(f32[1024,512]{1,0:T(8,128)S(1)} %fusion.32, bf16[1024,512]{1,0:T(8,128)(2,1)S(1)} %bitcast.88, bf16[512,512]{1,0:T(8,128)(2,1)S(1)} %collective-permute-done.4, pred[]{:T(512)S(6)} %eq.61, bf16[512,256]{1,0:T(8,128)(2,1)} %collective-permute-done.3, bf16[512,256]{1,0:T(8,128)(2,1)S(1)} %get-tuple-element.13), kind=kOutput, calls=%fused_computation.7 | convolution fusion | flops 538705920 | bytes 6291457 | tf_op jit(solution)/shard_map/dot_general | solution.py:33
  113.7 7.2 %all-to-all-start = ((f32[8,128,512]{2,1,0:T(8,128)}), f32[8,128,512]{2,1,0:T(8,128)S(1)}, u32[]{:S(2)}, u32[]{:S(2)}) async-start(f32[8,128,512]{2,1,0:T(8,128)} %bitcast.17), calls=%async_computation | async-start | bytes 4194304 | tf_op jit(solution)/shard_map/all_to_all | solution.py:96
  120.9 1.9 %fusion.88 = (bf16[16,128,256]{2,1,0:T(8,128)(2,1)S(1)}, bf16[16,128,256]{2,1,0:T(8,128)(2,1)S(1)}) fusion(bf16[16,256,512]{2,1,0:T(8,128)(2,1)} %bitcast.87), kind=kLoop, calls=%fused_computation.114 | loop fusion | bytes 4194304 | tf_op jit(solution)/shard_map/slice | solution.py:88
  123.1 2.6 %fusion = f32[512,256]{1,0:T(8,128)S(1)} fusion(bf16[2048,256]{1,0:T(8,128)(2,1)S(1)} %bitcast.102, bf16[512,2048]{0,1:T(8,128)(2,1)} %collective-permute-done.6, bf16[512,2048]{0,1:T(8,128)(2,1)S(1)} %bitcast.96, pred[]{:T(512)S(6)} %eq.61), kind=kOutput, calls=%fused_computation.1 | convolution fusion | flops 537919488 | bytes 5767169 | tf_op jit(solution)/shard_map/dot_general | solution.py:33
  127.5 12.6 %all-to-all-done = f32[8,128,512]{2,1,0:T(8,128)S(1)} async-done(((f32[8,128,512]{2,1,0:T(8,128)}), f32[8,128,512]{2,1,0:T(8,128)S(1)}, u32[]{:S(2)}, u32[]{:S(2)}) %all-to-all-start) | async-done | bytes 2097184 | tf_op jit(solution)/shard_map/all_to_all | solution.py:96
  140.4 17.3 %all_to_all.15 = bf16[8,128,512]{2,1,0:T(8,128)(2,1)S(1)} all-to-all(bf16[8,128,512]{2,1,0:T(8,128)(2,1)S(1)} %broadcast_in_dim.12), channel_id=1, replica_groups=mesh['yl'=2,'zh'=4,'zl'=4,'yh'=2,'x'=4,'c'=2] {'yh','x'}, dimensions={0} | all-to-all | bytes 2097152 | tf_op jit(solution)/shard_map/all_to_all | solution.py:99
  157.7 1.9 %collective-permute-start.7 = (bf16[1024,512]{1,0:T(8,128)(2,1)S(1)}, bf16[1024,512]{1,0:T(8,128)(2,1)S(1)}, u32[]{:S(2)}, u32[]{:S(2)}) collective-permute-start(bf16[1024,512]{1,0:T(8,128)(2,1)S(1)} %bitcast.98), channel_id=1, source_target_pairs={{0,1},{1,0},{2,3},{3,2},{4,5},{5,4},{6,7},{7,6},{8,9},{9,8},{10,11... | collective-permute-start | bytes 3145736 | tf_op jit(solution)/shard_map/ppermute | solution.py:29
  159.6 2.9 %all-gather.7.cloned.1.call-done = bf16[2048,256]{1,0:T(8,128)(2,1)} async-done(((bf16[512,256]{1,0:T(8,128)(2,1)}), bf16[2048,256]{1,0:T(8,128)(2,1)}) %all-gather.7.cloned.1.call-update) | async-done | bytes 1048592 | tf_op jit(solution)/shard_map/all_gather | solution.py:93
  164.7 3.4 %collective-permute-start.8 = (f32[256,256]{1,0:T(8,128)S(1)}, f32[256,256]{1,0:T(8,128)S(1)}, u32[]{:S(2)}, u32[]{:S(2)}) collective-permute-start(f32[256,256]{1,0:T(8,128)S(1)} %fusion.13), channel_id=1, source_target_pairs={{0,256},{256,0},{1,257},{257,1},{2,258},{258,2},{3,259},{259,3},{4... | collective-permute-start | bytes 786440 | tf_op jit(solution)/shard_map/ppermute | solution.py:29
  168.5 6.0 %collective-permute-done.8 = f32[256,256]{1,0:T(8,128)S(1)} collective-permute-done((f32[256,256]{1,0:T(8,128)S(1)}, f32[256,256]{1,0:T(8,128)S(1)}, u32[]{:S(2)}, u32[]{:S(2)}) %collective-permute-start.8) | collective-permute-done | bytes 262176 | tf_op jit(solution)/shard_map/ppermute | solution.py:29
  (43 shorter events, 18.1 us)
Async XLA Ops:
  6.5 15.7 %copy-start = (bf16[128,4096]{1,0:T(8,128)(2,1)S(1)}, bf16[128,4096]{1,0:T(8,128)(2,1)}, u32[]{:S(2)}) copy-start(bf16[128,4096]{1,0:T(8,128)(2,1)} %param.5) | copy-start | bytes 3145732
  6.5 100.6 %all-gather.5.cloned.1.call-start = ((), (), s32[]{:S(2)}) async-start(), calls=%async_computation.3 | async-start | bytes 4456448 | tf_op jit(solution)/shard_map/all_gather | solution.py:66
  9.8 8.8 %collective-permute-start.2 = (bf16[64,512]{1,0:T(8,128)(2,1)S(1)}, bf16[64,512]{1,0:T(8,128)(2,1)S(1)}, u32[]{:S(2)}, u32[]{:S(2)}) collective-permute-start(bf16[64,512]{1,0:T(8,128)(2,1)S(1)} %get-tuple-element.18), channel_id=1, source_target_pairs={{0,256},{1,0},{256,257},{257,1},{2,258},{3,2},{258,259},{259,3},{4... | collective-permute-start | bytes 196616 | tf_op jit(solution)/shard_map/ppermute | solution.py:61
  13.3 5.3 %collective-permute-start.1 = (bf16[64,512]{1,0:T(8,128)(2,1)S(1)}, bf16[64,512]{1,0:T(8,128)(2,1)S(1)}, u32[]{:S(2)}, u32[]{:S(2)}) collective-permute-start(bf16[64,512]{1,0:T(8,128)(2,1)S(1)} %get-tuple-element.17), channel_id=1, source_target_pairs={{0,0},{1,256},{256,1},{257,257},{2,2},{3,258},{258,3},{259,259},{4... | collective-permute-start | bytes 196616 | tf_op jit(solution)/shard_map/ppermute | solution.py:58
  14.9 6.5 %collective-permute-start = (bf16[128,256]{1,0:T(8,128)(2,1)S(1)}, bf16[128,256]{1,0:T(8,128)(2,1)S(1)}, u32[]{:S(2)}, u32[]{:S(2)}) collective-permute-start(bf16[128,256]{1,0:T(8,128)(2,1)S(1)} %get-tuple-element.16), channel_id=1, source_target_pairs={{0,256},{256,0},{1,257},{257,1},{2,258},{258,2},{3,259},{259,3},{4... | collective-permute-start | bytes 196616 | tf_op jit(solution)/shard_map/ppermute | solution.py:29
  22.5 5.8 %collective-permute-start.5 = (bf16[64,256]{1,0:T(8,128)(2,1)S(1)}, bf16[64,256]{1,0:T(8,128)(2,1)S(1)}, u32[]{:S(2)}, u32[]{:S(2)}) collective-permute-start(bf16[64,256]{1,0:T(8,128)(2,1)S(1)} %fusion.55), channel_id=1, source_target_pairs={{0,256},{256,0},{1,257},{257,1},{2,258},{258,2},{3,259},{259,3},{4... | collective-permute-start | bytes 98312 | tf_op jit(solution)/shard_map/ppermute | solution.py:29
  58.6 31.6 %all-to-all-start.2 = ((bf16[8,512,256]{2,1,0:T(8,128)(2,1)}), bf16[8,512,256]{2,1,0:T(8,128)(2,1)S(1)}, u32[]{:S(2)}, u32[]{:S(2)}) async-start(bf16[8,512,256]{2,1,0:T(8,128)(2,1)} %broadcast_in_dim.13), calls=%async_computation.2 | async-start | bytes 4194304 | tf_op jit(solution)/shard_map/all_to_all | solution.py:78
  67.5 27.0 %collective-permute-start.3 = (bf16[512,256]{1,0:T(8,128)(2,1)}, bf16[512,256]{1,0:T(8,128)(2,1)}, u32[]{:S(2)}, u32[]{:S(2)}) collective-permute-start(bf16[512,256]{1,0:T(8,128)(2,1)} %get-tuple-element.14), channel_id=1, source_target_pairs={{0,256},{256,0},{1,257},{257,1},{2,258},{258,2},{3,259},{259,3},{4... | collective-permute-start | bytes 786440 | tf_op jit(solution)/shard_map/ppermute | solution.py:29
  92.6 30.2 %collective-permute-start.6 = (bf16[512,2048]{0,1:T(8,128)(2,1)}, bf16[512,2048]{0,1:T(8,128)(2,1)}, u32[]{:S(2)}, u32[]{:S(2)}) collective-permute-start(bf16[512,2048]{0,1:T(8,128)(2,1)} %bitcast.95), channel_id=1, source_target_pairs={{0,1},{1,0},{2,3},{3,2},{4,5},{5,4},{6,7},{7,6},{8,9},{9,8},{10,11... | collective-permute-start | bytes 6291464 | tf_op jit(solution)/shard_map/ppermute | solution.py:29
  95.5 13.4 %collective-permute-start.4 = (bf16[512,512]{1,0:T(8,128)(2,1)S(1)}, bf16[512,512]{1,0:T(8,128)(2,1)S(1)}, u32[]{:S(2)}, u32[]{:S(2)}) collective-permute-start(bf16[512,512]{1,0:T(8,128)(2,1)S(1)} %pad_maximum_fusion), channel_id=1, source_target_pairs={{0,1},{1,0},{2,3},{3,2},{4,5},{5,4},{6,7},{7,6},{8,9},{9,8},{10,11... | collective-permute-start | bytes 1572872 | tf_op jit(solution)/shard_map/ppermute | solution.py:29
  113.7 26.4 %all-to-all-start = ((f32[8,128,512]{2,1,0:T(8,128)}), f32[8,128,512]{2,1,0:T(8,128)S(1)}, u32[]{:S(2)}, u32[]{:S(2)}) async-start(f32[8,128,512]{2,1,0:T(8,128)} %bitcast.17), calls=%async_computation | async-start | bytes 4194304 | tf_op jit(solution)/shard_map/all_to_all | solution.py:96
  120.9 41.6 %all-gather.7.cloned.1.call-start = ((), (), s32[]{:S(2)}) async-start(), calls=%async_computation.4 | async-start | bytes 1310720 | tf_op jit(solution)/shard_map/all_gather | solution.py:93
  120.9 2.3 %copy-start.1 = (bf16[8,512,256]{1,2,0:T(8,128)(2,1)S(1)}, bf16[8,512,256]{1,2,0:T(8,128)(2,1)}, u32[]{:S(2)}) copy-start(bf16[8,512,256]{1,2,0:T(8,128)(2,1)} %copy.8) | copy-start | bytes 6291460
  157.7 6.7 %collective-permute-start.7 = (bf16[1024,512]{1,0:T(8,128)(2,1)S(1)}, bf16[1024,512]{1,0:T(8,128)(2,1)S(1)}, u32[]{:S(2)}, u32[]{:S(2)}) collective-permute-start(bf16[1024,512]{1,0:T(8,128)(2,1)S(1)} %bitcast.98), channel_id=1, source_target_pairs={{0,1},{1,0},{2,3},{3,2},{4,5},{5,4},{6,7},{7,6},{8,9},{9,8},{10,11... | collective-permute-start | bytes 3145736 | tf_op jit(solution)/shard_map/ppermute | solution.py:29
  164.7 9.7 %collective-permute-start.8 = (f32[256,256]{1,0:T(8,128)S(1)}, f32[256,256]{1,0:T(8,128)S(1)}, u32[]{:S(2)}, u32[]{:S(2)}) collective-permute-start(f32[256,256]{1,0:T(8,128)S(1)} %fusion.13), channel_id=1, source_target_pairs={{0,256},{256,0},{1,257},{257,1},{2,258},{258,2},{3,259},{259,3},{4... | collective-permute-start | bytes 786440 | tf_op jit(solution)/shard_map/ppermute | solution.py:29
Sparse Core Ops, SparseCore 0:
  22.3 84.7 all-gather.4
  127.6 34.8 all-gather.6

commit v4 on v3

--- a/solution.py
+++ b/solution.py
@@ -1,6 +1,8 @@
 import jax
 import jax.numpy as jnp
 from jax import lax
+from jax.experimental import pallas as pl
+from jax.experimental.pallas import tpu as pltpu
 from jax.sharding import Mesh, PartitionSpec as P
 
 F32, BF16 = jnp.float32, jnp.bfloat16
@@ -33,6 +35,62 @@
     return jnp.dot(a, b, preferred_element_type=F32)
 
 
+def project_kernel(got, rows, rows_peer, basis, basis_peer, part, act, total):
+    step = pl.program_id(0)
+    blocks, height, _ = got.shape
+    cols = act.shape[1]
+    deep, slots = height // 2, height // 4
+
+    @pl.when(step == 0)
+    def _():
+        total[...] = jnp.zeros_like(total)
+
+    own = got[:, :deep, :cols].reshape(blocks * deep, cols)
+    other = got[:, :deep, cols:].reshape(blocks * deep, cols)
+    total[...] += dot(rows[...], own) + dot(rows_peer[...], other)
+    grad = got[:, deep : deep + slots].reshape(blocks * slots, 2 * cols)
+    grad_peer = got[:, deep + slots :].reshape(blocks * slots, 2 * cols)
+    part[...] = (dot(grad, basis[...]) + dot(grad_peer, basis_peer[...])).astype(part.dtype)
+
+    @pl.when(step == pl.num_programs(0) - 1)
+    def _():
+        act[...] = total[...].astype(act.dtype)
+
+
+def project(got, rows, rows_peer, basis, basis_peer, blocks):
+    nz, height, lanes = got.shape
+    count, keys, cols = rows.shape[0], basis.shape[1], lanes // 2
+    row_block = pl.BlockSpec((count, blocks * height // 2), lambda i: (0, i))
+    whole = pl.BlockSpec(basis.shape, lambda i: (0, 0))
+    made = nz * height // 4
+    return pl.pallas_call(
+        project_kernel,
+        grid=(nz // blocks,),
+        in_specs=[
+            pl.BlockSpec((blocks, height, lanes), lambda i: (i, 0, 0)),
+            row_block,
+            row_block,
+            whole,
+            whole,
+        ],
+        out_specs=[
+            pl.BlockSpec((blocks * height // 4, keys), lambda i: (i, 0)),
+            pl.BlockSpec((count, cols), lambda i: (0, 0)),
+        ],
+        out_shape=[
+            jax.ShapeDtypeStruct((made, keys), BF16),
+            jax.ShapeDtypeStruct((count, cols), BF16),
+        ],
+        scratch_shapes=[pltpu.VMEM((count, cols), F32)],
+        compiler_params=pltpu.CompilerParams(vmem_limit_bytes=32 * 1024 * 1024),
+        cost_estimate=pl.CostEstimate(
+            flops=4 * made * basis.shape[0] * keys + 4 * count * rows.shape[1] * cols,
+            bytes_accessed=2 * (got.size + 2 * rows.size + 2 * basis.size + made * keys + count * cols),
+            transcendentals=0,
+        ),
+    )(got, rows, rows_peer, basis, basis_peer)
+
+
 def per_device(tokens, act_basis, grad_basis, grads, expert_ids):
     tok_rows, width = tokens.shape
     capacity = tok_rows // 2
@@ -41,8 +99,7 @@
     token_total = tok_rows * lax.axis_size("yl") * nz
     planes = lax.axis_size("yh") * lax.axis_size("x")
     yl, core = lax.axis_index("yl"), lax.axis_index("c")
-    basis_rows, cols = act_basis.shape[1:]
-    hidden = grads.shape[2]
+    cols = act_basis.shape[2]
 
     def mine(x):
         return lax.dynamic_index_in_dim(x, yl, 0, keepdims=False)
@@ -61,8 +118,13 @@
     grad_b = lax.ppermute(
         lax.dynamic_index_in_dim(picked_grad, 1 - core, 0, keepdims=False), ("yl", "c"), crossed
     )
-    act_rows = jnp.concatenate([mine(act_basis), act_other], axis=1)
-    payload = jnp.concatenate([act_rows, grad_a, grad_b], axis=0)
+    same, act_own = yl == core, mine(act_basis)
+    act_rows = jnp.concatenate(
+        [jnp.where(same, act_own, act_other), jnp.where(same, act_other, act_own)], axis=1
+    )
+    payload = jnp.concatenate(
+        [act_rows, jnp.where(same, grad_a, grad_b), jnp.where(same, grad_b, grad_a)], axis=0
+    )
     gathered = lax.all_gather(payload, ("zh", "zl"), axis=0, tiled=False)
 
     plane = lax.axis_index("yh") * lax.axis_size("x") + lax.axis_index("x")
@@ -78,23 +140,14 @@
     rows = lax.all_to_all(copies, PLANE, 0, 0, tiled=True)
     rows = rows.transpose(1, 0, 2).reshape(rows.shape[1], planes * share)
     rows_peer = swap(rows, "c")
-    rows_own = jnp.where(yl == core, rows, rows_peer)
-    rows_other = jnp.where(yl == core, rows_peer, rows)
     basis_half = jnp.concatenate([mine(grad_basis), swap(theirs(grad_basis), "yl")], axis=1)
     basis_peer = swap(basis_half, "c")
-    basis_a = jnp.where(yl == core, basis_half, basis_peer)
-    basis_b = jnp.where(yl == core, basis_peer, basis_half)
 
-    own_basis = gathered[:, :basis_rows, :cols].reshape(nz * basis_rows, cols)
-    other_basis = gathered[:, :basis_rows, cols:].reshape(nz * basis_rows, cols)
-    act_proj = (dot(rows_own, own_basis) + dot(rows_other, other_basis)).astype(BF16)
-    got_a = gathered[:, basis_rows : basis_rows + capacity].reshape(nz * capacity, hidden)
-    got_b = gathered[:, basis_rows + capacity :].reshape(nz * capacity, hidden)
+    part, act_proj = project(gathered, rows, rows_peer, basis_half, basis_peer, nl)
     act_all = lax.all_gather(act_proj, "zl", axis=0, tiled=False)
 
-    part = dot(got_a, basis_a) + dot(got_b, basis_b)
     parts = lax.all_to_all(part.reshape(planes, part.shape[0] // planes, -1), PLANE, 0, 0, tiled=True)
-    grad_sq = jnp.square(jnp.sum(parts, axis=0)).astype(BF16)
+    grad_sq = jnp.square(jnp.sum(parts.astype(F32), axis=0)).astype(BF16)
     copies = jnp.broadcast_to(grad_sq[None], (planes,) + grad_sq.shape)
     grad_sq = lax.all_to_all(copies, PLANE, 0, 0, tiled=True).reshape(nz * capacity, -1)
     grad_sq_other = swap(grad_sq, "c")

time: 184 us -> 183 us (level)
  blocking collectives: 46 us -> 77.7 us
  waiting for transfers between devices: 55.4 us -> 35.6 us
  matrix products: 13.2 us -> 4.09 us
  starting transfers between devices: 38.3 us -> 31.5 us
  Pallas kernels: 0 us -> 3.97 us
    all_to_all x0 -> x1, blocking collectives: none -> 29.7 us  [per_device(): rows = lax.all_to_all(copies, PLANE, 0, 0, tiled=True)]
    all_to_all x1 -> x0, waiting for transfers between devices: 19.5 us -> none  [per_device(): rows = lax.all_to_all(copies, PLANE, 0, 0, tiled=True)]
    unnamed x4 -> x20, local copies, waits for them, and re-layouts: 0.37 us -> 9.78 us
    dot_general x4 -> x0, matrix products: 9.06 us -> none  [dot(): return jnp.dot(a, b, preferred_element_type=F32)]
    all_gather x1, waiting for transfers between devices: 9.17 us -> 1.3 us  [per_device(): gathered = lax.all_gather(payload, ('zh', 'zl'), axis=0, tiled=False)]
    all_to_all x1 -> x0, starting transfers between devices: 7.13 us -> none  [per_device(): rows = lax.all_to_all(copies, PLANE, 0, 0, tiled=True)]
    ppermute x7, waiting for transfers between devices: 11.2 us -> 17.3 us  [swap(): return lax.ppermute(x, axis, [(0, 1), (1, 0)])]
    pallas_call x0 -> x1, Pallas kernels: none -> 3.97 us  [project(): pl.pallas_call(project_kernel, grid=(nz // blocks,), in_specs=[pl.BlockSp...]
  transfers between devices with their start and end apart: 13 -> 12, of which waited for: 7 -> 8; matrix products, arithmetic and copies ran while one was open for 13% -> 4% of each run, Pallas kernels for 0% -> 0%
where the time goes in v4:
time: 183 us
  blocking collectives  77.7 us (42%)
  waiting for transfers between devices  35.6 us (19%)
  starting transfers between devices  31.5 us (17%)
  between operations  13.7 us (7%)
  local copies, waits for them, and re-layouts  11.3 us (6%)
  other arithmetic  4.88 us (3%)
  matrix products  4.09 us (2%)
  Pallas kernels  3.97 us (2%)
    all_to_all x1, blocking collectives, per_device(): rows = lax.all_to_all(copies, PLANE, 0, 0, tiled=True)  29.7 us
    all_gather x1, blocking collectives, per_device(): rows = lax.all_gather(rows, 'zh', axis=0, tiled=True)  28.7 us
    all_to_all x1, blocking collectives, per_device(): lax.all_to_all(copies, PLANE, 0, 0, tiled=True).reshape(nz * capacity, -1)  19.3 us
    ppermute x7, starting transfers between devices, swap(): return lax.ppermute(x, axis, [(0, 1), (1, 0)])  19.1 us
    ppermute x7, waiting for transfers between devices, swap(): return lax.ppermute(x, axis, [(0, 1), (1, 0)])  17.3 us
    all_to_all x1, waiting for transfers between devices, per_device(): lax.all_to_all(part.reshape(planes, part.shape[0] // planes, -1), PLANE,...  11.7 us
    unnamed x20, local copies, waits for them, and re-layouts  9.78 us
    all_to_all x1, starting transfers between devices, per_device(): lax.all_to_all(part.reshape(planes, part.shape[0] // planes, -1), PLANE,...  7.36 us
  transfers between devices with their start and end apart: 12, of which 8 were waited for; matrix products, arithmetic and copies ran while one was open for 4% of the time, Pallas kernels for 0%

profile of v4, /device:TPU:6, one launch (start us, length us, event | category | flops | bytes accessed | tf_op | source)
XLA Modules:
  0.0 182.7 jit_solution(5049056557897207586)
XLA Ops:
  7.5 3.5 %collective-permute-start = (bf16[128,256]{1,0:T(8,128)(2,1)S(1)}, bf16[128,256]{1,0:T(8,128)(2,1)S(1)}, u32[]{:S(2)}, u32[]{:S(2)}) collective-permute-start(bf16[128,256]{1,0:T(8,128)(2,1)S(1)} %dynamic-slice_bitcast_fusion.2), channel_id=1, source_target_pairs={{0,256},{256,0},{1,257},{257,1},{2,258},{258,2},{3,259},{259,3},{4... | collective-permute-start | bytes 196616 | tf_op jit(solution)/shard_map/ppermute | solution.py:31
  14.8 4.3 %collective-permute-start.2 = (bf16[64,512]{1,0:T(8,128)(2,1)S(1)}, bf16[64,512]{1,0:T(8,128)(2,1)S(1)}, u32[]{:S(2)}, u32[]{:S(2)}) collective-permute-start(bf16[64,512]{1,0:T(8,128)(2,1)S(1)} %get-tuple-element.20), channel_id=1, source_target_pairs={{0,256},{1,0},{256,257},{257,1},{2,258},{3,2},{258,259},{259,3},{4... | collective-permute-start | bytes 196616 | tf_op jit(solution)/shard_map/ppermute | solution.py:118
  22.2 4.3 %collective-permute-start.3 = (bf16[64,256]{1,0:T(8,128)(2,1)S(1)}, bf16[64,256]{1,0:T(8,128)(2,1)S(1)}, u32[]{:S(2)}, u32[]{:S(2)}) collective-permute-start(bf16[64,256]{1,0:T(8,128)(2,1)S(1)} %fusion.38), channel_id=1, source_target_pairs={{0,256},{256,0},{1,257},{257,1},{2,258},{258,2},{3,259},{259,3},{4... | collective-permute-start | bytes 98312 | tf_op jit(solution)/shard_map/ppermute | solution.py:31
  26.4 1.9 %collective-permute-done.3 = bf16[64,256]{1,0:T(8,128)(2,1)S(1)} collective-permute-done((bf16[64,256]{1,0:T(8,128)(2,1)S(1)}, bf16[64,256]{1,0:T(8,128)(2,1)S(1)}, u32[]{:S(2)}, u32[]{:S(2)}) %collective-permute-start.3) | collective-permute-done | bytes 32800 | tf_op jit(solution)/shard_map/ppermute | solution.py:31
  28.4 28.7 %all_gather.17 = bf16[512,256]{1,0:T(8,128)(2,1)S(1)} all-gather(bf16[128,256]{1,0:T(8,128)(2,1)S(1)} %pad_maximum_fusion.3), channel_id=1, replica_groups=mesh['yl'=2,'zh'=4,'zl'=4,'yh'=2,'x'=4,'c'=2] {'zh'}, dimensions={0}, use_global_device_ids=true | all-gather | bytes 327680 | tf_op jit(solution)/shard_map/all_gather | solution.py:138
  57.2 29.7 %all_to_all.15 = bf16[8,512,256]{2,1,0:T(8,128)(2,1)S(1)} all-to-all(bf16[8,512,256]{2,1,0:T(8,128)(2,1)S(1)} %broadcast_in_dim.12), channel_id=1, replica_groups=mesh['yl'=2,'zh'=4,'zl'=4,'yh'=2,'x'=4,'c'=2] {'yh','x'}, dimensions={0} | all-to-all | bytes 4194304 | tf_op jit(solution)/shard_map/all_to_all | solution.py:140
  87.2 1.9 %collective-permute-start.4 = (bf16[512,2048]{1,0:T(8,128)(2,1)S(1)}, bf16[512,2048]{1,0:T(8,128)(2,1)S(1)}, u32[]{:S(2)}, u32[]{:S(2)}) collective-permute-start(bf16[512,2048]{1,0:T(8,128)(2,1)S(1)} %bitcast.79), channel_id=1, source_target_pairs={{0,1},{1,0},{2,3},{3,2},{4,5},{5,4},{6,7},{7,6},{8,9},{9,8},{10,11... | collective-permute-start | bytes 6291464 | tf_op jit(solution)/shard_map/ppermute | solution.py:31
  89.2 2.2 %collective-permute-start.5 = (bf16[512,256]{1,0:T(8,128)(2,1)S(1)}, bf16[512,256]{1,0:T(8,128)(2,1)S(1)}, u32[]{:S(2)}, u32[]{:S(2)}) collective-permute-start(bf16[512,256]{1,0:T(8,128)(2,1)S(1)} %get-tuple-element.14), channel_id=1, source_target_pairs={{0,256},{256,0},{1,257},{257,1},{2,258},{258,2},{3,259},{259,3},{4... | collective-permute-start | bytes 786440 | tf_op jit(solution)/shard_map/ppermute | solution.py:31
  91.4 8.4 %collective-permute-done.5 = bf16[512,256]{1,0:T(8,128)(2,1)S(1)} collective-permute-done((bf16[512,256]{1,0:T(8,128)(2,1)S(1)}, bf16[512,256]{1,0:T(8,128)(2,1)S(1)}, u32[]{:S(2)}, u32[]{:S(2)}) %collective-permute-start.5) | collective-permute-done | bytes 262176 | tf_op jit(solution)/shard_map/ppermute | solution.py:31
  99.8 1.9 %collective-permute-start.6 = (bf16[512,512]{1,0:T(8,128)(2,1)S(1)}, bf16[512,512]{1,0:T(8,128)(2,1)S(1)}, u32[]{:S(2)}, u32[]{:S(2)}) collective-permute-start(bf16[512,512]{1,0:T(8,128)(2,1)S(1)} %pad_maximum_fusion.basis), channel_id=1, source_target_pairs={{0,1},{1,0},{2,3},{3,2},{4,5},{5,4},{6,7},{7,6},{8,9},{9,8},{10,11... | collective-permute-start | bytes 1572872 | tf_op jit(solution)/shard_map/ppermute | solution.py:31
  102.6 1.1 collective-permute-done.6.basis_peer
  104.4 1.4 copy-done.4
  105.8 1.3 all-gather.5.cloned.1.call-done
  107.1 2.2 %copy-done.1 = bf16[4096,512]{1,0:T(8,128)(2,1)S(1)} copy-done((bf16[4096,512]{1,0:T(8,128)(2,1)S(1)}, bf16[4096,512]{1,0:T(8,128)(2,1)}, u32[]{:S(2)}) %copy-start.1) | copy-done | bytes 4194328
  110.3 1.6 copy-done.5
  113.0 4.0 %shard_map.55 = (bf16[1024,512]{1,0:T(8,128)(2,1)S(1)}, bf16[512,256]{1,0:T(8,128)(2,1)}) custom-call(bf16[16,256,512]{2,1,0:T(8,128)(2,1)S(1)} %bitcast.81, bf16[512,2048]{1,0:T(8,128)(2,1)S(1)} %bitcast.80, bf16[512,2048]{1,0:T(8,128)(2,1)S(1)} %copy-done.5, bf16[512,512]{1,0:T(8,128)(2,1)S(1)} %copy-done.3, bf16[512,512]{1,0:T(8,128)(2,1)S(1)} %copy-done.8), custom_call_target="tpu_custom_call" | custom-call | flops 2147483648 | bytes 10747904 | tf_op jit(solution)/shard_map/pallas_call | solution.py:66
  117.9 7.4 %all-to-all-start.1 = ((bf16[8,128,512]{2,1,0:T(8,128)(2,1)}), bf16[8,128,512]{2,1,0:T(8,128)(2,1)S(1)}, u32[]{:S(2)}, u32[]{:S(2)}) async-start(bf16[8,128,512]{2,1,0:T(8,128)(2,1)} %bitcast.82), calls=%async_computation.1 | async-start | bytes 2097152 | tf_op jit(solution)/shard_map/all_to_all | solution.py:149
  126.0 11.7 %all-to-all-done.1 = bf16[8,128,512]{2,1,0:T(8,128)(2,1)S(1)} async-done(((bf16[8,128,512]{2,1,0:T(8,128)(2,1)}), bf16[8,128,512]{2,1,0:T(8,128)(2,1)S(1)}, u32[]{:S(2)}, u32[]{:S(2)}) %all-to-all-start.1) | async-done | bytes 1048608 | tf_op jit(solution)/shard_map/all_to_all | solution.py:149
  137.9 19.3 %all_to_all.16 = bf16[8,128,512]{2,1,0:T(8,128)(2,1)S(1)} all-to-all(bf16[8,128,512]{2,1,0:T(8,128)(2,1)S(1)} %broadcast_in_dim.13), channel_id=1, replica_groups=mesh['yl'=2,'zh'=4,'zl'=4,'yh'=2,'x'=4,'c'=2] {'yh','x'}, dimensions={0} | all-to-all | bytes 2097152 | tf_op jit(solution)/shard_map/all_to_all | solution.py:152
  157.2 1.9 %collective-permute-start.7 = (bf16[1024,512]{1,0:T(8,128)(2,1)S(1)}, bf16[1024,512]{1,0:T(8,128)(2,1)S(1)}, u32[]{:S(2)}, u32[]{:S(2)}) collective-permute-start(bf16[1024,512]{1,0:T(8,128)(2,1)S(1)} %bitcast.89), channel_id=1, source_target_pairs={{0,1},{1,0},{2,3},{3,2},{4,5},{5,4},{6,7},{7,6},{8,9},{9,8},{10,11... | collective-permute-start | bytes 3145736 | tf_op jit(solution)/shard_map/ppermute | solution.py:31
  159.1 3.5 %all-gather.7.cloned.1.call-done = bf16[2048,256]{1,0:T(8,128)(2,1)} async-done(((bf16[512,256]{1,0:T(8,128)(2,1)}), bf16[2048,256]{1,0:T(8,128)(2,1)}) %all-gather.7.cloned.1.call-update) | async-done | bytes 1048592 | tf_op jit(solution)/shard_map/all_gather | solution.py:147
  162.6 1.4 multiply_convert_fusion
  164.9 3.4 %collective-permute-start.8 = (f32[256,256]{1,0:T(8,128)S(1)}, f32[256,256]{1,0:T(8,128)S(1)}, u32[]{:S(2)}, u32[]{:S(2)}) collective-permute-start(f32[256,256]{1,0:T(8,128)S(1)} %fusion.1), channel_id=1, source_target_pairs={{0,256},{256,0},{1,257},{257,1},{2,258},{258,2},{3,259},{259,3},{4... | collective-permute-start | bytes 786440 | tf_op jit(solution)/shard_map/ppermute | solution.py:31
  168.7 6.0 %collective-permute-done.8 = f32[256,256]{1,0:T(8,128)S(1)} collective-permute-done((f32[256,256]{1,0:T(8,128)S(1)}, f32[256,256]{1,0:T(8,128)S(1)}, u32[]{:S(2)}, u32[]{:S(2)}) %collective-permute-start.8) | collective-permute-done | bytes 262176 | tf_op jit(solution)/shard_map/ppermute | solution.py:31
  (55 shorter events, 16.2 us)
Async XLA Ops:
  6.5 15.3 %copy-start = (bf16[128,4096]{1,0:T(8,128)(2,1)S(1)}, bf16[128,4096]{1,0:T(8,128)(2,1)}, u32[]{:S(2)}) copy-start(bf16[128,4096]{1,0:T(8,128)(2,1)} %param.5) | copy-start | bytes 3145732
  6.5 100.6 %all-gather.5.cloned.1.call-start = ((), (), s32[]{:S(2)}) async-start(), calls=%async_computation.3 | async-start | bytes 4456448 | tf_op jit(solution)/shard_map/all_gather | solution.py:128
  7.5 11.7 %collective-permute-start = (bf16[128,256]{1,0:T(8,128)(2,1)S(1)}, bf16[128,256]{1,0:T(8,128)(2,1)S(1)}, u32[]{:S(2)}, u32[]{:S(2)}) collective-permute-start(bf16[128,256]{1,0:T(8,128)(2,1)S(1)} %dynamic-slice_bitcast_fusion.2), channel_id=1, source_target_pairs={{0,256},{256,0},{1,257},{257,1},{2,258},{258,2},{3,259},{259,3},{4... | collective-permute-start | bytes 196616 | tf_op jit(solution)/shard_map/ppermute | solution.py:31
  14.2 5.9 %collective-permute-start.1 = (bf16[64,512]{1,0:T(8,128)(2,1)S(1)}, bf16[64,512]{1,0:T(8,128)(2,1)S(1)}, u32[]{:S(2)}, u32[]{:S(2)}) collective-permute-start(bf16[64,512]{1,0:T(8,128)(2,1)S(1)} %get-tuple-element.19), channel_id=1, source_target_pairs={{0,0},{1,256},{256,1},{257,257},{2,2},{3,258},{258,3},{259,259},{4... | collective-permute-start | bytes 196616 | tf_op jit(solution)/shard_map/ppermute | solution.py:115
  14.8 6.2 %collective-permute-start.2 = (bf16[64,512]{1,0:T(8,128)(2,1)S(1)}, bf16[64,512]{1,0:T(8,128)(2,1)S(1)}, u32[]{:S(2)}, u32[]{:S(2)}) collective-permute-start(bf16[64,512]{1,0:T(8,128)(2,1)S(1)} %get-tuple-element.20), channel_id=1, source_target_pairs={{0,256},{1,0},{256,257},{257,1},{2,258},{3,2},{258,259},{259,3},{4... | collective-permute-start | bytes 196616 | tf_op jit(solution)/shard_map/ppermute | solution.py:118
  22.2 6.2 %collective-permute-start.3 = (bf16[64,256]{1,0:T(8,128)(2,1)S(1)}, bf16[64,256]{1,0:T(8,128)(2,1)S(1)}, u32[]{:S(2)}, u32[]{:S(2)}) collective-permute-start(bf16[64,256]{1,0:T(8,128)(2,1)S(1)} %fusion.38), channel_id=1, source_target_pairs={{0,256},{256,0},{1,257},{257,1},{2,258},{258,2},{3,259},{259,3},{4... | collective-permute-start | bytes 98312 | tf_op jit(solution)/shard_map/ppermute | solution.py:31
  86.9 2.2 %copy-start.9 = (bf16[2,512,256]{2,1,0:T(8,128)(2,1)S(1)}, bf16[2,512,256]{2,1,0:T(8,128)(2,1)}, u32[]{:S(2)}) copy-start(bf16[2,512,256]{2,1,0:T(8,128)(2,1)} %param.7) | copy-start | bytes 1572868
  87.2 17.2 %collective-permute-start.4 = (bf16[512,2048]{1,0:T(8,128)(2,1)S(1)}, bf16[512,2048]{1,0:T(8,128)(2,1)S(1)}, u32[]{:S(2)}, u32[]{:S(2)}) collective-permute-start(bf16[512,2048]{1,0:T(8,128)(2,1)S(1)} %bitcast.79), channel_id=1, source_target_pairs={{0,1},{1,0},{2,3},{3,2},{4,5},{5,4},{6,7},{7,6},{8,9},{9,8},{10,11... | collective-permute-start | bytes 6291464 | tf_op jit(solution)/shard_map/ppermute | solution.py:31
  89.2 10.6 %collective-permute-start.5 = (bf16[512,256]{1,0:T(8,128)(2,1)S(1)}, bf16[512,256]{1,0:T(8,128)(2,1)S(1)}, u32[]{:S(2)}, u32[]{:S(2)}) collective-permute-start(bf16[512,256]{1,0:T(8,128)(2,1)S(1)} %get-tuple-element.14), channel_id=1, source_target_pairs={{0,256},{256,0},{1,257},{257,1},{2,258},{258,2},{3,259},{259,3},{4... | collective-permute-start | bytes 786440 | tf_op jit(solution)/shard_map/ppermute | solution.py:31
  99.8 3.8 %collective-permute-start.6 = (bf16[512,512]{1,0:T(8,128)(2,1)S(1)}, bf16[512,512]{1,0:T(8,128)(2,1)S(1)}, u32[]{:S(2)}, u32[]{:S(2)}) collective-permute-start(bf16[512,512]{1,0:T(8,128)(2,1)S(1)} %pad_maximum_fusion.basis), channel_id=1, source_target_pairs={{0,1},{1,0},{2,3},{3,2},{4,5},{5,4},{6,7},{7,6},{8,9},{9,8},{10,11... | collective-permute-start | bytes 1572872 | tf_op jit(solution)/shard_map/ppermute | solution.py:31
  101.8 0.8 copy-start.2
  103.6 0.8 copy-start.7
  104.4 1.4 copy-start.4
  107.1 2.2 %copy-start.1 = (bf16[4096,512]{1,0:T(8,128)(2,1)S(1)}, bf16[4096,512]{1,0:T(8,128)(2,1)}, u32[]{:S(2)}) copy-start(bf16[4096,512]{1,0:T(8,128)(2,1)} %all-gather.5.cloned.1.call-done) | copy-start | bytes 12582916
  109.3 1.0 copy-start.3
  110.3 1.6 copy-start.5
  111.9 1.0 copy-start.8
  116.9 1.0 copy-start.6
  117.9 19.8 %all-to-all-start.1 = ((bf16[8,128,512]{2,1,0:T(8,128)(2,1)}), bf16[8,128,512]{2,1,0:T(8,128)(2,1)S(1)}, u32[]{:S(2)}, u32[]{:S(2)}) async-start(bf16[8,128,512]{2,1,0:T(8,128)(2,1)} %bitcast.82), calls=%async_computation.1 | async-start | bytes 2097152 | tf_op jit(solution)/shard_map/all_to_all | solution.py:149
  125.3 37.4 %all-gather.7.cloned.1.call-start = ((), (), s32[]{:S(2)}) async-start(), calls=%async_computation.4 | async-start | bytes 1310720 | tf_op jit(solution)/shard_map/all_gather | solution.py:147
  157.2 7.3 %collective-permute-start.7 = (bf16[1024,512]{1,0:T(8,128)(2,1)S(1)}, bf16[1024,512]{1,0:T(8,128)(2,1)S(1)}, u32[]{:S(2)}, u32[]{:S(2)}) collective-permute-start(bf16[1024,512]{1,0:T(8,128)(2,1)S(1)} %bitcast.89), channel_id=1, source_target_pairs={{0,1},{1,0},{2,3},{3,2},{4,5},{5,4},{6,7},{7,6},{8,9},{9,8},{10,11... | collective-permute-start | bytes 3145736 | tf_op jit(solution)/shard_map/ppermute | solution.py:31
  164.9 9.7 %collective-permute-start.8 = (f32[256,256]{1,0:T(8,128)S(1)}, f32[256,256]{1,0:T(8,128)S(1)}, u32[]{:S(2)}, u32[]{:S(2)}) collective-permute-start(f32[256,256]{1,0:T(8,128)S(1)} %fusion.1), channel_id=1, source_target_pairs={{0,256},{256,0},{1,257},{257,1},{2,258},{258,2},{3,259},{259,3},{4... | collective-permute-start | bytes 786440 | tf_op jit(solution)/shard_map/ppermute | solution.py:31
Sparse Core Ops, SparseCore 0:
  21.9 85.1 all-gather.4
  128.2 34.4 all-gather.6

commit v5 on v4

--- a/solution.py
+++ b/solution.py
@@ -50,11 +50,13 @@
     total[...] += dot(rows[...], own) + dot(rows_peer[...], other)
     grad = got[:, deep : deep + slots].reshape(blocks * slots, 2 * cols)
     grad_peer = got[:, deep + slots :].reshape(blocks * slots, 2 * cols)
-    part[...] = (dot(grad, basis[...]) + dot(grad_peer, basis_peer[...])).astype(part.dtype)
+    sums = dot(grad, basis[...]) + dot(grad_peer, basis_peer[...])
+    part[...] = sums.astype(part.dtype).reshape(part.shape)
 
     @pl.when(step == pl.num_programs(0) - 1)
     def _():
-        act[...] = total[...].astype(act.dtype)
+        rounded = total[...].astype(act.dtype).astype(F32)
+        act[...] = (rounded * rounded).astype(act.dtype)
 
 
 def project(got, rows, rows_peer, basis, basis_peer, blocks):
@@ -74,15 +76,15 @@
             whole,
         ],
         out_specs=[
-            pl.BlockSpec((blocks * height // 4, keys), lambda i: (i, 0)),
+            pl.BlockSpec((blocks, 1, height // 4, keys), lambda i: (0, i, 0, 0)),
             pl.BlockSpec((count, cols), lambda i: (0, 0)),
         ],
         out_shape=[
-            jax.ShapeDtypeStruct((made, keys), BF16),
+            jax.ShapeDtypeStruct((blocks, nz // blocks, height // 4, keys), BF16),
             jax.ShapeDtypeStruct((count, cols), BF16),
         ],
         scratch_shapes=[pltpu.VMEM((count, cols), F32)],
-        compiler_params=pltpu.CompilerParams(vmem_limit_bytes=32 * 1024 * 1024),
+        compiler_params=pltpu.CompilerParams(vmem_limit_bytes=56 * 1024 * 1024),
         cost_estimate=pl.CostEstimate(
             flops=4 * made * basis.shape[0] * keys + 4 * count * rows.shape[1] * cols,
             bytes_accessed=2 * (got.size + 2 * rows.size + 2 * basis.size + made * keys + count * cols),
@@ -138,25 +140,27 @@
     rows = lax.all_gather(rows, "zh", axis=0, tiled=True)
     copies = jnp.broadcast_to(rows[None], (planes,) + rows.shape)
     rows = lax.all_to_all(copies, PLANE, 0, 0, tiled=True)
-    rows = rows.transpose(1, 0, 2).reshape(rows.shape[1], planes * share)
+    rows = rows.reshape(planes, nz // nl, 2, capacity, share).transpose(2, 1, 3, 0, 4)
+    rows = rows.reshape(2 * nz // nl * capacity, planes * share)
     rows_peer = swap(rows, "c")
     basis_half = jnp.concatenate([mine(grad_basis), swap(theirs(grad_basis), "yl")], axis=1)
     basis_peer = swap(basis_half, "c")
 
-    part, act_proj = project(gathered, rows, rows_peer, basis_half, basis_peer, nl)
-    act_all = lax.all_gather(act_proj, "zl", axis=0, tiled=False)
+    part, act_sq = project(gathered, rows, rows_peer, basis_half, basis_peer, nl)
+    act_sq = lax.all_gather(act_sq, "zl", axis=0, tiled=False)
 
-    parts = lax.all_to_all(part.reshape(planes, part.shape[0] // planes, -1), PLANE, 0, 0, tiled=True)
+    parts = lax.all_to_all(part.reshape(planes, nz * capacity // planes, -1), PLANE, 0, 0, tiled=True)
     grad_sq = jnp.square(jnp.sum(parts.astype(F32), axis=0)).astype(BF16)
     copies = jnp.broadcast_to(grad_sq[None], (planes,) + grad_sq.shape)
     grad_sq = lax.all_to_all(copies, PLANE, 0, 0, tiled=True).reshape(nz * capacity, -1)
     grad_sq_other = swap(grad_sq, "c")
 
-    act_sq = jnp.square(act_all.astype(F32)).astype(BF16)
-    act_sq = act_sq.reshape(nl, nz // nl, 2, capacity, cols).transpose(2, 1, 0, 3, 4)
-    act_sq = act_sq.reshape(2, nz * capacity, cols)
-    act_first = lax.dynamic_index_in_dim(act_sq, core, 0, keepdims=False)
-    act_second = lax.dynamic_index_in_dim(act_sq, 1 - core, 0, keepdims=False)
+    act_sq = act_sq.reshape(nl, 2, nz // nl * capacity, cols)
+
+    def group(index):
+        return lax.dynamic_index_in_dim(act_sq, index, 1, keepdims=False).reshape(nz * capacity, cols)
+
+    act_first, act_second = group(core), group(1 - core)
 
     def outer(g, a):
         return lax.dot_general(g, a, (((0,), (0,)), ((), ())), preferred_element_type=F32)

time: 183 us -> 181 us (0.989); the launches traced: 183 us -> 179 us
  local copies, waits for them, and re-layouts: 11.3 us -> 6.04 us
  Pallas kernels: 3.97 us -> 6.87 us
    unnamed x20 -> x11, local copies, waits for them, and re-layouts: 9.78 us -> 2.29 us
    pallas_call x1, Pallas kernels: 3.97 us -> 6.87 us  [project(): pl.pallas_call(project_kernel, grid=(nz // blocks,), in_specs=[pl.BlockSp...]
  transfers between devices with their start and end apart: 12 -> 12, of which waited for: 8 -> 8; matrix products, arithmetic and copies ran while one was open for 4% -> 5% of each run, Pallas kernels for 0% -> 0%
where the time goes in v5:
time: 181 us; the launch traced here: 179 us
  blocking collectives  78.5 us (43%)
  waiting for transfers between devices  34.6 us (19%)
  starting transfers between devices  31.5 us (17%)
  between operations  13.7 us (8%)
  Pallas kernels  6.87 us (4%)
  local copies, waits for them, and re-layouts  6.04 us (3%)
  matrix products  4.05 us (2%)
  other arithmetic  3.46 us (2%)
    all_to_all x1, blocking collectives, per_device(): rows = lax.all_to_all(copies, PLANE, 0, 0, tiled=True)  29.7 us
    all_gather x1, blocking collectives, per_device(): rows = lax.all_gather(rows, 'zh', axis=0, tiled=True)  28.7 us
    all_to_all x1, blocking collectives, per_device(): lax.all_to_all(copies, PLANE, 0, 0, tiled=True).reshape(nz * capacity, -1)  20 us
    ppermute x7, starting transfers between devices, swap(): return lax.ppermute(x, axis, [(0, 1), (1, 0)])  19.1 us
    ppermute x7, waiting for transfers between devices, swap(): return lax.ppermute(x, axis, [(0, 1), (1, 0)])  18.1 us
    all_to_all x1, waiting for transfers between devices, per_device(): lax.all_to_all(part.reshape(planes, nz * capacity // planes, -1), PLANE,...  12.8 us
    all_to_all x1, starting transfers between devices, per_device(): lax.all_to_all(part.reshape(planes, nz * capacity // planes, -1), PLANE,...  7.44 us
    pallas_call x1, Pallas kernels, project(): pl.pallas_call(project_kernel, grid=(nz // blocks,), in_specs=[pl.BlockSp...  6.87 us
  transfers between devices with their start and end apart: 12, of which 8 were waited for; matrix products, arithmetic and copies ran while one was open for 5% of the time, Pallas kernels for 0%

profile of v5, /device:TPU:6, one launch (start us, length us, event | category | flops | bytes accessed | tf_op | source)
XLA Modules:
  0.0 178.6 jit_solution(10104083739467904366)
XLA Ops:
  7.5 3.5 %collective-permute-start = (bf16[128,256]{1,0:T(8,128)(2,1)S(1)}, bf16[128,256]{1,0:T(8,128)(2,1)S(1)}, u32[]{:S(2)}, u32[]{:S(2)}) collective-permute-start(bf16[128,256]{1,0:T(8,128)(2,1)S(1)} %dynamic-slice_bitcast_fusion.2), channel_id=1, source_target_pairs={{0,256},{256,0},{1,257},{257,1},{2,258},{258,2},{3,259},{259,3},{4... | collective-permute-start | bytes 196616 | tf_op jit(solution)/shard_map/ppermute | solution.py:31
  11.9 1.1 fusion.3
  13.0 1.1 fusion.2
  14.8 4.3 %collective-permute-start.2 = (bf16[64,512]{1,0:T(8,128)(2,1)S(1)}, bf16[64,512]{1,0:T(8,128)(2,1)S(1)}, u32[]{:S(2)}, u32[]{:S(2)}) collective-permute-start(bf16[64,512]{1,0:T(8,128)(2,1)S(1)} %get-tuple-element.22), channel_id=1, source_target_pairs={{0,256},{1,0},{256,257},{257,1},{2,258},{3,2},{258,259},{259,3},{4... | collective-permute-start | bytes 196616 | tf_op jit(solution)/shard_map/ppermute | solution.py:120
  20.1 1.0 collective-permute-done.2
  22.2 4.3 %collective-permute-start.3 = (bf16[64,256]{1,0:T(8,128)(2,1)S(1)}, bf16[64,256]{1,0:T(8,128)(2,1)S(1)}, u32[]{:S(2)}, u32[]{:S(2)}) collective-permute-start(bf16[64,256]{1,0:T(8,128)(2,1)S(1)} %fusion.30), channel_id=1, source_target_pairs={{0,256},{256,0},{1,257},{257,1},{2,258},{258,2},{3,259},{259,3},{4... | collective-permute-start | bytes 98312 | tf_op jit(solution)/shard_map/ppermute | solution.py:31
  26.5 1.9 %collective-permute-done.3 = bf16[64,256]{1,0:T(8,128)(2,1)S(1)} collective-permute-done((bf16[64,256]{1,0:T(8,128)(2,1)S(1)}, bf16[64,256]{1,0:T(8,128)(2,1)S(1)}, u32[]{:S(2)}, u32[]{:S(2)}) %collective-permute-start.3) | collective-permute-done | bytes 32800 | tf_op jit(solution)/shard_map/ppermute | solution.py:31
  28.4 28.7 %all_gather.17 = bf16[512,256]{1,0:T(8,128)(2,1)S(1)} all-gather(bf16[128,256]{1,0:T(8,128)(2,1)S(1)} %pad_maximum_fusion.3), channel_id=1, replica_groups=mesh['yl'=2,'zh'=4,'zl'=4,'yh'=2,'x'=4,'c'=2] {'zh'}, dimensions={0}, use_global_device_ids=true | all-gather | bytes 327680 | tf_op jit(solution)/shard_map/all_gather | solution.py:140
  57.2 29.7 %all_to_all.15 = bf16[8,512,256]{2,1,0:T(8,128)(2,1)S(1)} all-to-all(bf16[8,512,256]{2,1,0:T(8,128)(2,1)S(1)} %broadcast_in_dim.12), channel_id=1, replica_groups=mesh['yl'=2,'zh'=4,'zl'=4,'yh'=2,'x'=4,'c'=2] {'yh','x'}, dimensions={0} | all-to-all | bytes 4194304 | tf_op jit(solution)/shard_map/all_to_all | solution.py:142
  86.9 1.3 copy.6
  88.9 1.9 %collective-permute-start.4 = (bf16[512,2048]{1,0:T(8,128)(2,1)S(1)}, bf16[512,2048]{1,0:T(8,128)(2,1)}, u32[]{:S(2)}, u32[]{:S(2)}) collective-permute-start(bf16[512,2048]{1,0:T(8,128)(2,1)S(1)} %bitcast.75), channel_id=1, source_target_pairs={{0,1},{1,0},{2,3},{3,2},{4,5},{5,4},{6,7},{7,6},{8,9},{9,8},{10,11... | collective-permute-start | bytes 6291464 | tf_op jit(solution)/shard_map/ppermute | solution.py:31
  90.9 2.2 %collective-permute-start.5 = (bf16[512,256]{1,0:T(8,128)(2,1)S(1)}, bf16[512,256]{1,0:T(8,128)(2,1)S(1)}, u32[]{:S(2)}, u32[]{:S(2)}) collective-permute-start(bf16[512,256]{1,0:T(8,128)(2,1)S(1)} %get-tuple-element.16), channel_id=1, source_target_pairs={{0,256},{256,0},{1,257},{257,1},{2,258},{258,2},{3,259},{259,3},{4... | collective-permute-start | bytes 786440 | tf_op jit(solution)/shard_map/ppermute | solution.py:31
  93.1 8.4 %collective-permute-done.5 = bf16[512,256]{1,0:T(8,128)(2,1)S(1)} collective-permute-done((bf16[512,256]{1,0:T(8,128)(2,1)S(1)}, bf16[512,256]{1,0:T(8,128)(2,1)S(1)}, u32[]{:S(2)}, u32[]{:S(2)}) %collective-permute-start.5) | collective-permute-done | bytes 262176 | tf_op jit(solution)/shard_map/ppermute | solution.py:31
  102.4 1.9 %collective-permute-start.6 = (bf16[512,512]{1,0:T(8,128)(2,1)S(1)}, bf16[512,512]{1,0:T(8,128)(2,1)S(1)}, u32[]{:S(2)}, u32[]{:S(2)}) collective-permute-start(bf16[512,512]{1,0:T(8,128)(2,1)S(1)} %pad_maximum_fusion.basis), channel_id=1, source_target_pairs={{0,1},{1,0},{2,3},{3,2},{4,5},{5,4},{6,7},{7,6},{8,9},{9,8},{10,11... | collective-permute-start | bytes 1572872 | tf_op jit(solution)/shard_map/ppermute | solution.py:31
  104.3 1.9 %collective-permute-done.6.basis_peer = bf16[512,512]{1,0:T(8,128)(2,1)S(1)} collective-permute-done((bf16[512,512]{1,0:T(8,128)(2,1)S(1)}, bf16[512,512]{1,0:T(8,128)(2,1)S(1)}, u32[]{:S(2)}, u32[]{:S(2)}) %collective-permute-start.6) | collective-permute-done | bytes 524320 | tf_op jit(solution)/shard_map/ppermute | solution.py:31
  107.1 6.9 %shard_map.55 = (bf16[4,4,64,512]{3,2,1,0:T(8,128)(2,1)}, bf16[512,256]{1,0:T(8,128)(2,1)}) custom-call(bf16[16,256,512]{2,1,0:T(8,128)(2,1)} %bitcast.77, bf16[512,2048]{1,0:T(8,128)(2,1)} %bitcast.76, bf16[512,2048]{1,0:T(8,128)(2,1)} %collective-permute-done.4.rows_peer, bf16[512,512]{1,0:T(8,128)(2,1)} %copy-done.2, bf16[512,512]{1,0:T(8,128)(2,1)} %copy-done.3), custom_call_target="tpu_custom_call" | custom-call | flops 2147483648 | bytes 10747904 | tf_op jit(solution)/shard_map/pallas_call | solution.py:68
  114.0 7.4 %all-to-all-start.1 = ((bf16[8,128,512]{2,1,0:T(8,128)(2,1)}), bf16[8,128,512]{2,1,0:T(8,128)(2,1)S(1)}, u32[]{:S(2)}, u32[]{:S(2)}) async-start(bf16[8,128,512]{2,1,0:T(8,128)(2,1)} %bitcast.83), calls=%async_computation.1 | async-start | bytes 2097152 | tf_op jit(solution)/shard_map/all_to_all | solution.py:152
  122.2 12.8 %all-to-all-done.1 = bf16[8,128,512]{2,1,0:T(8,128)(2,1)S(1)} async-done(((bf16[8,128,512]{2,1,0:T(8,128)(2,1)}), bf16[8,128,512]{2,1,0:T(8,128)(2,1)S(1)}, u32[]{:S(2)}, u32[]{:S(2)}) %all-to-all-start.1) | async-done | bytes 1048608 | tf_op jit(solution)/shard_map/all_to_all | solution.py:152
  135.2 20.0 %all_to_all.16 = bf16[8,128,512]{2,1,0:T(8,128)(2,1)S(1)} all-to-all(bf16[8,128,512]{2,1,0:T(8,128)(2,1)S(1)} %broadcast_in_dim.13), channel_id=1, replica_groups=mesh['yl'=2,'zh'=4,'zl'=4,'yh'=2,'x'=4,'c'=2] {'yh','x'}, dimensions={0} | all-to-all | bytes 2097152 | tf_op jit(solution)/shard_map/all_to_all | solution.py:155
  155.2 1.9 %collective-permute-start.7 = (bf16[1024,512]{1,0:T(8,128)(2,1)S(1)}, bf16[1024,512]{1,0:T(8,128)(2,1)S(1)}, u32[]{:S(2)}, u32[]{:S(2)}) collective-permute-start(bf16[1024,512]{1,0:T(8,128)(2,1)S(1)} %bitcast.80), channel_id=1, source_target_pairs={{0,1},{1,0},{2,3},{3,2},{4,5},{5,4},{6,7},{7,6},{8,9},{9,8},{10,11... | collective-permute-start | bytes 3145736 | tf_op jit(solution)/shard_map/ppermute | solution.py:31
  157.2 1.8 all-gather.7.cloned.1.call-done
  158.9 1.3 constant_dynamic-slice_fusion
  160.9 3.4 %collective-permute-start.8 = (f32[256,256]{1,0:T(8,128)S(1)}, f32[256,256]{1,0:T(8,128)S(1)}, u32[]{:S(2)}, u32[]{:S(2)}) collective-permute-start(f32[256,256]{1,0:T(8,128)S(1)} %fusion.1), channel_id=1, source_target_pairs={{0,256},{256,0},{1,257},{257,1},{2,258},{258,2},{3,259},{259,3},{4... | collective-permute-start | bytes 786440 | tf_op jit(solution)/shard_map/ppermute | solution.py:31
  164.6 6.0 %collective-permute-done.8 = f32[256,256]{1,0:T(8,128)S(1)} collective-permute-done((f32[256,256]{1,0:T(8,128)S(1)}, f32[256,256]{1,0:T(8,128)S(1)}, u32[]{:S(2)}, u32[]{:S(2)}) %collective-permute-start.8) | collective-permute-done | bytes 262176 | tf_op jit(solution)/shard_map/ppermute | solution.py:31
  (45 shorter events, 10.4 us)
Async XLA Ops:
  6.5 15.3 %copy-start = (bf16[128,4096]{1,0:T(8,128)(2,1)S(1)}, bf16[128,4096]{1,0:T(8,128)(2,1)}, u32[]{:S(2)}) copy-start(bf16[128,4096]{1,0:T(8,128)(2,1)} %param.5) | copy-start | bytes 3145732
  6.5 100.6 %all-gather.5.cloned.1.call-start = ((), (), s32[]{:S(2)}) async-start(), calls=%async_computation.3 | async-start | bytes 4456448 | tf_op jit(solution)/shard_map/all_gather | solution.py:130
  7.5 11.7 %collective-permute-start = (bf16[128,256]{1,0:T(8,128)(2,1)S(1)}, bf16[128,256]{1,0:T(8,128)(2,1)S(1)}, u32[]{:S(2)}, u32[]{:S(2)}) collective-permute-start(bf16[128,256]{1,0:T(8,128)(2,1)S(1)} %dynamic-slice_bitcast_fusion.2), channel_id=1, source_target_pairs={{0,256},{256,0},{1,257},{257,1},{2,258},{258,2},{3,259},{259,3},{4... | collective-permute-start | bytes 196616 | tf_op jit(solution)/shard_map/ppermute | solution.py:31
  14.2 5.9 %collective-permute-start.1 = (bf16[64,512]{1,0:T(8,128)(2,1)S(1)}, bf16[64,512]{1,0:T(8,128)(2,1)S(1)}, u32[]{:S(2)}, u32[]{:S(2)}) collective-permute-start(bf16[64,512]{1,0:T(8,128)(2,1)S(1)} %get-tuple-element.21), channel_id=1, source_target_pairs={{0,0},{1,256},{256,1},{257,257},{2,2},{3,258},{258,3},{259,259},{4... | collective-permute-start | bytes 196616 | tf_op jit(solution)/shard_map/ppermute | solution.py:117
  14.8 6.2 %collective-permute-start.2 = (bf16[64,512]{1,0:T(8,128)(2,1)S(1)}, bf16[64,512]{1,0:T(8,128)(2,1)S(1)}, u32[]{:S(2)}, u32[]{:S(2)}) collective-permute-start(bf16[64,512]{1,0:T(8,128)(2,1)S(1)} %get-tuple-element.22), channel_id=1, source_target_pairs={{0,256},{1,0},{256,257},{257,1},{2,258},{3,2},{258,259},{259,3},{4... | collective-permute-start | bytes 196616 | tf_op jit(solution)/shard_map/ppermute | solution.py:120
  22.2 6.2 %collective-permute-start.3 = (bf16[64,256]{1,0:T(8,128)(2,1)S(1)}, bf16[64,256]{1,0:T(8,128)(2,1)S(1)}, u32[]{:S(2)}, u32[]{:S(2)}) collective-permute-start(bf16[64,256]{1,0:T(8,128)(2,1)S(1)} %fusion.30), channel_id=1, source_target_pairs={{0,256},{256,0},{1,257},{257,1},{2,258},{258,2},{3,259},{259,3},{4... | collective-permute-start | bytes 98312 | tf_op jit(solution)/shard_map/ppermute | solution.py:31
  88.2 2.6 %copy-start.4 = (bf16[2,512,256]{2,1,0:T(8,128)(2,1)S(1)}, bf16[2,512,256]{2,1,0:T(8,128)(2,1)}, u32[]{:S(2)}) copy-start(bf16[2,512,256]{2,1,0:T(8,128)(2,1)} %param.7) | copy-start | bytes 1572868
  88.9 18.2 %copy-start.1 = (bf16[64,8,8,256]{3,1,2,0:T(8,128)(2,1)}, bf16[64,8,8,256]{3,1,2,0:T(8,128)(2,1)S(1)}, u32[]{:S(2)}) copy-start(bf16[64,8,8,256]{3,1,2,0:T(8,128)(2,1)S(1)} %copy.7) | copy-start | bytes 6291460
  88.9 18.0 %collective-permute-start.4 = (bf16[512,2048]{1,0:T(8,128)(2,1)S(1)}, bf16[512,2048]{1,0:T(8,128)(2,1)}, u32[]{:S(2)}, u32[]{:S(2)}) collective-permute-start(bf16[512,2048]{1,0:T(8,128)(2,1)S(1)} %bitcast.75), channel_id=1, source_target_pairs={{0,1},{1,0},{2,3},{3,2},{4,5},{5,4},{6,7},{7,6},{8,9},{9,8},{10,11... | collective-permute-start | bytes 6291464 | tf_op jit(solution)/shard_map/ppermute | solution.py:31
  90.9 10.6 %collective-permute-start.5 = (bf16[512,256]{1,0:T(8,128)(2,1)S(1)}, bf16[512,256]{1,0:T(8,128)(2,1)S(1)}, u32[]{:S(2)}, u32[]{:S(2)}) collective-permute-start(bf16[512,256]{1,0:T(8,128)(2,1)S(1)} %get-tuple-element.16), channel_id=1, source_target_pairs={{0,256},{256,0},{1,257},{257,1},{2,258},{258,2},{3,259},{259,3},{4... | collective-permute-start | bytes 786440 | tf_op jit(solution)/shard_map/ppermute | solution.py:31
  101.6 0.8 copy-start.2
  102.4 3.8 %collective-permute-start.6 = (bf16[512,512]{1,0:T(8,128)(2,1)S(1)}, bf16[512,512]{1,0:T(8,128)(2,1)S(1)}, u32[]{:S(2)}, u32[]{:S(2)}) collective-permute-start(bf16[512,512]{1,0:T(8,128)(2,1)S(1)} %pad_maximum_fusion.basis), channel_id=1, source_target_pairs={{0,1},{1,0},{2,3},{3,2},{4,5},{5,4},{6,7},{7,6},{8,9},{9,8},{10,11... | collective-permute-start | bytes 1572872 | tf_op jit(solution)/shard_map/ppermute | solution.py:31
  106.2 0.8 copy-start.3
  114.0 20.9 %all-to-all-start.1 = ((bf16[8,128,512]{2,1,0:T(8,128)(2,1)}), bf16[8,128,512]{2,1,0:T(8,128)(2,1)S(1)}, u32[]{:S(2)}, u32[]{:S(2)}) async-start(bf16[8,128,512]{2,1,0:T(8,128)(2,1)} %bitcast.83), calls=%async_computation.1 | async-start | bytes 2097152 | tf_op jit(solution)/shard_map/all_to_all | solution.py:152
  121.4 37.5 %all-gather.7.cloned.1.call-start = ((), (), s32[]{:S(2)}) async-start(), calls=%async_computation.4 | async-start | bytes 1310720 | tf_op jit(solution)/shard_map/all_gather | solution.py:150
  155.2 5.3 %collective-permute-start.7 = (bf16[1024,512]{1,0:T(8,128)(2,1)S(1)}, bf16[1024,512]{1,0:T(8,128)(2,1)S(1)}, u32[]{:S(2)}, u32[]{:S(2)}) collective-permute-start(bf16[1024,512]{1,0:T(8,128)(2,1)S(1)} %bitcast.80), channel_id=1, source_target_pairs={{0,1},{1,0},{2,3},{3,2},{4,5},{5,4},{6,7},{7,6},{8,9},{9,8},{10,11... | collective-permute-start | bytes 3145736 | tf_op jit(solution)/shard_map/ppermute | solution.py:31
  160.9 9.7 %collective-permute-start.8 = (f32[256,256]{1,0:T(8,128)S(1)}, f32[256,256]{1,0:T(8,128)S(1)}, u32[]{:S(2)}, u32[]{:S(2)}) collective-permute-start(f32[256,256]{1,0:T(8,128)S(1)} %fusion.1), channel_id=1, source_target_pairs={{0,256},{256,0},{1,257},{257,1},{2,258},{258,2},{3,259},{259,3},{4... | collective-permute-start | bytes 786440 | tf_op jit(solution)/shard_map/ppermute | solution.py:31
Sparse Core Ops, SparseCore 0:
  22.0 85.1 all-gather.4
  124.4 34.5 all-gather.6

commit v6 on v5

v6 whole, which is shorter than its diff:
```python
import jax
import jax.numpy as jnp
from jax import lax
from jax.experimental import pallas as pl
from jax.experimental.pallas import tpu as pltpu
from jax.sharding import Mesh, PartitionSpec as P

F32, BF16 = jnp.float32, jnp.bfloat16
PLANE = ("yh", "x")


def pick_kernel(ids, grads, picked, chooser):
    experts, capacity, rows = chooser.shape
    first, second = ids[0:1, :], ids[1:2, :]
    source = lax.broadcasted_iota(jnp.int32, (rows, rows), 0)
    target = lax.broadcasted_iota(jnp.int32, (rows, rows), 1)
    before = (source <= target).astype(F32).astype(BF16)
    slot_order = lax.broadcasted_iota(jnp.int32, (capacity, rows), 0)
    for expert in range(experts):
        routed = jnp.logical_or(first == expert, second == expert)
        flags = jnp.broadcast_to(routed.astype(F32), (16, rows)).astype(BF16)
        slot_index = dot(flags, before)[0:1].astype(jnp.int32) - 1
        hit = jnp.logical_and(slot_order == slot_index, routed)
        chosen = hit.astype(F32).astype(BF16)
        chooser[expert] = chosen
        picked[expert] = dot(chosen, grads[expert]).astype(BF16)


def pick_grads(ids, grads, capacity):
    experts, rows, hidden = grads.shape
    return pl.pallas_call(
        pick_kernel,
        out_shape=[
            jax.ShapeDtypeStruct((experts, capacity, hidden), BF16),
            jax.ShapeDtypeStruct((experts, capacity, rows), BF16),
        ],
    )(ids.T, grads)


def swap(x, axis):
    return lax.ppermute(x, axis, [(0, 1), (1, 0)])


def dot(a, b):
    return jnp.dot(a, b, preferred_element_type=F32)


def part_kernel(got, basis, basis_peer, part):
    blocks, height, lanes = got.shape
    slots = height // 2
    own = got[:, :slots].reshape(blocks * slots, lanes)
    other = got[:, slots:].reshape(blocks * slots, lanes)
    sums = dot(own, basis[...]) + dot(other, basis_peer[...])
    part[...] = sums.astype(part.dtype).reshape(part.shape)


def act_kernel(got, rows, rows_peer, act, total):
    step = pl.program_id(0)
    blocks, height, _ = got.shape
    cols = act.shape[1]

    @pl.when(step == 0)
    def _():
        total[...] = jnp.zeros_like(total)

    own = got[:, :, :cols].reshape(blocks * height, cols)
    other = got[:, :, cols:].reshape(blocks * height, cols)
    total[...] += dot(rows[...], own) + dot(rows_peer[...], other)

    @pl.when(step == pl.num_programs(0) - 1)
    def _():
        rounded = total[...].astype(act.dtype).astype(F32)
        act[...] = (rounded * rounded).astype(act.dtype)


ROOM = pltpu.CompilerParams(vmem_limit_bytes=56 * 1024 * 1024)


def partial_sums(got, basis, basis_peer, blocks):
    nz, height, lanes = got.shape
    keys, made = basis.shape[1], height // 4
    whole = pl.BlockSpec(basis.shape, lambda i: (0, 0))
    return pl.pallas_call(
        part_kernel,
        grid=(nz // blocks,),
        in_specs=[pl.BlockSpec((blocks, height // 2, lanes), lambda i: (i, 1, 0)), whole, whole],
        out_specs=pl.BlockSpec((blocks, 1, made, keys), lambda i: (0, i, 0, 0)),
        out_shape=jax.ShapeDtypeStruct((blocks, nz // blocks, made, keys), BF16),
        compiler_params=ROOM,
        cost_estimate=pl.CostEstimate(
            flops=4 * nz * made * lanes * keys,
            bytes_accessed=got.size + 4 * basis.size + 2 * nz * made * keys,
            transcendentals=0,
        ),
    )(got, basis, basis_peer)


def project_act(got, rows, rows_peer, blocks):
    nz, height, lanes = got.shape
    count, cols = rows.shape[0], lanes // 2
    row_block = pl.BlockSpec((count, blocks * height // 2), lambda i: (0, i))
    return pl.pallas_call(
        act_kernel,
        grid=(nz // blocks,),
        in_specs=[
            pl.BlockSpec((blocks, height // 2, lanes), lambda i: (i, 0, 0)),
            row_block,
            row_block,
        ],
        out_specs=pl.BlockSpec((count, cols), lambda i: (0, 0)),
        out_shape=jax.ShapeDtypeStruct((count, cols), BF16),
        scratch_shapes=[pltpu.VMEM((count, cols), F32)],
        compiler_params=ROOM,
        cost_estimate=pl.CostEstimate(
            flops=4 * count * rows.shape[1] * cols,
            bytes_accessed=got.size + 4 * rows.size + 2 * count * cols,
            transcendentals=0,
        ),
    )(got, rows, rows_peer)


def per_device(tokens, act_basis, grad_basis, grads, expert_ids):
    tok_rows, width = tokens.shape
    capacity = tok_rows // 2
    nl = lax.axis_size("zl")
    nz = lax.axis_size("zh") * nl
    token_total = tok_rows * lax.axis_size("yl") * nz
    planes = lax.axis_size("yh") * lax.axis_size("x")
    yl, core = lax.axis_index("yl"), lax.axis_index("c")
    cols = act_basis.shape[2]

    def mine(x):
        return lax.dynamic_index_in_dim(x, yl, 0, keepdims=False)

    def theirs(x):
        return lax.dynamic_index_in_dim(x, 1 - yl, 0, keepdims=False)

    act_other = swap(theirs(act_basis), "yl")
    picked_grad, choose = pick_grads(expert_ids, grads, capacity)
    straight = [(2 * y + c, 2 * c + y) for y in range(2) for c in range(2)]
    crossed = [(2 * y + c, 2 * (1 - c) + y) for y in range(2) for c in range(2)]
    grad_a = lax.ppermute(
        lax.dynamic_index_in_dim(picked_grad, core, 0, keepdims=False), ("yl", "c"), straight
    )
    grad_b = lax.ppermute(
        lax.dynamic_index_in_dim(picked_grad, 1 - core, 0, keepdims=False), ("yl", "c"), crossed
    )
    same, act_own = yl == core, mine(act_basis)
    act_rows = jnp.concatenate(
        [jnp.where(same, act_own, act_other), jnp.where(same, act_other, act_own)], axis=1
    )
    payload = jnp.concatenate(
        [act_rows, jnp.where(same, grad_a, grad_b), jnp.where(same, grad_b, grad_a)], axis=0
    )
    gathered = lax.all_gather(payload, ("zh", "zl"), axis=0, tiled=False)

    plane = lax.axis_index("yh") * lax.axis_size("x") + lax.axis_index("x")
    share = width // (2 * planes)
    piece = lax.dynamic_slice_in_dim(tokens, core * (width // 2) + plane * share, share, 1)
    picked_act = jnp.stack([dot(choose[e], piece).astype(BF16) for e in range(2)])
    act_in, act_in_other = mine(picked_act), swap(theirs(picked_act), "yl")
    rows = jnp.concatenate(
        [jnp.where(yl == 0, act_in, act_in_other), jnp.where(yl == 0, act_in_other, act_in)], axis=0
    )
    rows = lax.all_gather(rows, "zh", axis=0, tiled=True)
    basis_half = jnp.concatenate([mine(grad_basis), swap(theirs(grad_basis), "yl")], axis=1)
    rows, basis_half = lax.optimization_barrier((rows, basis_half))
    basis_peer = swap(basis_half, "c")
    copies = jnp.broadcast_to(rows[None], (planes,) + rows.shape)
    rows = lax.all_to_all(copies, PLANE, 0, 0, tiled=True)
    rows = rows.reshape(planes, nz // nl, 2, capacity, share).transpose(2, 1, 3, 0, 4)
    rows = rows.reshape(2 * nz // nl * capacity, planes * share)
    rows_peer = swap(rows, "c")

    part = partial_sums(gathered, basis_half, basis_peer, nl)
    act_sq = lax.all_gather(project_act(gathered, rows, rows_peer, nl), "zl", axis=0, tiled=False)

    parts = lax.all_to_all(part.reshape(planes, nz * capacity // planes, -1), PLANE, 0, 0, tiled=True)
    grad_sq = jnp.square(jnp.sum(parts.astype(F32), axis=0)).astype(BF16)
    copies = jnp.broadcast_to(grad_sq[None], (planes,) + grad_sq.shape)
    grad_sq = lax.all_to_all(copies, PLANE, 0, 0, tiled=True).reshape(nz * capacity, -1)
    grad_sq_other = swap(grad_sq, "c")

    act_sq = act_sq.reshape(nl, 2, nz // nl * capacity, cols)

    def group(index):
        return lax.dynamic_index_in_dim(act_sq, index, 1, keepdims=False).reshape(nz * capacity, cols)

    act_first, act_second = group(core), group(1 - core)

    def outer(g, a):
        return lax.dot_general(g, a, (((0,), (0,)), ((), ())), preferred_element_type=F32)

    def block(lo, hi):
        own, other = grad_sq[:, lo:hi], grad_sq_other[:, lo:hi]
        return (outer(own, act_first) + outer(other, act_second)) / token_total

    keys = grad_sq.shape[1]
    got = swap(block(keys // 2, keys), "yl")
    kept = block(0, keys // 2)
    expert = lax.broadcasted_iota(jnp.int32, (2,) + kept.shape, 0)
    return jnp.where(expert == yl, kept[None], got[None])


def solution(mesh):
    dp, owner = mesh.devices.shape
    split = Mesh(
        mesh.devices.reshape(2, dp // 8, 4, 2, owner // 4, 2), ("yl", "zh", "zl", "yh", "x", "c")
    )
    rows, cols = ("yl", "zh", "zl"), ("yh", "x", "c")
    placed = (
        P(rows, None),
        P(None, rows, cols),
        P(None, cols, rows),
        P(None, rows, cols),
        P(rows, None),
    )
    return jax.shard_map(
        per_device, mesh=split, in_specs=placed, out_specs=P(None, rows, cols), check_vma=False
    )
```

time: 181 us -> 182 us (level)
  waiting for transfers between devices: 34.6 us -> 40 us
  blocking collectives: 78.5 us -> 73.3 us
  Pallas kernels: 6.87 us -> 11.9 us
    all_gather x1, waiting for transfers between devices: 0.15 us -> 11.9 us  [per_device(): gathered = lax.all_gather(payload, ('zh', 'zl'), axis=0, tiled=False)]
    all_gather x1, waiting for transfers between devices: 1.77 us -> 9.63 us  [per_device(): lax.all_gather(project_act(gathered, rows, rows_peer, nl), 'zl', axis=0,...]
    all_to_all x1, waiting for transfers between devices: 12.8 us -> 5.73 us  [per_device(): lax.all_to_all(part.reshape(planes, nz * capacity // planes, -1), PLANE,...]
    ppermute x7, waiting for transfers between devices: 18.1 us -> 12.8 us  [swap(): return lax.ppermute(x, axis, [(0, 1), (1, 0)])]
    pallas_call x1 -> x3, Pallas kernels: 6.87 us -> 11.9 us  [the longest x1 5.01 us: project_act(): pl.pallas_call(act_kernel, grid=(nz // blocks,), in_specs=[pl.BlockSpec((...]
    all_to_all x1, blocking collectives: 20 us -> 15.7 us  [per_device(): lax.all_to_all(copies, PLANE, 0, 0, tiled=True).reshape(nz * capacity, -1)]
  transfers between devices with their start and end apart: 12 -> 12, of which waited for: 8 -> 6; matrix products, arithmetic and copies ran while one was open for 5% -> 5% of each run, Pallas kernels for 0% -> 5%
where the time goes in v6:
time: 182 us; the launch traced here: 181 us
  blocking collectives  73.3 us (40%)
  waiting for transfers between devices  40 us (22%)
  starting transfers between devices  29.8 us (16%)
  between operations  13.7 us (8%)
  Pallas kernels  11.9 us (7%)
  local copies, waits for them, and re-layouts  5.24 us (3%)
  other arithmetic  4.02 us (2%)
  matrix products  3.06 us (2%)
    all_to_all x1, blocking collectives, per_device(): rows = lax.all_to_all(copies, PLANE, 0, 0, tiled=True)  29.4 us
    all_gather x1, blocking collectives, per_device(): rows = lax.all_gather(rows, 'zh', axis=0, tiled=True)  28.2 us
    ppermute x7, starting transfers between devices, swap(): return lax.ppermute(x, axis, [(0, 1), (1, 0)])  17.4 us
    all_to_all x1, blocking collectives, per_device(): lax.all_to_all(copies, PLANE, 0, 0, tiled=True).reshape(nz * capacity, -1)  15.7 us
    ppermute x7, waiting for transfers between devices, swap(): return lax.ppermute(x, axis, [(0, 1), (1, 0)])  12.8 us
    all_gather x1, waiting for transfers between devices, per_device(): gathered = lax.all_gather(payload, ('zh', 'zl'), axis=0, tiled=False)  11.9 us
    all_gather x1, waiting for transfers between devices, per_device(): lax.all_gather(project_act(gathered, rows, rows_peer, nl), 'zl', axis=0,...  9.63 us
    all_to_all x1, starting transfers between devices, per_device(): lax.all_to_all(part.reshape(planes, nz * capacity // planes, -1), PLANE,...  6.97 us
  transfers between devices with their start and end apart: 12, of which 6 were waited for; matrix products, arithmetic and copies ran while one was open for 5% of the time, Pallas kernels for 5%

profile of v6, /device:TPU:6, one launch (start us, length us, event | category | flops | bytes accessed | tf_op | source)
XLA Modules:
  0.0 181.1 jit_solution(10957854138312456225)
XLA Ops:
  6.5 2.2 %shard_map.55 = (bf16[2,64,512]{2,1,0:T(8,128)(2,1)}, bf16[2,64,128]{2,1,0:T(8,128)(2,1)}) custom-call(s32[2,128]{1,0:T(2,128)} %bitcast.63, bf16[2,128,512]{2,1,0:T(8,128)(2,1)} %grads.1), custom_call_target="tpu_custom_call" | custom-call | tf_op jit(solution)/shard_map/pallas_call | solution.py:31
  10.3 4.7 %collective-permute-start.2 = (bf16[64,512]{1,0:T(8,128)(2,1)S(1)}, bf16[64,512]{1,0:T(8,128)(2,1)S(1)}, u32[]{:S(2)}, u32[]{:S(2)}) collective-permute-start(bf16[64,512]{1,0:T(8,128)(2,1)S(1)} %get-tuple-element.22), channel_id=1, source_target_pairs={{0,256},{1,0},{256,257},{257,1},{2,258},{3,2},{258,259},{259,3},{4... | collective-permute-start | bytes 196616 | tf_op jit(solution)/shard_map/ppermute | solution.py:145
  15.9 1.9 %collective-permute-start = (bf16[128,256]{1,0:T(8,128)(2,1)S(1)}, bf16[128,256]{1,0:T(8,128)(2,1)S(1)}, u32[]{:S(2)}, u32[]{:S(2)}) collective-permute-start(bf16[128,256]{1,0:T(8,128)(2,1)S(1)} %dynamic-slice_bitcast_fusion.4), channel_id=1, source_target_pairs={{0,256},{256,0},{1,257},{257,1},{2,258},{258,2},{3,259},{259,3},{4... | collective-permute-start | bytes 196616 | tf_op jit(solution)/shard_map/ppermute | solution.py:41
  17.8 4.2 %collective-permute-done = bf16[128,256]{1,0:T(8,128)(2,1)S(1)} collective-permute-done((bf16[128,256]{1,0:T(8,128)(2,1)S(1)}, bf16[128,256]{1,0:T(8,128)(2,1)S(1)}, u32[]{:S(2)}, u32[]{:S(2)}) %collective-permute-start) | collective-permute-done | bytes 65568 | tf_op jit(solution)/shard_map/ppermute | solution.py:41
  25.4 1.9 %collective-permute-start.3 = (bf16[64,256]{1,0:T(8,128)(2,1)S(1)}, bf16[64,256]{1,0:T(8,128)(2,1)S(1)}, u32[]{:S(2)}, u32[]{:S(2)}) collective-permute-start(bf16[64,256]{1,0:T(8,128)(2,1)S(1)} %fusion.13), channel_id=1, source_target_pairs={{0,256},{256,0},{1,257},{257,1},{2,258},{258,2},{3,259},{259,3},{4... | collective-permute-start | bytes 98312 | tf_op jit(solution)/shard_map/ppermute | solution.py:41
  27.4 3.9 %collective-permute-start.4 = (bf16[512,256]{1,0:T(8,128)(2,1)S(1)}, bf16[512,256]{1,0:T(8,128)(2,1)S(1)}, u32[]{:S(2)}, u32[]{:S(2)}) collective-permute-start(bf16[512,256]{1,0:T(8,128)(2,1)S(1)} %get-tuple-element.16), channel_id=1, source_target_pairs={{0,256},{256,0},{1,257},{257,1},{2,258},{258,2},{3,259},{259,3},{4... | collective-permute-start | bytes 786440 | tf_op jit(solution)/shard_map/ppermute | solution.py:41
  31.4 28.2 %all_gather.17 = bf16[512,256]{1,0:T(8,128)(2,1)S(1)} all-gather(bf16[128,256]{1,0:T(8,128)(2,1)S(1)} %pad_maximum_fusion.2), channel_id=1, replica_groups=mesh['yl'=2,'zh'=4,'zl'=4,'yh'=2,'x'=4,'c'=2] {'zh'}, dimensions={0}, use_global_device_ids=true | all-gather | bytes 327680 | tf_op jit(solution)/shard_map/all_gather | solution.py:165
  59.7 29.4 %all_to_all.15 = bf16[8,512,256]{2,1,0:T(8,128)(2,1)S(1)} all-to-all(bf16[8,512,256]{2,1,0:T(8,128)(2,1)S(1)} %broadcast_in_dim.15), channel_id=1, replica_groups=mesh['yl'=2,'zh'=4,'zl'=4,'yh'=2,'x'=4,'c'=2] {'yh','x'}, dimensions={0} | all-to-all | bytes 4194304 | tf_op jit(solution)/shard_map/all_to_all | solution.py:170
  89.2 1.3 copy.6
  91.1 1.9 %collective-permute-start.6 = (bf16[512,2048]{1,0:T(8,128)(2,1)S(1)}, bf16[512,2048]{1,0:T(8,128)(2,1)}, u32[]{:S(2)}, u32[]{:S(2)}) collective-permute-start(bf16[512,2048]{1,0:T(8,128)(2,1)S(1)} %bitcast.52), channel_id=1, source_target_pairs={{0,1},{1,0},{2,3},{3,2},{4,5},{5,4},{6,7},{7,6},{8,9},{9,8},{10,11... | collective-permute-start | bytes 6291464 | tf_op jit(solution)/shard_map/ppermute | solution.py:41
  93.1 2.4 %collective-permute-start.5 = (bf16[512,512]{1,0:T(8,128)(2,1)S(1)}, bf16[512,512]{1,0:T(8,128)(2,1)}, u32[]{:S(2)}, u32[]{:S(2)}) collective-permute-start(bf16[512,512]{1,0:T(8,128)(2,1)S(1)} %pad_maximum_fusion.basis), channel_id=1, source_target_pairs={{0,1},{1,0},{2,3},{3,2},{4,5},{5,4},{6,7},{7,6},{8,9},{9,8},{10,11... | collective-permute-start | bytes 1572872 | tf_op jit(solution)/shard_map/ppermute | solution.py:41
  95.5 2.6 %collective-permute-done.5.basis_peer = bf16[512,512]{1,0:T(8,128)(2,1)} collective-permute-done((bf16[512,512]{1,0:T(8,128)(2,1)S(1)}, bf16[512,512]{1,0:T(8,128)(2,1)}, u32[]{:S(2)}, u32[]{:S(2)}) %collective-permute-start.5) | collective-permute-done | bytes 524320 | tf_op jit(solution)/shard_map/ppermute | solution.py:41
  98.1 11.9 %all-gather.5.cloned.1.call-done = bf16[4096,512]{1,0:T(8,128)(2,1)} async-done(((bf16[256,512]{1,0:T(8,128)(2,1)}), bf16[4096,512]{1,0:T(8,128)(2,1)}) %all-gather.5.cloned.1.call-update) | async-done | bytes 4194320 | tf_op jit(solution)/shard_map/all_gather | solution.py:155
  110.0 4.7 %shard_map.56 = bf16[4,4,64,512]{3,2,1,0:T(8,128)(2,1)} custom-call(bf16[16,256,512]{2,1,0:T(8,128)(2,1)} %bitcast.48, bf16[512,512]{1,0:T(8,128)(2,1)} %copy-done.2, bf16[512,512]{1,0:T(8,128)(2,1)} %collective-permute-done.5.basis_peer), custom_call_target="tpu_custom_call" | custom-call | flops 1073741824 | bytes 4194304 | tf_op jit(solution)/shard_map/pallas_call | solution.py:83
  114.7 7.0 %all-to-all-start = ((bf16[8,128,512]{2,1,0:T(8,128)(2,1)}), bf16[8,128,512]{2,1,0:T(8,128)(2,1)}, u32[]{:S(2)}, u32[]{:S(2)}) async-start(bf16[8,128,512]{2,1,0:T(8,128)(2,1)} %bitcast.54), calls=%async_computation | async-start | bytes 2097152 | tf_op jit(solution)/shard_map/all_to_all | solution.py:178
  121.7 5.0 %shard_map.57 = bf16[512,256]{1,0:T(8,128)(2,1)} custom-call(bf16[16,256,512]{2,1,0:T(8,128)(2,1)} %bitcast.49, bf16[512,2048]{1,0:T(8,128)(2,1)} %bitcast.53, bf16[512,2048]{1,0:T(8,128)(2,1)} %collective-permute-done.6.rows_peer), custom_call_target="tpu_custom_call" | custom-call | flops 1073741824 | bytes 6553600 | tf_op jit(solution)/shard_map/pallas_call | solution.py:102
  126.7 5.7 %all-to-all-done = bf16[8,128,512]{2,1,0:T(8,128)(2,1)} async-done(((bf16[8,128,512]{2,1,0:T(8,128)(2,1)}), bf16[8,128,512]{2,1,0:T(8,128)(2,1)}, u32[]{:S(2)}, u32[]{:S(2)}) %all-to-all-start) | async-done | bytes 1048608 | tf_op jit(solution)/shard_map/all_to_all | solution.py:178
  132.4 1.4 convert_reduce_fusion
  134.0 15.7 %all_to_all.16 = bf16[8,128,512]{2,1,0:T(8,128)(2,1)S(1)} all-to-all(bf16[8,128,512]{2,1,0:T(8,128)(2,1)S(1)} %broadcast_in_dim.14), channel_id=1, replica_groups=mesh['yl'=2,'zh'=4,'zl'=4,'yh'=2,'x'=4,'c'=2] {'yh','x'}, dimensions={0} | all-to-all | bytes 2097152 | tf_op jit(solution)/shard_map/all_to_all | solution.py:181
  149.7 1.9 %collective-permute-start.7 = (bf16[1024,512]{1,0:T(8,128)(2,1)S(1)}, bf16[1024,512]{1,0:T(8,128)(2,1)S(1)}, u32[]{:S(2)}, u32[]{:S(2)}) collective-permute-start(bf16[1024,512]{1,0:T(8,128)(2,1)S(1)} %bitcast.55), channel_id=1, source_target_pairs={{0,1},{1,0},{2,3},{3,2},{4,5},{5,4},{6,7},{7,6},{8,9},{9,8},{10,11... | collective-permute-start | bytes 3145736 | tf_op jit(solution)/shard_map/ppermute | solution.py:41
  151.6 9.6 %all-gather.7.cloned.1.call-done = bf16[2048,256]{1,0:T(8,128)(2,1)} async-done(((bf16[512,256]{1,0:T(8,128)(2,1)}), bf16[2048,256]{1,0:T(8,128)(2,1)}) %all-gather.7.cloned.1.call-update) | async-done | bytes 1048592 | tf_op jit(solution)/shard_map/all_gather | solution.py:176
  161.3 1.3 constant_dynamic-slice_fusion
  163.6 3.4 %collective-permute-start.8 = (f32[256,256]{1,0:T(8,128)S(1)}, f32[256,256]{1,0:T(8,128)S(1)}, u32[]{:S(2)}, u32[]{:S(2)}) collective-permute-start(f32[256,256]{1,0:T(8,128)S(1)} %fusion.1), channel_id=1, source_target_pairs={{0,256},{256,0},{1,257},{257,1},{2,258},{258,2},{3,259},{259,3},{4... | collective-permute-start | bytes 786440 | tf_op jit(solution)/shard_map/ppermute | solution.py:41
  167.3 6.0 %collective-permute-done.8 = f32[256,256]{1,0:T(8,128)S(1)} collective-permute-done((f32[256,256]{1,0:T(8,128)S(1)}, f32[256,256]{1,0:T(8,128)S(1)}, u32[]{:S(2)}, u32[]{:S(2)}) %collective-permute-start.8) | collective-permute-done | bytes 262176 | tf_op jit(solution)/shard_map/ppermute | solution.py:41
  (41 shorter events, 9.1 us)
Async XLA Ops:
  6.5 17.1 %copy-start = (bf16[128,4096]{1,0:T(8,128)(2,1)S(1)}, bf16[128,4096]{1,0:T(8,128)(2,1)}, u32[]{:S(2)}) copy-start(bf16[128,4096]{1,0:T(8,128)(2,1)} %param.5) | copy-start | bytes 3145732
  6.5 20.8 %copy-start.3 = (bf16[2,512,256]{2,1,0:T(8,128)(2,1)S(1)}, bf16[2,512,256]{2,1,0:T(8,128)(2,1)}, u32[]{:S(2)}) copy-start(bf16[2,512,256]{2,1,0:T(8,128)(2,1)} %param.7) | copy-start | bytes 1572868
  6.5 103.4 %all-gather.5.cloned.1.call-start = ((), (), s32[]{:S(2)}) async-start(), calls=%async_computation.3 | async-start | bytes 4456448 | tf_op jit(solution)/shard_map/all_gather | solution.py:155
  9.6 8.2 %collective-permute-start.1 = (bf16[64,512]{1,0:T(8,128)(2,1)S(1)}, bf16[64,512]{1,0:T(8,128)(2,1)S(1)}, u32[]{:S(2)}, u32[]{:S(2)}) collective-permute-start(bf16[64,512]{1,0:T(8,128)(2,1)S(1)} %get-tuple-element.21), channel_id=1, source_target_pairs={{0,0},{1,256},{256,1},{257,257},{2,2},{3,258},{258,3},{259,259},{4... | collective-permute-start | bytes 196616 | tf_op jit(solution)/shard_map/ppermute | solution.py:142
  10.3 7.5 %collective-permute-start.2 = (bf16[64,512]{1,0:T(8,128)(2,1)S(1)}, bf16[64,512]{1,0:T(8,128)(2,1)S(1)}, u32[]{:S(2)}, u32[]{:S(2)}) collective-permute-start(bf16[64,512]{1,0:T(8,128)(2,1)S(1)} %get-tuple-element.22), channel_id=1, source_target_pairs={{0,256},{1,0},{256,257},{257,1},{2,258},{3,2},{258,259},{259,3},{4... | collective-permute-start | bytes 196616 | tf_op jit(solution)/shard_map/ppermute | solution.py:145
  15.9 6.1 %collective-permute-start = (bf16[128,256]{1,0:T(8,128)(2,1)S(1)}, bf16[128,256]{1,0:T(8,128)(2,1)S(1)}, u32[]{:S(2)}, u32[]{:S(2)}) collective-permute-start(bf16[128,256]{1,0:T(8,128)(2,1)S(1)} %dynamic-slice_bitcast_fusion.4), channel_id=1, source_target_pairs={{0,256},{256,0},{1,257},{257,1},{2,258},{258,2},{3,259},{259,3},{4... | collective-permute-start | bytes 196616 | tf_op jit(solution)/shard_map/ppermute | solution.py:41
  25.4 5.9 %collective-permute-start.3 = (bf16[64,256]{1,0:T(8,128)(2,1)S(1)}, bf16[64,256]{1,0:T(8,128)(2,1)S(1)}, u32[]{:S(2)}, u32[]{:S(2)}) collective-permute-start(bf16[64,256]{1,0:T(8,128)(2,1)S(1)} %fusion.13), channel_id=1, source_target_pairs={{0,256},{256,0},{1,257},{257,1},{2,258},{258,2},{3,259},{259,3},{4... | collective-permute-start | bytes 98312 | tf_op jit(solution)/shard_map/ppermute | solution.py:41
  27.4 32.2 %collective-permute-start.4 = (bf16[512,256]{1,0:T(8,128)(2,1)S(1)}, bf16[512,256]{1,0:T(8,128)(2,1)S(1)}, u32[]{:S(2)}, u32[]{:S(2)}) collective-permute-start(bf16[512,256]{1,0:T(8,128)(2,1)S(1)} %get-tuple-element.16), channel_id=1, source_target_pairs={{0,256},{256,0},{1,257},{257,1},{2,258},{258,2},{3,259},{259,3},{4... | collective-permute-start | bytes 786440 | tf_op jit(solution)/shard_map/ppermute | solution.py:41
  59.6 33.5 %copy-start.2 = (bf16[512,512]{1,0:T(8,128)(2,1)}, bf16[512,512]{1,0:T(8,128)(2,1)S(1)}, u32[]{:S(2)}) copy-start(bf16[512,512]{1,0:T(8,128)(2,1)S(1)} %pad_maximum_fusion.basis) | copy-start | bytes 1572868
  91.1 23.6 %copy-start.1 = (bf16[64,8,8,256]{3,1,2,0:T(8,128)(2,1)}, bf16[64,8,8,256]{3,1,2,0:T(8,128)(2,1)S(1)}, u32[]{:S(2)}) copy-start(bf16[64,8,8,256]{3,1,2,0:T(8,128)(2,1)S(1)} %copy.7) | copy-start | bytes 6291460
  91.1 30.5 %collective-permute-start.6 = (bf16[512,2048]{1,0:T(8,128)(2,1)S(1)}, bf16[512,2048]{1,0:T(8,128)(2,1)}, u32[]{:S(2)}, u32[]{:S(2)}) collective-permute-start(bf16[512,2048]{1,0:T(8,128)(2,1)S(1)} %bitcast.52), channel_id=1, source_target_pairs={{0,1},{1,0},{2,3},{3,2},{4,5},{5,4},{6,7},{7,6},{8,9},{9,8},{10,11... | collective-permute-start | bytes 6291464 | tf_op jit(solution)/shard_map/ppermute | solution.py:41
  93.1 5.0 %collective-permute-start.5 = (bf16[512,512]{1,0:T(8,128)(2,1)S(1)}, bf16[512,512]{1,0:T(8,128)(2,1)}, u32[]{:S(2)}, u32[]{:S(2)}) collective-permute-start(bf16[512,512]{1,0:T(8,128)(2,1)S(1)} %pad_maximum_fusion.basis), channel_id=1, source_target_pairs={{0,1},{1,0},{2,3},{3,2},{4,5},{5,4},{6,7},{7,6},{8,9},{9,8},{10,11... | collective-permute-start | bytes 1572872 | tf_op jit(solution)/shard_map/ppermute | solution.py:41
  114.7 17.7 %all-to-all-start = ((bf16[8,128,512]{2,1,0:T(8,128)(2,1)}), bf16[8,128,512]{2,1,0:T(8,128)(2,1)}, u32[]{:S(2)}, u32[]{:S(2)}) async-start(bf16[8,128,512]{2,1,0:T(8,128)(2,1)} %bitcast.54), calls=%async_computation | async-start | bytes 2097152 | tf_op jit(solution)/shard_map/all_to_all | solution.py:178
  121.7 39.6 %all-gather.7.cloned.1.call-start = ((), (), s32[]{:S(2)}) async-start(), calls=%async_computation.4 | async-start | bytes 1310720 | tf_op jit(solution)/shard_map/all_gather | solution.py:176
  149.7 13.5 %collective-permute-start.7 = (bf16[1024,512]{1,0:T(8,128)(2,1)S(1)}, bf16[1024,512]{1,0:T(8,128)(2,1)S(1)}, u32[]{:S(2)}, u32[]{:S(2)}) collective-permute-start(bf16[1024,512]{1,0:T(8,128)(2,1)S(1)} %bitcast.55), channel_id=1, source_target_pairs={{0,1},{1,0},{2,3},{3,2},{4,5},{5,4},{6,7},{7,6},{8,9},{9,8},{10,11... | collective-permute-start | bytes 3145736 | tf_op jit(solution)/shard_map/ppermute | solution.py:41
  163.6 9.7 %collective-permute-start.8 = (f32[256,256]{1,0:T(8,128)S(1)}, f32[256,256]{1,0:T(8,128)S(1)}, u32[]{:S(2)}, u32[]{:S(2)}) collective-permute-start(f32[256,256]{1,0:T(8,128)S(1)} %fusion.1), channel_id=1, source_target_pairs={{0,256},{256,0},{1,257},{257,1},{2,258},{258,2},{3,259},{259,3},{4... | collective-permute-start | bytes 786440 | tf_op jit(solution)/shard_map/ppermute | solution.py:41
Sparse Core Ops, SparseCore 0:
  23.7 86.1 all-gather.4
  126.8 34.3 all-gather.6

commit v7 on v5

--- a/solution.py
+++ b/solution.py
@@ -7,24 +7,35 @@
 
 F32, BF16 = jnp.float32, jnp.bfloat16
 PLANE = ("yh", "x")
-
-
-def choosers(expert_ids, experts, capacity):
-    slot_order = jnp.arange(capacity, dtype=jnp.int32)[:, None]
-    rows = expert_ids.shape[0]
-    before = jnp.tril(jnp.ones((rows, rows), BF16))
-    out = []
+VMEM_GRANT = 56
+
+
+def pick_kernel(ids, grads, picked, chooser):
+    experts, capacity, rows = chooser.shape
+    first, second = ids[0:1, :], ids[1:2, :]
+    source = lax.broadcasted_iota(jnp.int32, (rows, rows), 0)
+    target = lax.broadcasted_iota(jnp.int32, (rows, rows), 1)
+    before = (source <= target).astype(F32).astype(BF16)
+    slot_order = lax.broadcasted_iota(jnp.int32, (capacity, rows), 0)
     for expert in range(experts):
-        routed = jnp.any(expert_ids == expert, axis=1)
-        count = jnp.dot(before, routed.astype(BF16)[:, None], preferred_element_type=F32)[:, 0]
-        slot_index = count.astype(jnp.int32) - 1
-        chosen = jnp.logical_and(routed[None, :], slot_index[None, :] == slot_order)
-        out.append(chosen.astype(BF16))
-    return out
-
-
-def pick(chooser, rows):
-    return jnp.dot(chooser, rows, preferred_element_type=F32).astype(BF16)
+        routed = jnp.logical_or(first == expert, second == expert)
+        flags = jnp.broadcast_to(routed.astype(F32), (16, rows)).astype(BF16)
+        slot_index = dot(flags, before)[0:1].astype(jnp.int32) - 1
+        hit = jnp.logical_and(slot_order == slot_index, routed)
+        chosen = hit.astype(F32).astype(BF16)
+        chooser[expert] = chosen
+        picked[expert] = dot(chosen, grads[expert]).astype(BF16)
+
+
+def pick_grads(ids, grads, capacity):
+    experts, rows, hidden = grads.shape
+    return pl.pallas_call(
+        pick_kernel,
+        out_shape=[
+            jax.ShapeDtypeStruct((experts, capacity, hidden), BF16),
+            jax.ShapeDtypeStruct((experts, capacity, rows), BF16),
+        ],
+    )(ids.T, grads)
 
 
 def swap(x, axis):
@@ -45,13 +56,13 @@
     def _():
         total[...] = jnp.zeros_like(total)
 
-    own = got[:, :deep, :cols].reshape(blocks * deep, cols)
-    other = got[:, :deep, cols:].reshape(blocks * deep, cols)
-    total[...] += dot(rows[...], own) + dot(rows_peer[...], other)
     grad = got[:, deep : deep + slots].reshape(blocks * slots, 2 * cols)
     grad_peer = got[:, deep + slots :].reshape(blocks * slots, 2 * cols)
     sums = dot(grad, basis[...]) + dot(grad_peer, basis_peer[...])
     part[...] = sums.astype(part.dtype).reshape(part.shape)
+    own = got[:, :deep, :cols].reshape(blocks * deep, cols)
+    other = got[:, :deep, cols:].reshape(blocks * deep, cols)
+    total[...] += dot(rows[...], own) + dot(rows_peer[...], other)
 
     @pl.when(step == pl.num_programs(0) - 1)
     def _():
@@ -84,7 +95,7 @@
             jax.ShapeDtypeStruct((count, cols), BF16),
         ],
         scratch_shapes=[pltpu.VMEM((count, cols), F32)],
-        compiler_params=pltpu.CompilerParams(vmem_limit_bytes=56 * 1024 * 1024),
+        compiler_params=pltpu.CompilerParams(vmem_limit_bytes=VMEM_GRANT * 1024 * 1024),
         cost_estimate=pl.CostEstimate(
             flops=4 * made * basis.shape[0] * keys + 4 * count * rows.shape[1] * cols,
             bytes_accessed=2 * (got.size + 2 * rows.size + 2 * basis.size + made * keys + count * cols),
@@ -110,8 +121,7 @@
         return lax.dynamic_index_in_dim(x, 1 - yl, 0, keepdims=False)
 
     act_other = swap(theirs(act_basis), "yl")
-    choose = choosers(expert_ids, 2, capacity)
-    picked_grad = jnp.stack([pick(choose[e], grads[e]) for e in range(2)])
+    picked_grad, choose = pick_grads(expert_ids, grads, capacity)
     straight = [(2 * y + c, 2 * c + y) for y in range(2) for c in range(2)]
     crossed = [(2 * y + c, 2 * (1 - c) + y) for y in range(2) for c in range(2)]
     grad_a = lax.ppermute(
@@ -132,24 +142,30 @@
     plane = lax.axis_index("yh") * lax.axis_size("x") + lax.axis_index("x")
     share = width // (2 * planes)
     piece = lax.dynamic_slice_in_dim(tokens, core * (width // 2) + plane * share, share, 1)
-    picked_act = jnp.stack([pick(choose[e], piece) for e in range(2)])
+    picked_act = jnp.stack([dot(choose[e], piece).astype(BF16) for e in range(2)])
     act_in, act_in_other = mine(picked_act), swap(theirs(picked_act), "yl")
     rows = jnp.concatenate(
         [jnp.where(yl == 0, act_in, act_in_other), jnp.where(yl == 0, act_in_other, act_in)], axis=0
     )
     rows = lax.all_gather(rows, "zh", axis=0, tiled=True)
+    basis_half = jnp.concatenate([mine(grad_basis), swap(theirs(grad_basis), "yl")], axis=1)
+    rows, basis_half = lax.optimization_barrier((rows, basis_half))
+    basis_peer = swap(basis_half, "c")
     copies = jnp.broadcast_to(rows[None], (planes,) + rows.shape)
     rows = lax.all_to_all(copies, PLANE, 0, 0, tiled=True)
     rows = rows.reshape(planes, nz // nl, 2, capacity, share).transpose(2, 1, 3, 0, 4)
     rows = rows.reshape(2 * nz // nl * capacity, planes * share)
     rows_peer = swap(rows, "c")
-    basis_half = jnp.concatenate([mine(grad_basis), swap(theirs(grad_basis), "yl")], axis=1)
-    basis_peer = swap(basis_half, "c")
 
     part, act_sq = project(gathered, rows, rows_peer, basis_half, basis_peer, nl)
     act_sq = lax.all_gather(act_sq, "zl", axis=0, tiled=False)
 
-    parts = lax.all_to_all(part.reshape(planes, nz * capacity // planes, -1), PLANE, 0, 0, tiled=True)
+    parts = lax.fori_loop(
+        0,
+        lax.optimization_barrier(jnp.int32(1)),
+        lambda trip, x: lax.all_to_all(x, PLANE, 0, 0, tiled=True),
+        part.reshape(planes, nz * capacity // planes, -1),
+    )
     grad_sq = jnp.square(jnp.sum(parts.astype(F32), axis=0)).astype(BF16)
     copies = jnp.broadcast_to(grad_sq[None], (planes,) + grad_sq.shape)
     grad_sq = lax.all_to_all(copies, PLANE, 0, 0, tiled=True).reshape(nz * capacity, -1)
@@ -172,7 +188,8 @@
     keys = grad_sq.shape[1]
     got = swap(block(keys // 2, keys), "yl")
     kept = block(0, keys // 2)
-    return jnp.stack([jnp.where(yl == 0, kept, got), jnp.where(yl == 0, got, kept)])
+    expert = lax.broadcasted_iota(jnp.int32, (2,) + kept.shape, 0)
+    return jnp.where(expert == yl, kept[None], got[None])
 
 
 def solution(mesh):

time: 181 us -> 178 us (0.983)
  blocking collectives: 78.5 us -> 75 us
  waiting for transfers between devices: 34.6 us -> 32 us
  Pallas kernels: 6.87 us -> 8.93 us
    all_gather x1, waiting for transfers between devices: 0.15 us -> 9.98 us  [per_device(): gathered = lax.all_gather(payload, ('zh', 'zl'), axis=0, tiled=False)]
    ppermute x7, waiting for transfers between devices: 18.1 us -> 10.2 us  [swap(): return lax.ppermute(x, axis, [(0, 1), (1, 0)])]
    all_to_all x1, blocking collectives: 20 us -> 15.7 us  [per_device(): lax.all_to_all(copies, PLANE, 0, 0, tiled=True).reshape(nz * capacity, -1)]
    all_to_all x1, waiting for transfers between devices: 12.8 us -> 10.7 us  [per_device(): lax.all_to_all(x, PLANE, 0, 0, tiled=True)]
    pallas_call x0 -> x1, Pallas kernels: none -> 2.04 us  [pick_grads(): pl.pallas_call(pick_kernel, out_shape=[jax.ShapeDtypeStruct((experts, cap...]
  transfers between devices with their start and end apart: 12 -> 12, of which waited for: 8 -> 6; matrix products, arithmetic and copies ran while one was open for 5% -> 6% of each run, Pallas kernels for 0% -> 1%
where the time goes in v7:
time: 178 us; the launch traced here: 175 us
  blocking collectives  75 us (42%)
  waiting for transfers between devices  32 us (18%)
  starting transfers between devices  31 us (17%)
  between operations  13.7 us (8%)
  Pallas kernels  8.93 us (5%)
  local copies, waits for them, and re-layouts  7.23 us (4%)
  other arithmetic  4.06 us (2%)
  matrix products  3.06 us (2%)
    all_to_all x1, blocking collectives, per_device(): rows = lax.all_to_all(copies, PLANE, 0, 0, tiled=True)  31.4 us
    all_gather x1, blocking collectives, per_device(): rows = lax.all_gather(rows, 'zh', axis=0, tiled=True)  27.9 us
    ppermute x7, starting transfers between devices, swap(): return lax.ppermute(x, axis, [(0, 1), (1, 0)])  18.6 us
    all_to_all x1, blocking collectives, per_device(): lax.all_to_all(copies, PLANE, 0, 0, tiled=True).reshape(nz * capacity, -1)  15.7 us
    all_to_all x1, waiting for transfers between devices, per_device(): lax.all_to_all(x, PLANE, 0, 0, tiled=True)  10.7 us
    ppermute x7, waiting for transfers between devices, swap(): return lax.ppermute(x, axis, [(0, 1), (1, 0)])  10.2 us
    all_gather x1, waiting for transfers between devices, per_device(): gathered = lax.all_gather(payload, ('zh', 'zl'), axis=0, tiled=False)  9.98 us
    all_to_all x1, starting transfers between devices, per_device(): lax.all_to_all(x, PLANE, 0, 0, tiled=True)  7.31 us
  transfers between devices with their start and end apart: 12, of which 6 were waited for; matrix products, arithmetic and copies ran while one was open for 6% of the time, Pallas kernels for 1%

profile of v7, /device:TPU:6, one launch (start us, length us, event | category | flops | bytes accessed | tf_op | source)
XLA Modules:
  0.0 175.0 jit_solution(11317277202107354149)
XLA Ops:
  7.5 3.5 %collective-permute-start = (bf16[128,256]{1,0:T(8,128)(2,1)S(1)}, bf16[128,256]{1,0:T(8,128)(2,1)S(1)}, u32[]{:S(2)}, u32[]{:S(2)}) collective-permute-start(bf16[128,256]{1,0:T(8,128)(2,1)S(1)} %dynamic-slice_bitcast_fusion.4), channel_id=1, source_target_pairs={{0,256},{256,0},{1,257},{257,1},{2,258},{258,2},{3,259},{259,3},{4... | collective-permute-start | bytes 196616 | tf_op jit(solution)/shard_map/ppermute | solution.py:42
  11.0 2.0 %shard_map.55 = (bf16[2,64,512]{2,1,0:T(8,128)(2,1)}, bf16[2,64,128]{2,1,0:T(8,128)(2,1)}) custom-call(s32[2,128]{1,0:T(2,128)} %bitcast.61, bf16[2,128,512]{2,1,0:T(8,128)(2,1)} %grads.1), custom_call_target="tpu_custom_call" | custom-call | tf_op jit(solution)/shard_map/pallas_call | solution.py:32
  14.6 4.3 %collective-permute-start.2 = (bf16[64,512]{1,0:T(8,128)(2,1)S(1)}, bf16[64,512]{1,0:T(8,128)(2,1)S(1)}, u32[]{:S(2)}, u32[]{:S(2)}) collective-permute-start(bf16[64,512]{1,0:T(8,128)(2,1)S(1)} %get-tuple-element.51), channel_id=1, source_target_pairs={{0,256},{1,0},{256,257},{257,1},{2,258},{3,2},{258,259},{259,3},{4... | collective-permute-start | bytes 196616 | tf_op jit(solution)/shard_map/ppermute | solution.py:130
  19.8 1.0 collective-permute-done.2
  23.4 4.3 %collective-permute-start.3 = (bf16[64,256]{1,0:T(8,128)(2,1)S(1)}, bf16[64,256]{1,0:T(8,128)(2,1)S(1)}, u32[]{:S(2)}, u32[]{:S(2)}) collective-permute-start(bf16[64,256]{1,0:T(8,128)(2,1)S(1)} %fusion.13), channel_id=1, source_target_pairs={{0,256},{256,0},{1,257},{257,1},{2,258},{258,2},{3,259},{259,3},{4... | collective-permute-start | bytes 98312 | tf_op jit(solution)/shard_map/ppermute | solution.py:42
  27.8 1.9 %collective-permute-start.4 = (bf16[512,256]{1,0:T(8,128)(2,1)S(1)}, bf16[512,256]{1,0:T(8,128)(2,1)S(1)}, u32[]{:S(2)}, u32[]{:S(2)}) collective-permute-start(bf16[512,256]{1,0:T(8,128)(2,1)S(1)} %get-tuple-element.45), channel_id=1, source_target_pairs={{0,256},{256,0},{1,257},{257,1},{2,258},{258,2},{3,259},{259,3},{4... | collective-permute-start | bytes 786440 | tf_op jit(solution)/shard_map/ppermute | solution.py:42
  29.8 27.9 %all_gather.17 = bf16[512,256]{1,0:T(8,128)(2,1)S(1)} all-gather(bf16[128,256]{1,0:T(8,128)(2,1)S(1)} %pad_maximum_fusion.2), channel_id=1, replica_groups=mesh['yl'=2,'zh'=4,'zl'=4,'yh'=2,'x'=4,'c'=2] {'zh'}, dimensions={0}, use_global_device_ids=true | all-gather | bytes 327680 | tf_op jit(solution)/shard_map/all_gather | solution.py:150
  57.9 31.4 %all_to_all.16 = bf16[8,512,256]{2,1,0:T(8,128)(2,1)S(1)} all-to-all(bf16[8,512,256]{2,1,0:T(8,128)(2,1)S(1)} %broadcast_in_dim.14), channel_id=1, replica_groups=mesh['yl'=2,'zh'=4,'zl'=4,'yh'=2,'x'=4,'c'=2] {'yh','x'}, dimensions={0} | all-to-all | bytes 4194304 | tf_op jit(solution)/shard_map/all_to_all | solution.py:155
  89.3 1.3 copy.6
  91.3 1.9 %collective-permute-start.5 = (bf16[512,2048]{1,0:T(8,128)(2,1)S(1)}, bf16[512,2048]{1,0:T(8,128)(2,1)}, u32[]{:S(2)}, u32[]{:S(2)}) collective-permute-start(bf16[512,2048]{1,0:T(8,128)(2,1)S(1)} %bitcast.50), channel_id=1, source_target_pairs={{0,1},{1,0},{2,3},{3,2},{4,5},{5,4},{6,7},{7,6},{8,9},{9,8},{10,11... | collective-permute-start | bytes 6291464 | tf_op jit(solution)/shard_map/ppermute | solution.py:42
  93.2 2.4 %collective-permute-start.6 = (bf16[512,512]{1,0:T(8,128)(2,1)S(1)}, bf16[512,512]{1,0:T(8,128)(2,1)S(1)}, u32[]{:S(2)}, u32[]{:S(2)}) collective-permute-start(bf16[512,512]{1,0:T(8,128)(2,1)S(1)} %pad_maximum_fusion.basis), channel_id=1, source_target_pairs={{0,1},{1,0},{2,3},{3,2},{4,5},{5,4},{6,7},{7,6},{8,9},{9,8},{10,11... | collective-permute-start | bytes 1572872 | tf_op jit(solution)/shard_map/ppermute | solution.py:42
  95.6 2.5 %collective-permute-done.6.basis_peer = bf16[512,512]{1,0:T(8,128)(2,1)S(1)} collective-permute-done((bf16[512,512]{1,0:T(8,128)(2,1)S(1)}, bf16[512,512]{1,0:T(8,128)(2,1)S(1)}, u32[]{:S(2)}, u32[]{:S(2)}) %collective-permute-start.6) | collective-permute-done | bytes 524320 | tf_op jit(solution)/shard_map/ppermute | solution.py:42
  98.9 10.0 %all-gather.5.cloned.1.call-done = bf16[4096,512]{1,0:T(8,128)(2,1)} async-done(((bf16[256,512]{1,0:T(8,128)(2,1)}), bf16[4096,512]{1,0:T(8,128)(2,1)}) %all-gather.5.cloned.1.call-update) | async-done | bytes 4194320 | tf_op jit(solution)/shard_map/all_gather | solution.py:140
  108.9 6.9 %shard_map.56 = (bf16[4,4,64,512]{3,2,1,0:T(8,128)(2,1)}, bf16[512,256]{1,0:T(8,128)(2,1)}) custom-call(bf16[16,256,512]{2,1,0:T(8,128)(2,1)} %bitcast.52, bf16[512,2048]{1,0:T(8,128)(2,1)} %bitcast.51, bf16[512,2048]{1,0:T(8,128)(2,1)} %collective-permute-done.5.rows_peer, bf16[512,512]{1,0:T(8,128)(2,1)} %copy-done.2, bf16[512,512]{1,0:T(8,128)(2,1)} %copy-done.3), custom_call_target="tpu_custom_call" | custom-call | flops 2147483648 | bytes 10747904 | tf_op jit(solution)/shard_map/pallas_call | solution.py:79
  115.8 19.1 %while.10 = (s32[]{:T(128)}, bf16[8,128,512]{2,1,0:T(8,128)(2,1)}, s32[]{:T(128)}, s32[]{:T(128)}) while((s32[]{:T(128)}, bf16[8,128,512]{2,1,0:T(8,128)(2,1)}, s32[]{:T(128)}, s32[]{:T(128)}) %tuple.26), condition=%wide.region_1.2_spmd, body=%wide.region_0.1_spmd.sunk | while | flops 2 | bytes 5242965 | solution.py:163
  115.8 7.3 %all-to-all-start = ((bf16[8,128,512]{2,1,0:T(8,128)(2,1)}), bf16[8,128,512]{2,1,0:T(8,128)(2,1)S(1)}, u32[]{:S(2)}, u32[]{:S(2)}) async-start(bf16[8,128,512]{2,1,0:T(8,128)(2,1)} %get-tuple-element.79), calls=%async_computation | async-start | bytes 2097152 | tf_op jit(solution)/shard_map/while/body/all_to_all | solution.py:166
  123.1 10.7 %all-to-all-done = bf16[8,128,512]{2,1,0:T(8,128)(2,1)S(1)} async-done(((bf16[8,128,512]{2,1,0:T(8,128)(2,1)}), bf16[8,128,512]{2,1,0:T(8,128)(2,1)S(1)}, u32[]{:S(2)}, u32[]{:S(2)}) %all-to-all-start) | async-done | bytes 1048608 | tf_op jit(solution)/shard_map/while/body/all_to_all | solution.py:166
  133.8 1.1 copy.13
  134.9 1.4 convert_reduce_fusion
  136.4 15.7 %all_to_all.17 = bf16[8,128,512]{2,1,0:T(8,128)(2,1)S(1)} all-to-all(bf16[8,128,512]{2,1,0:T(8,128)(2,1)S(1)} %broadcast_in_dim.15), channel_id=1, replica_groups=mesh['yl'=2,'zh'=4,'zl'=4,'yh'=2,'x'=4,'c'=2] {'yh','x'}, dimensions={0} | all-to-all | bytes 2097152 | tf_op jit(solution)/shard_map/all_to_all | solution.py:171
  152.1 1.9 %collective-permute-start.7 = (bf16[1024,512]{1,0:T(8,128)(2,1)S(1)}, bf16[1024,512]{1,0:T(8,128)(2,1)S(1)}, u32[]{:S(2)}, u32[]{:S(2)}) collective-permute-start(bf16[1024,512]{1,0:T(8,128)(2,1)S(1)} %bitcast.53), channel_id=1, source_target_pairs={{0,1},{1,0},{2,3},{3,2},{4,5},{5,4},{6,7},{7,6},{8,9},{9,8},{10,11... | collective-permute-start | bytes 3145736 | tf_op jit(solution)/shard_map/ppermute | solution.py:42
  154.1 1.3 constant_dynamic-slice_fusion
  157.0 2.7 %collective-permute-start.8 = (f32[256,256]{1,0:T(8,128)S(1)}, f32[256,256]{1,0:T(8,128)S(1)}, u32[]{:S(2)}, u32[]{:S(2)}) collective-permute-start(f32[256,256]{1,0:T(8,128)S(1)} %fusion.1), channel_id=1, source_target_pairs={{0,256},{256,0},{1,257},{257,1},{2,258},{258,2},{3,259},{259,3},{4... | collective-permute-start | bytes 786440 | tf_op jit(solution)/shard_map/ppermute | solution.py:42
  160.1 7.2 %collective-permute-done.8 = f32[256,256]{1,0:T(8,128)S(1)} collective-permute-done((f32[256,256]{1,0:T(8,128)S(1)}, f32[256,256]{1,0:T(8,128)S(1)}, u32[]{:S(2)}, u32[]{:S(2)}) %collective-permute-start.8) | collective-permute-done | bytes 262176 | tf_op jit(solution)/shard_map/ppermute | solution.py:42
  (44 shorter events, 10.7 us)
Async XLA Ops:
  6.5 15.1 %copy-start = (bf16[128,4096]{1,0:T(8,128)(2,1)S(1)}, bf16[128,4096]{1,0:T(8,128)(2,1)}, u32[]{:S(2)}) copy-start(bf16[128,4096]{1,0:T(8,128)(2,1)} %param.7) | copy-start | bytes 3145732
  6.5 21.2 %copy-start.4 = (bf16[2,512,256]{2,1,0:T(8,128)(2,1)S(1)}, bf16[2,512,256]{2,1,0:T(8,128)(2,1)}, u32[]{:S(2)}) copy-start(bf16[2,512,256]{2,1,0:T(8,128)(2,1)} %param.9) | copy-start | bytes 1572868
  6.5 102.3 %all-gather.5.cloned.1.call-start = ((), (), s32[]{:S(2)}) async-start(), calls=%async_computation.3 | async-start | bytes 4456448 | tf_op jit(solution)/shard_map/all_gather | solution.py:140
  7.5 11.4 %collective-permute-start = (bf16[128,256]{1,0:T(8,128)(2,1)S(1)}, bf16[128,256]{1,0:T(8,128)(2,1)S(1)}, u32[]{:S(2)}, u32[]{:S(2)}) collective-permute-start(bf16[128,256]{1,0:T(8,128)(2,1)S(1)} %dynamic-slice_bitcast_fusion.4), channel_id=1, source_target_pairs={{0,256},{256,0},{1,257},{257,1},{2,258},{258,2},{3,259},{259,3},{4... | collective-permute-start | bytes 196616 | tf_op jit(solution)/shard_map/ppermute | solution.py:42
  13.9 5.9 %collective-permute-start.1 = (bf16[64,512]{1,0:T(8,128)(2,1)S(1)}, bf16[64,512]{1,0:T(8,128)(2,1)S(1)}, u32[]{:S(2)}, u32[]{:S(2)}) collective-permute-start(bf16[64,512]{1,0:T(8,128)(2,1)S(1)} %get-tuple-element.50), channel_id=1, source_target_pairs={{0,0},{1,256},{256,1},{257,257},{2,2},{3,258},{258,3},{259,259},{4... | collective-permute-start | bytes 196616 | tf_op jit(solution)/shard_map/ppermute | solution.py:127
  14.6 6.2 %collective-permute-start.2 = (bf16[64,512]{1,0:T(8,128)(2,1)S(1)}, bf16[64,512]{1,0:T(8,128)(2,1)S(1)}, u32[]{:S(2)}, u32[]{:S(2)}) collective-permute-start(bf16[64,512]{1,0:T(8,128)(2,1)S(1)} %get-tuple-element.51), channel_id=1, source_target_pairs={{0,256},{1,0},{256,257},{257,1},{2,258},{3,2},{258,259},{259,3},{4... | collective-permute-start | bytes 196616 | tf_op jit(solution)/shard_map/ppermute | solution.py:130
  21.6 132.4 %all-gather.7.cloned.1.call-start = ((), (), s32[]{:S(2)}) async-start(), calls=%async_computation.4 | async-start | bytes 1310720 | tf_op jit(solution)/shard_map/all_gather | solution.py:161
  23.4 6.3 %collective-permute-start.3 = (bf16[64,256]{1,0:T(8,128)(2,1)S(1)}, bf16[64,256]{1,0:T(8,128)(2,1)S(1)}, u32[]{:S(2)}, u32[]{:S(2)}) collective-permute-start(bf16[64,256]{1,0:T(8,128)(2,1)S(1)} %fusion.13), channel_id=1, source_target_pairs={{0,256},{256,0},{1,257},{257,1},{2,258},{258,2},{3,259},{259,3},{4... | collective-permute-start | bytes 98312 | tf_op jit(solution)/shard_map/ppermute | solution.py:42
  27.8 29.9 %collective-permute-start.4 = (bf16[512,256]{1,0:T(8,128)(2,1)S(1)}, bf16[512,256]{1,0:T(8,128)(2,1)S(1)}, u32[]{:S(2)}, u32[]{:S(2)}) collective-permute-start(bf16[512,256]{1,0:T(8,128)(2,1)S(1)} %get-tuple-element.45), channel_id=1, source_target_pairs={{0,256},{256,0},{1,257},{257,1},{2,258},{258,2},{3,259},{259,3},{4... | collective-permute-start | bytes 786440 | tf_op jit(solution)/shard_map/ppermute | solution.py:42
  57.7 35.5 %copy-start.2 = (bf16[512,512]{1,0:T(8,128)(2,1)}, bf16[512,512]{1,0:T(8,128)(2,1)S(1)}, u32[]{:S(2)}) copy-start(bf16[512,512]{1,0:T(8,128)(2,1)S(1)} %pad_maximum_fusion.basis) | copy-start | bytes 1572868
  91.3 17.6 %copy-start.1 = (bf16[64,8,8,256]{3,1,2,0:T(8,128)(2,1)}, bf16[64,8,8,256]{3,1,2,0:T(8,128)(2,1)S(1)}, u32[]{:S(2)}) copy-start(bf16[64,8,8,256]{3,1,2,0:T(8,128)(2,1)S(1)} %copy.7) | copy-start | bytes 6291460
  91.3 7.6 %collective-permute-start.5 = (bf16[512,2048]{1,0:T(8,128)(2,1)S(1)}, bf16[512,2048]{1,0:T(8,128)(2,1)}, u32[]{:S(2)}, u32[]{:S(2)}) collective-permute-start(bf16[512,2048]{1,0:T(8,128)(2,1)S(1)} %bitcast.50), channel_id=1, source_target_pairs={{0,1},{1,0},{2,3},{3,2},{4,5},{5,4},{6,7},{7,6},{8,9},{9,8},{10,11... | collective-permute-start | bytes 6291464 | tf_op jit(solution)/shard_map/ppermute | solution.py:42
  93.2 4.9 %collective-permute-start.6 = (bf16[512,512]{1,0:T(8,128)(2,1)S(1)}, bf16[512,512]{1,0:T(8,128)(2,1)S(1)}, u32[]{:S(2)}, u32[]{:S(2)}) collective-permute-start(bf16[512,512]{1,0:T(8,128)(2,1)S(1)} %pad_maximum_fusion.basis), channel_id=1, source_target_pairs={{0,1},{1,0},{2,3},{3,2},{4,5},{5,4},{6,7},{7,6},{8,9},{9,8},{10,11... | collective-permute-start | bytes 1572872 | tf_op jit(solution)/shard_map/ppermute | solution.py:42
  98.1 0.8 copy-start.3
  115.8 18.0 %all-to-all-start = ((bf16[8,128,512]{2,1,0:T(8,128)(2,1)}), bf16[8,128,512]{2,1,0:T(8,128)(2,1)S(1)}, u32[]{:S(2)}, u32[]{:S(2)}) async-start(bf16[8,128,512]{2,1,0:T(8,128)(2,1)} %get-tuple-element.79), calls=%async_computation | async-start | bytes 2097152 | tf_op jit(solution)/shard_map/while/body/all_to_all | solution.py:166
  152.1 4.5 %collective-permute-start.7 = (bf16[1024,512]{1,0:T(8,128)(2,1)S(1)}, bf16[1024,512]{1,0:T(8,128)(2,1)S(1)}, u32[]{:S(2)}, u32[]{:S(2)}) collective-permute-start(bf16[1024,512]{1,0:T(8,128)(2,1)S(1)} %bitcast.53), channel_id=1, source_target_pairs={{0,1},{1,0},{2,3},{3,2},{4,5},{5,4},{6,7},{7,6},{8,9},{9,8},{10,11... | collective-permute-start | bytes 3145736 | tf_op jit(solution)/shard_map/ppermute | solution.py:42
  157.0 10.2 %collective-permute-start.8 = (f32[256,256]{1,0:T(8,128)S(1)}, f32[256,256]{1,0:T(8,128)S(1)}, u32[]{:S(2)}, u32[]{:S(2)}) collective-permute-start(f32[256,256]{1,0:T(8,128)S(1)} %fusion.1), channel_id=1, source_target_pairs={{0,256},{256,0},{1,257},{257,1},{2,258},{258,2},{3,259},{259,3},{4... | collective-permute-start | bytes 786440 | tf_op jit(solution)/shard_map/ppermute | solution.py:42
Sparse Core Ops, SparseCore 0:
  21.7 87.0 all-gather.4
  115.9 34.4 all-gather.6

commit v8 on v7

--- a/solution.py
+++ b/solution.py
@@ -7,7 +7,7 @@
 
 F32, BF16 = jnp.float32, jnp.bfloat16
 PLANE = ("yh", "x")
-VMEM_GRANT = 56
+VMEM_GRANT = 24
 
 
 def pick_kernel(ids, grads, picked, chooser):
@@ -46,59 +46,44 @@
     return jnp.dot(a, b, preferred_element_type=F32)
 
 
-def project_kernel(got, rows, rows_peer, basis, basis_peer, part, act, total):
-    step = pl.program_id(0)
-    blocks, height, _ = got.shape
+def project_kernel(got, rows, rows_peer, basis, basis_peer, part, act):
+    blocks, steps = part.shape[:2]
+    height = got.shape[1]
     cols = act.shape[1]
     deep, slots = height // 2, height // 4
-
-    @pl.when(step == 0)
-    def _():
-        total[...] = jnp.zeros_like(total)
-
-    grad = got[:, deep : deep + slots].reshape(blocks * slots, 2 * cols)
-    grad_peer = got[:, deep + slots :].reshape(blocks * slots, 2 * cols)
-    sums = dot(grad, basis[...]) + dot(grad_peer, basis_peer[...])
-    part[...] = sums.astype(part.dtype).reshape(part.shape)
-    own = got[:, :deep, :cols].reshape(blocks * deep, cols)
-    other = got[:, :deep, cols:].reshape(blocks * deep, cols)
-    total[...] += dot(rows[...], own) + dot(rows_peer[...], other)
-
-    @pl.when(step == pl.num_programs(0) - 1)
-    def _():
-        rounded = total[...].astype(act.dtype).astype(F32)
-        act[...] = (rounded * rounded).astype(act.dtype)
+    total = None
+    for step in range(steps):
+        span = slice(step * blocks, (step + 1) * blocks)
+        deeps = slice(step * blocks * deep, (step + 1) * blocks * deep)
+        grad = got[span, deep : deep + slots].reshape(blocks * slots, 2 * cols)
+        grad_peer = got[span, deep + slots :].reshape(blocks * slots, 2 * cols)
+        sums = dot(grad, basis[...]) + dot(grad_peer, basis_peer[...])
+        part[:, step] = sums.astype(part.dtype).reshape(blocks, slots, 2 * cols)
+        own = got[span, :deep, :cols].reshape(blocks * deep, cols)
+        other = got[span, :deep, cols:].reshape(blocks * deep, cols)
+        more = dot(rows[:, deeps], own) + dot(rows_peer[:, deeps], other)
+        total = more if total is None else total + more
+    rounded = total.astype(act.dtype).astype(F32)
+    act[...] = (rounded * rounded).astype(act.dtype)
 
 
 def project(got, rows, rows_peer, basis, basis_peer, blocks):
     nz, height, lanes = got.shape
     count, keys, cols = rows.shape[0], basis.shape[1], lanes // 2
-    row_block = pl.BlockSpec((count, blocks * height // 2), lambda i: (0, i))
-    whole = pl.BlockSpec(basis.shape, lambda i: (0, 0))
-    made = nz * height // 4
+    steps, made = nz // blocks, height // 4
+    near = pl.BlockSpec(memory_space=pltpu.VMEM)
     return pl.pallas_call(
         project_kernel,
-        grid=(nz // blocks,),
-        in_specs=[
-            pl.BlockSpec((blocks, height, lanes), lambda i: (i, 0, 0)),
-            row_block,
-            row_block,
-            whole,
-            whole,
-        ],
-        out_specs=[
-            pl.BlockSpec((blocks, 1, height // 4, keys), lambda i: (0, i, 0, 0)),
-            pl.BlockSpec((count, cols), lambda i: (0, 0)),
-        ],
+        in_specs=[near] * 5,
+        out_specs=[near] * 2,
         out_shape=[
-            jax.ShapeDtypeStruct((blocks, nz // blocks, height // 4, keys), BF16),
+            jax.ShapeDtypeStruct((blocks, steps, made, keys), BF16),
             jax.ShapeDtypeStruct((count, cols), BF16),
         ],
-        scratch_shapes=[pltpu.VMEM((count, cols), F32)],
         compiler_params=pltpu.CompilerParams(vmem_limit_bytes=VMEM_GRANT * 1024 * 1024),
         cost_estimate=pl.CostEstimate(
-            flops=4 * made * basis.shape[0] * keys + 4 * count * rows.shape[1] * cols,
-            bytes_accessed=2 * (got.size + 2 * rows.size + 2 * basis.size + made * keys + count * cols),
+            flops=4 * nz * made * basis.shape[0] * keys + 4 * count * rows.shape[1] * cols,
+            bytes_accessed=2 * (got.size + 2 * rows.size + 2 * basis.size + nz * made * keys + count * cols),
             transcendentals=0,
         ),
     )(got, rows, rows_peer, basis, basis_peer)
@@ -153,17 +138,19 @@
     basis_peer = swap(basis_half, "c")
     copies = jnp.broadcast_to(rows[None], (planes,) + rows.shape)
     rows = lax.all_to_all(copies, PLANE, 0, 0, tiled=True)
-    rows = rows.reshape(planes, nz // nl, 2, capacity, share).transpose(2, 1, 3, 0, 4)
-    rows = rows.reshape(2 * nz // nl * capacity, planes * share)
-    rows_peer = swap(rows, "c")
+    def lay(x):
+        x = x.reshape(planes, nz // nl, 2, capacity, share).transpose(2, 1, 3, 0, 4)
+        return x.reshape(2 * nz // nl * capacity, planes * share)
+
+    rows, rows_peer = lay(rows), lay(swap(rows, "c"))
 
     part, act_sq = project(gathered, rows, rows_peer, basis_half, basis_peer, nl)
     act_sq = lax.all_gather(act_sq, "zl", axis=0, tiled=False)
 
-    parts = lax.fori_loop(
-        0,
-        lax.optimization_barrier(jnp.int32(1)),
-        lambda trip, x: lax.all_to_all(x, PLANE, 0, 0, tiled=True),
+    parts = lax.cond(
+        lax.optimization_barrier(jnp.int32(1)) > 0,
+        lambda x: lax.all_to_all(x, PLANE, 0, 0, tiled=True),
+        lambda x: x,
         part.reshape(planes, nz * capacity // planes, -1),
     )
     grad_sq = jnp.square(jnp.sum(parts.astype(F32), axis=0)).astype(BF16)

time: 178 us -> 180 us (1.011)
  blocking collectives: 75 us -> 90.9 us
  waiting for transfers between devices: 32 us -> 19.6 us
  local copies, waits for them, and re-layouts: 7.23 us -> 16.7 us
  starting transfers between devices: 31 us -> 21.6 us
  Pallas kernels: 8.93 us -> 6.77 us
    all_to_all x0 -> x1, blocking collectives: none -> 17.7 us  [per_device(): lax.all_to_all(x, PLANE, 0, 0, tiled=True)]
    all_to_all x1 -> x0, waiting for transfers between devices: 10.7 us -> none  [per_device(): lax.all_to_all(x, PLANE, 0, 0, tiled=True)]
    all_to_all x1 -> x0, starting transfers between devices: 7.31 us -> none  [per_device(): lax.all_to_all(x, PLANE, 0, 0, tiled=True)]
    unnamed x11 -> x10, local copies, waits for them, and re-layouts: 1.49 us -> 6.51 us
    transpose x1 -> x2, local copies, waits for them, and re-layouts: 1.29 us -> 5.73 us  [lay(): x = x.reshape(planes, nz // nl, 2, capacity, share).transpose(2, 1, 3, 0, 4)]
    all_gather x1, waiting for transfers between devices: 9.98 us -> 7.09 us  [per_device(): gathered = lax.all_gather(payload, ('zh', 'zl'), axis=0, tiled=False)]
    ppermute x7, starting transfers between devices: 18.6 us -> 16.2 us  [swap(): return lax.ppermute(x, axis, [(0, 1), (1, 0)])]
    pallas_call x1, Pallas kernels: 6.89 us -> 4.61 us  [project(): pl.pallas_call(project_kernel, in_specs=[near] * 5, out_specs=[near] * 2,...]
  transfers between devices with their start and end apart: 12 -> 11, of which waited for: 6 -> 4; matrix products, arithmetic and copies ran while one was open for 6% -> 9% of each run, Pallas kernels for 1% -> 0%
where the time goes in v8:
time: 180 us; the launch traced here: 177 us
  blocking collectives  90.9 us (50%)
  starting transfers between devices  21.6 us (12%)
  waiting for transfers between devices  19.6 us (11%)
  local copies, waits for them, and re-layouts  16.7 us (9%)
  between operations  13.7 us (8%)
  Pallas kernels  6.77 us (4%)
  other arithmetic  4.82 us (3%)
  matrix products  3.06 us (2%)
    all_to_all x1, blocking collectives, per_device(): rows = lax.all_to_all(copies, PLANE, 0, 0, tiled=True)  29.5 us
    all_gather x1, blocking collectives, per_device(): rows = lax.all_gather(rows, 'zh', axis=0, tiled=True)  28.2 us
    all_to_all x1, blocking collectives, per_device(): lax.all_to_all(x, PLANE, 0, 0, tiled=True)  17.7 us
    ppermute x7, starting transfers between devices, swap(): return lax.ppermute(x, axis, [(0, 1), (1, 0)])  16.2 us
    all_to_all x1, blocking collectives, per_device(): lax.all_to_all(copies, PLANE, 0, 0, tiled=True).reshape(nz * capacity, -1)  15.5 us
    ppermute x7, waiting for transfers between devices, swap(): return lax.ppermute(x, axis, [(0, 1), (1, 0)])  12.5 us
    all_gather x1, waiting for transfers between devices, per_device(): gathered = lax.all_gather(payload, ('zh', 'zl'), axis=0, tiled=False)  7.09 us
    unnamed x10, local copies, waits for them, and re-layouts  6.51 us
  transfers between devices with their start and end apart: 11, of which 4 were waited for; matrix products, arithmetic and copies ran while one was open for 9% of the time, Pallas kernels for 0%

profile of v8, /device:TPU:6, one launch (start us, length us, event | category | flops | bytes accessed | tf_op | source)
XLA Modules:
  0.0 177.2 jit_solution(18304094892630906324)
XLA Ops:
  6.5 2.2 %shard_map.55 = (bf16[2,64,512]{2,1,0:T(8,128)(2,1)}, bf16[2,64,128]{2,1,0:T(8,128)(2,1)}) custom-call(s32[2,128]{1,0:T(2,128)} %bitcast.69, bf16[2,128,512]{2,1,0:T(8,128)(2,1)} %grads.1), custom_call_target="tpu_custom_call" | custom-call | tf_op jit(solution)/shard_map/pallas_call | solution.py:32
  10.3 4.7 %collective-permute-start.2 = (bf16[64,512]{1,0:T(8,128)(2,1)S(1)}, bf16[64,512]{1,0:T(8,128)(2,1)S(1)}, u32[]{:S(2)}, u32[]{:S(2)}) collective-permute-start(bf16[64,512]{1,0:T(8,128)(2,1)S(1)} %get-tuple-element.31), channel_id=1, source_target_pairs={{0,256},{1,0},{256,257},{257,1},{2,258},{3,2},{258,259},{259,3},{4... | collective-permute-start | bytes 196616 | tf_op jit(solution)/shard_map/ppermute | solution.py:115
  15.9 1.9 %collective-permute-start = (bf16[128,256]{1,0:T(8,128)(2,1)S(1)}, bf16[128,256]{1,0:T(8,128)(2,1)S(1)}, u32[]{:S(2)}, u32[]{:S(2)}) collective-permute-start(bf16[128,256]{1,0:T(8,128)(2,1)S(1)} %dynamic-slice_bitcast_fusion.4), channel_id=1, source_target_pairs={{0,256},{256,0},{1,257},{257,1},{2,258},{258,2},{3,259},{259,3},{4... | collective-permute-start | bytes 196616 | tf_op jit(solution)/shard_map/ppermute | solution.py:42
  17.8 4.2 %collective-permute-done = bf16[128,256]{1,0:T(8,128)(2,1)S(1)} collective-permute-done((bf16[128,256]{1,0:T(8,128)(2,1)S(1)}, bf16[128,256]{1,0:T(8,128)(2,1)S(1)}, u32[]{:S(2)}, u32[]{:S(2)}) %collective-permute-start) | collective-permute-done | bytes 65568 | tf_op jit(solution)/shard_map/ppermute | solution.py:42
  25.4 1.9 %collective-permute-start.3 = (bf16[64,256]{1,0:T(8,128)(2,1)S(1)}, bf16[64,256]{1,0:T(8,128)(2,1)S(1)}, u32[]{:S(2)}, u32[]{:S(2)}) collective-permute-start(bf16[64,256]{1,0:T(8,128)(2,1)S(1)} %fusion.13), channel_id=1, source_target_pairs={{0,256},{256,0},{1,257},{257,1},{2,258},{258,2},{3,259},{259,3},{4... | collective-permute-start | bytes 98312 | tf_op jit(solution)/shard_map/ppermute | solution.py:42
  27.4 3.9 %collective-permute-start.4 = (bf16[512,256]{1,0:T(8,128)(2,1)S(1)}, bf16[512,256]{1,0:T(8,128)(2,1)S(1)}, u32[]{:S(2)}, u32[]{:S(2)}) collective-permute-start(bf16[512,256]{1,0:T(8,128)(2,1)S(1)} %get-tuple-element.25), channel_id=1, source_target_pairs={{0,256},{256,0},{1,257},{257,1},{2,258},{258,2},{3,259},{259,3},{4... | collective-permute-start | bytes 786440 | tf_op jit(solution)/shard_map/ppermute | solution.py:42
  31.4 28.2 %all_gather.17 = bf16[512,256]{1,0:T(8,128)(2,1)S(1)} all-gather(bf16[128,256]{1,0:T(8,128)(2,1)S(1)} %pad_maximum_fusion.2), channel_id=1, replica_groups=mesh['yl'=2,'zh'=4,'zl'=4,'yh'=2,'x'=4,'c'=2] {'zh'}, dimensions={0}, use_global_device_ids=true | all-gather | bytes 327680 | tf_op jit(solution)/shard_map/all_gather | solution.py:135
  60.6 29.5 %all_to_all.15 = bf16[8,512,256]{2,1,0:T(8,128)(2,1)} all-to-all(bf16[8,512,256]{2,1,0:T(8,128)(2,1)S(1)} %broadcast_in_dim.14), channel_id=1, replica_groups=mesh['yl'=2,'zh'=4,'zl'=4,'yh'=2,'x'=4,'c'=2] {'yh','x'}, dimensions={0} | all-to-all | bytes 4194304 | tf_op jit(solution)/shard_map/all_to_all | solution.py:140
  90.1 1.9 %collective-permute-start.5 = (bf16[8,512,256]{2,1,0:T(8,128)(2,1)}, bf16[8,512,256]{2,1,0:T(8,128)(2,1)}, u32[]{:S(2)}, u32[]{:S(2)}) collective-permute-start(bf16[8,512,256]{2,1,0:T(8,128)(2,1)} %all_to_all.15), channel_id=1, source_target_pairs={{0,1},{1,0},{2,3},{3,2},{4,5},{5,4},{6,7},{7,6},{8,9},{9,8},{10,11... | collective-permute-start | bytes 6291464 | tf_op jit(solution)/shard_map/ppermute | solution.py:42
  92.0 2.4 %collective-permute-start.6 = (bf16[512,512]{1,0:T(8,128)(2,1)}, bf16[512,512]{1,0:T(8,128)(2,1)}, u32[]{:S(2)}, u32[]{:S(2)}) collective-permute-start(bf16[512,512]{1,0:T(8,128)(2,1)} %pad_maximum_fusion.basis), channel_id=1, source_target_pairs={{0,1},{1,0},{2,3},{3,2},{4,5},{5,4},{6,7},{7,6},{8,9},{9,8},{10,11... | collective-permute-start | bytes 1572872 | tf_op jit(solution)/shard_map/ppermute | solution.py:42
  94.4 2.9 %copy.6 = bf16[2,4,64,8,256]{4,3,2,1,0:T(8,128)(2,1)S(1)} copy(bf16[2,4,64,8,256]{4,2,0,1,3:T(8,128)(2,1)} %bitcast.15) | data formatting | bytes 4194304 | tf_op jit(solution)/shard_map/transpose | solution.py:142
  98.0 2.9 %copy.7 = bf16[2,4,64,8,256]{4,3,2,1,0:T(8,128)(2,1)S(1)} copy(bf16[2,4,64,8,256]{4,2,0,1,3:T(8,128)(2,1)} %bitcast.17) | data formatting | bytes 4194304 | tf_op jit(solution)/shard_map/transpose | solution.py:142
  100.8 2.0 %copy.9 = bf16[64,8,8,256]{3,1,2,0:T(8,128)(2,1)} copy(bf16[64,8,8,256]{3,2,1,0:T(8,128)(2,1)S(1)} %bitcast.57) | data formatting | bytes 4194304
  102.9 7.1 %all-gather.5.cloned.1.call-done = bf16[4096,512]{1,0:T(8,128)(2,1)} async-done(((bf16[256,512]{1,0:T(8,128)(2,1)}), bf16[4096,512]{1,0:T(8,128)(2,1)}) %all-gather.5.cloned.1.call-update) | async-done | bytes 4194320 | tf_op jit(solution)/shard_map/all_gather | solution.py:125
  110.0 1.6 copy-done.1
  111.6 2.2 %copy-done.2 = bf16[4096,512]{1,0:T(8,128)(2,1)S(1)} copy-done((bf16[4096,512]{1,0:T(8,128)(2,1)S(1)}, bf16[4096,512]{1,0:T(8,128)(2,1)}, u32[]{:S(2)}) %copy-start.2) | copy-done | bytes 4194328
  113.8 4.6 %shard_map.56 = (bf16[4,4,64,512]{3,2,1,0:T(8,128)(2,1)}, bf16[512,256]{1,0:T(8,128)(2,1)}) custom-call(bf16[16,256,512]{2,1,0:T(8,128)(2,1)S(1)} %bitcast.56, bf16[512,2048]{1,0:T(8,128)(2,1)S(1)} %bitcast.54, bf16[512,2048]{1,0:T(8,128)(2,1)S(1)} %bitcast.55, bf16[512,512]{1,0:T(8,128)(2,1)} %pad_maximum_fusion.basis, ...), custom_call_target="tpu_custom_call" | custom-call | flops 2147483648 | bytes 10747904 | tf_op jit(solution)/shard_map/pallas_call | solution.py:75
  118.4 18.9 %conditional.1 = (bf16[8,128,512]{2,1,0:T(8,128)(2,1)}) conditional(s32[]{:T(128)} %convert_element_type.19, bf16[8,128,512]{2,1,0:T(8,128)(2,1)} %bitcast.59, bf16[8,128,512]{2,1,0:T(8,128)(2,1)} %bitcast.60), branch_computations={%region_0.1_spmd, %region_1.2_spmd} | conditional | bytes 6291492 | solution.py:150
  119.6 17.7 %all_to_all.14 = bf16[8,128,512]{2,1,0:T(8,128)(2,1)} all-to-all(bf16[8,128,512]{2,1,0:T(8,128)(2,1)S(1)} %copy-done.3), channel_id=1, replica_groups=mesh['yl'=2,'zh'=4,'zl'=4,'yh'=2,'x'=4,'c'=2] {'yh','x'}, dimensions={0} | all-to-all | bytes 2097152 | tf_op jit(solution)/shard_map/cond/branch_1_fun/all_to_all | solution.py:152
  137.3 1.4 convert_reduce_fusion
  138.8 15.5 %all_to_all.16 = bf16[8,128,512]{2,1,0:T(8,128)(2,1)S(1)} all-to-all(bf16[8,128,512]{2,1,0:T(8,128)(2,1)S(1)} %broadcast_in_dim.15), channel_id=1, replica_groups=mesh['yl'=2,'zh'=4,'zl'=4,'yh'=2,'x'=4,'c'=2] {'yh','x'}, dimensions={0} | all-to-all | bytes 2097152 | tf_op jit(solution)/shard_map/all_to_all | solution.py:158
  154.3 1.9 %collective-permute-start.7 = (bf16[1024,512]{1,0:T(8,128)(2,1)S(1)}, bf16[1024,512]{1,0:T(8,128)(2,1)S(1)}, u32[]{:S(2)}, u32[]{:S(2)}) collective-permute-start(bf16[1024,512]{1,0:T(8,128)(2,1)S(1)} %bitcast.61), channel_id=1, source_target_pairs={{0,1},{1,0},{2,3},{3,2},{4,5},{5,4},{6,7},{7,6},{8,9},{9,8},{10,11... | collective-permute-start | bytes 3145736 | tf_op jit(solution)/shard_map/ppermute | solution.py:42
  159.2 2.2 %collective-permute-start.8 = (f32[256,256]{1,0:T(8,128)S(1)}, f32[256,256]{1,0:T(8,128)S(1)}, u32[]{:S(2)}, u32[]{:S(2)}) collective-permute-start(f32[256,256]{1,0:T(8,128)S(1)} %fusion.1), channel_id=1, source_target_pairs={{0,256},{256,0},{1,257},{257,1},{2,258},{258,2},{3,259},{259,3},{4... | collective-permute-start | bytes 786440 | tf_op jit(solution)/shard_map/ppermute | solution.py:42
  161.8 7.7 %collective-permute-done.8 = f32[256,256]{1,0:T(8,128)S(1)} collective-permute-done((f32[256,256]{1,0:T(8,128)S(1)}, f32[256,256]{1,0:T(8,128)S(1)}, u32[]{:S(2)}, u32[]{:S(2)}) %collective-permute-start.8) | collective-permute-done | bytes 262176 | tf_op jit(solution)/shard_map/ppermute | solution.py:42
  (44 shorter events, 13.0 us)
Async XLA Ops:
  6.5 17.1 %copy-start = (bf16[128,4096]{1,0:T(8,128)(2,1)S(1)}, bf16[128,4096]{1,0:T(8,128)(2,1)}, u32[]{:S(2)}) copy-start(bf16[128,4096]{1,0:T(8,128)(2,1)} %param.7) | copy-start | bytes 3145732
  6.5 20.8 %copy-start.4 = (bf16[2,512,256]{2,1,0:T(8,128)(2,1)S(1)}, bf16[2,512,256]{2,1,0:T(8,128)(2,1)}, u32[]{:S(2)}) copy-start(bf16[2,512,256]{2,1,0:T(8,128)(2,1)} %param.9) | copy-start | bytes 1572868
  6.5 103.4 %all-gather.5.cloned.1.call-start = ((), (), s32[]{:S(2)}) async-start(), calls=%async_computation.3 | async-start | bytes 4456448 | tf_op jit(solution)/shard_map/all_gather | solution.py:125
  9.6 8.2 %collective-permute-start.1 = (bf16[64,512]{1,0:T(8,128)(2,1)S(1)}, bf16[64,512]{1,0:T(8,128)(2,1)S(1)}, u32[]{:S(2)}, u32[]{:S(2)}) collective-permute-start(bf16[64,512]{1,0:T(8,128)(2,1)S(1)} %get-tuple-element.30), channel_id=1, source_target_pairs={{0,0},{1,256},{256,1},{257,257},{2,2},{3,258},{258,3},{259,259},{4... | collective-permute-start | bytes 196616 | tf_op jit(solution)/shard_map/ppermute | solution.py:112
  10.3 7.5 %collective-permute-start.2 = (bf16[64,512]{1,0:T(8,128)(2,1)S(1)}, bf16[64,512]{1,0:T(8,128)(2,1)S(1)}, u32[]{:S(2)}, u32[]{:S(2)}) collective-permute-start(bf16[64,512]{1,0:T(8,128)(2,1)S(1)} %get-tuple-element.31), channel_id=1, source_target_pairs={{0,256},{1,0},{256,257},{257,1},{2,258},{3,2},{258,259},{259,3},{4... | collective-permute-start | bytes 196616 | tf_op jit(solution)/shard_map/ppermute | solution.py:115
  15.9 6.1 %collective-permute-start = (bf16[128,256]{1,0:T(8,128)(2,1)S(1)}, bf16[128,256]{1,0:T(8,128)(2,1)S(1)}, u32[]{:S(2)}, u32[]{:S(2)}) collective-permute-start(bf16[128,256]{1,0:T(8,128)(2,1)S(1)} %dynamic-slice_bitcast_fusion.4), channel_id=1, source_target_pairs={{0,256},{256,0},{1,257},{257,1},{2,258},{258,2},{3,259},{259,3},{4... | collective-permute-start | bytes 196616 | tf_op jit(solution)/shard_map/ppermute | solution.py:42
  23.6 132.7 %all-gather.7.cloned.1.call-start = ((), (), s32[]{:S(2)}) async-start(), calls=%async_computation.4 | async-start | bytes 1310720 | tf_op jit(solution)/shard_map/all_gather | solution.py:148
  25.4 5.9 %collective-permute-start.3 = (bf16[64,256]{1,0:T(8,128)(2,1)S(1)}, bf16[64,256]{1,0:T(8,128)(2,1)S(1)}, u32[]{:S(2)}, u32[]{:S(2)}) collective-permute-start(bf16[64,256]{1,0:T(8,128)(2,1)S(1)} %fusion.13), channel_id=1, source_target_pairs={{0,256},{256,0},{1,257},{257,1},{2,258},{258,2},{3,259},{259,3},{4... | collective-permute-start | bytes 98312 | tf_op jit(solution)/shard_map/ppermute | solution.py:42
  27.4 32.2 %collective-permute-start.4 = (bf16[512,256]{1,0:T(8,128)(2,1)S(1)}, bf16[512,256]{1,0:T(8,128)(2,1)S(1)}, u32[]{:S(2)}, u32[]{:S(2)}) collective-permute-start(bf16[512,256]{1,0:T(8,128)(2,1)S(1)} %get-tuple-element.25), channel_id=1, source_target_pairs={{0,256},{256,0},{1,257},{257,1},{2,258},{258,2},{3,259},{259,3},{4... | collective-permute-start | bytes 786440 | tf_op jit(solution)/shard_map/ppermute | solution.py:42
  90.1 7.9 %collective-permute-start.5 = (bf16[8,512,256]{2,1,0:T(8,128)(2,1)}, bf16[8,512,256]{2,1,0:T(8,128)(2,1)}, u32[]{:S(2)}, u32[]{:S(2)}) collective-permute-start(bf16[8,512,256]{2,1,0:T(8,128)(2,1)} %all_to_all.15), channel_id=1, source_target_pairs={{0,1},{1,0},{2,3},{3,2},{4,5},{5,4},{6,7},{7,6},{8,9},{9,8},{10,11... | collective-permute-start | bytes 6291464 | tf_op jit(solution)/shard_map/ppermute | solution.py:42
  92.0 10.9 %collective-permute-start.6 = (bf16[512,512]{1,0:T(8,128)(2,1)}, bf16[512,512]{1,0:T(8,128)(2,1)}, u32[]{:S(2)}, u32[]{:S(2)}) collective-permute-start(bf16[512,512]{1,0:T(8,128)(2,1)} %pad_maximum_fusion.basis), channel_id=1, source_target_pairs={{0,1},{1,0},{2,3},{3,2},{4,5},{5,4},{6,7},{7,6},{8,9},{9,8},{10,11... | collective-permute-start | bytes 1572872 | tf_op jit(solution)/shard_map/ppermute | solution.py:42
  110.0 1.6 copy-start.1
  111.6 2.2 %copy-start.2 = (bf16[4096,512]{1,0:T(8,128)(2,1)S(1)}, bf16[4096,512]{1,0:T(8,128)(2,1)}, u32[]{:S(2)}) copy-start(bf16[4096,512]{1,0:T(8,128)(2,1)} %all-gather.5.cloned.1.call-done) | copy-start | bytes 12582916
  118.4 1.2 copy-start.3
  154.3 4.5 %collective-permute-start.7 = (bf16[1024,512]{1,0:T(8,128)(2,1)S(1)}, bf16[1024,512]{1,0:T(8,128)(2,1)S(1)}, u32[]{:S(2)}, u32[]{:S(2)}) collective-permute-start(bf16[1024,512]{1,0:T(8,128)(2,1)S(1)} %bitcast.61), channel_id=1, source_target_pairs={{0,1},{1,0},{2,3},{3,2},{4,5},{5,4},{6,7},{7,6},{8,9},{9,8},{10,11... | collective-permute-start | bytes 3145736 | tf_op jit(solution)/shard_map/ppermute | solution.py:42
  159.2 10.2 %collective-permute-start.8 = (f32[256,256]{1,0:T(8,128)S(1)}, f32[256,256]{1,0:T(8,128)S(1)}, u32[]{:S(2)}, u32[]{:S(2)}) collective-permute-start(f32[256,256]{1,0:T(8,128)S(1)} %fusion.1), channel_id=1, source_target_pairs={{0,256},{256,0},{1,257},{257,1},{2,258},{258,2},{3,259},{259,3},{4... | collective-permute-start | bytes 786440 | tf_op jit(solution)/shard_map/ppermute | solution.py:42
Sparse Core Ops, SparseCore 0:
  23.7 86.2 all-gather.4
  118.5 34.3 all-gather.6

commit v9 on v7

--- a/solution.py
+++ b/solution.py
@@ -59,7 +59,9 @@
     grad = got[:, deep : deep + slots].reshape(blocks * slots, 2 * cols)
     grad_peer = got[:, deep + slots :].reshape(blocks * slots, 2 * cols)
     sums = dot(grad, basis[...]) + dot(grad_peer, basis_peer[...])
-    part[...] = sums.astype(part.dtype).reshape(part.shape)
+    sums = sums.astype(part.dtype).reshape((part.shape[1], part.shape[0]) + part.shape[2:])
+    for group in range(part.shape[1]):
+        part[:, group] = sums[group]
     own = got[:, :deep, :cols].reshape(blocks * deep, cols)
     other = got[:, :deep, cols:].reshape(blocks * deep, cols)
     total[...] += dot(rows[...], own) + dot(rows_peer[...], other)
@@ -73,21 +75,23 @@
 def project(got, rows, rows_peer, basis, basis_peer, blocks):
     nz, height, lanes = got.shape
     count, keys, cols = rows.shape[0], basis.shape[1], lanes // 2
-    row_block = pl.BlockSpec((count, blocks * height // 2), lambda i: (0, i))
+    row_block = pl.BlockSpec((count, 2 * blocks * height // 2), lambda i: (0, i))
     whole = pl.BlockSpec(basis.shape, lambda i: (0, 0))
     made = nz * height // 4
+    groups = 2
+    step = groups * blocks
     return pl.pallas_call(
         project_kernel,
-        grid=(nz // blocks,),
+        grid=(nz // step,),
         in_specs=[
-            pl.BlockSpec((blocks, height, lanes), lambda i: (i, 0, 0)),
+            pl.BlockSpec((step, height, lanes), lambda i: (i, 0, 0)),
             row_block,
             row_block,
             whole,
             whole,
         ],
         out_specs=[
-            pl.BlockSpec((blocks, 1, height // 4, keys), lambda i: (0, i, 0, 0)),
+            pl.BlockSpec((blocks, groups, height // 4, keys), lambda i: (0, i, 0, 0)),
             pl.BlockSpec((count, cols), lambda i: (0, 0)),
         ],
         out_shape=[
@@ -130,13 +134,8 @@
     grad_b = lax.ppermute(
         lax.dynamic_index_in_dim(picked_grad, 1 - core, 0, keepdims=False), ("yl", "c"), crossed
     )
-    same, act_own = yl == core, mine(act_basis)
-    act_rows = jnp.concatenate(
-        [jnp.where(same, act_own, act_other), jnp.where(same, act_other, act_own)], axis=1
-    )
-    payload = jnp.concatenate(
-        [act_rows, jnp.where(same, grad_a, grad_b), jnp.where(same, grad_b, grad_a)], axis=0
-    )
+    act_rows = jnp.concatenate([mine(act_basis), act_other], axis=1)
+    payload = jnp.concatenate([act_rows, grad_a, grad_b], axis=0)
     gathered = lax.all_gather(payload, ("zh", "zl"), axis=0, tiled=False)
 
     plane = lax.axis_index("yh") * lax.axis_size("x") + lax.axis_index("x")
@@ -157,13 +156,17 @@
     rows = rows.reshape(2 * nz // nl * capacity, planes * share)
     rows_peer = swap(rows, "c")
 
-    part, act_sq = project(gathered, rows, rows_peer, basis_half, basis_peer, nl)
+    same = yl == core
+    rows_a, rows_b = jnp.where(same, rows, rows_peer), jnp.where(same, rows_peer, rows)
+    basis_a = jnp.where(same, basis_half, basis_peer)
+    basis_b = jnp.where(same, basis_peer, basis_half)
+    part, act_sq = project(gathered, rows_a, rows_b, basis_a, basis_b, nl)
     act_sq = lax.all_gather(act_sq, "zl", axis=0, tiled=False)
 
-    parts = lax.fori_loop(
-        0,
-        lax.optimization_barrier(jnp.int32(1)),
-        lambda trip, x: lax.all_to_all(x, PLANE, 0, 0, tiled=True),
+    parts = lax.cond(
+        lax.optimization_barrier(jnp.int32(1)) > 0,
+        lambda x: lax.all_to_all(x, PLANE, 0, 0, tiled=True),
+        lambda x: x,
         part.reshape(planes, nz * capacity // planes, -1),
     )
     grad_sq = jnp.square(jnp.sum(parts.astype(F32), axis=0)).astype(BF16)

time: 178 us -> 174 us (0.978)
  blocking collectives: 75 us -> 92.8 us
  waiting for transfers between devices: 32 us -> 16 us
  starting transfers between devices: 31 us -> 23.7 us
  other arithmetic: 4.06 us -> 8.93 us
    all_to_all x0 -> x1, blocking collectives: none -> 17.9 us  [per_device(): lax.all_to_all(x, PLANE, 0, 0, tiled=True)]
    all_to_all x1 -> x0, waiting for transfers between devices: 10.7 us -> none  [per_device(): lax.all_to_all(x, PLANE, 0, 0, tiled=True)]
    all_to_all x1 -> x0, starting transfers between devices: 7.31 us -> none  [per_device(): lax.all_to_all(x, PLANE, 0, 0, tiled=True)]
    all_gather x1, waiting for transfers between devices: 9.98 us -> 3.44 us  [per_device(): gathered = lax.all_gather(payload, ('zh', 'zl'), axis=0, tiled=False)]
    select_n x2, other arithmetic: 0.87 us -> 6.24 us  [the longest x1 3.97 us: per_device(): jnp.where(same, rows_peer, rows)]
  transfers between devices with their start and end apart: 12 -> 11, of which waited for: 6 -> 5; matrix products, arithmetic and copies ran while one was open for 6% -> 8% of each run, Pallas kernels for 1% -> 1%
where the time goes in v9:
time: 174 us; the launch traced here: 172 us
  blocking collectives  92.8 us (53%)
  starting transfers between devices  23.7 us (14%)
  waiting for transfers between devices  16 us (9%)
  between operations  13.7 us (8%)
  other arithmetic  8.93 us (5%)
  Pallas kernels  8.22 us (5%)
  local copies, waits for them, and re-layouts  5.46 us (3%)
  matrix products  3.06 us (2%)
    all_to_all x1, blocking collectives, per_device(): rows = lax.all_to_all(copies, PLANE, 0, 0, tiled=True)  31.4 us
    all_gather x1, blocking collectives, per_device(): rows = lax.all_gather(rows, 'zh', axis=0, tiled=True)  27.9 us
    ppermute x7, starting transfers between devices, swap(): return lax.ppermute(x, axis, [(0, 1), (1, 0)])  18.6 us
    all_to_all x1, blocking collectives, per_device(): lax.all_to_all(x, PLANE, 0, 0, tiled=True)  17.9 us
    all_to_all x1, blocking collectives, per_device(): lax.all_to_all(copies, PLANE, 0, 0, tiled=True).reshape(nz * capacity, -1)  15.5 us
    ppermute x7, waiting for transfers between devices, swap(): return lax.ppermute(x, axis, [(0, 1), (1, 0)])  10.6 us
    pallas_call x1, Pallas kernels, project(): pl.pallas_call(project_kernel, grid=(nz // step,), in_specs=[pl.BlockSpec...  6.18 us
    ppermute x1, starting transfers between devices, per_device(): lax.ppermute(lax.dynamic_index_in_dim(picked_grad, 1 - core, 0, keepdims=...  4.34 us
  transfers between devices with their start and end apart: 11, of which 5 were waited for; matrix products, arithmetic and copies ran while one was open for 8% of the time, Pallas kernels for 1%

profile of v9, /device:TPU:6, one launch (start us, length us, event | category | flops | bytes accessed | tf_op | source)
XLA Modules:
  0.0 171.8 jit_solution(11604225373237422621)
XLA Ops:
  6.5 1.0 dynamic-slice_bitcast_fusion.5
  7.5 3.5 %collective-permute-start = (bf16[128,256]{1,0:T(8,128)(2,1)S(1)}, bf16[128,256]{1,0:T(8,128)(2,1)S(1)}, u32[]{:S(2)}, u32[]{:S(2)}) collective-permute-start(bf16[128,256]{1,0:T(8,128)(2,1)S(1)} %get-tuple-element.31), channel_id=1, source_target_pairs={{0,256},{256,0},{1,257},{257,1},{2,258},{258,2},{3,259},{259,3},{4... | collective-permute-start | bytes 196616 | tf_op jit(solution)/shard_map/ppermute | solution.py:42
  11.0 2.0 %shard_map.55 = (bf16[2,64,512]{2,1,0:T(8,128)(2,1)}, bf16[2,64,128]{2,1,0:T(8,128)(2,1)}) custom-call(s32[2,128]{1,0:T(2,128)} %bitcast.62, bf16[2,128,512]{2,1,0:T(8,128)(2,1)} %grads.1), custom_call_target="tpu_custom_call" | custom-call | tf_op jit(solution)/shard_map/pallas_call | solution.py:32
  14.6 4.3 %collective-permute-start.2 = (bf16[64,512]{1,0:T(8,128)(2,1)S(1)}, bf16[64,512]{1,0:T(8,128)(2,1)S(1)}, u32[]{:S(2)}, u32[]{:S(2)}) collective-permute-start(bf16[64,512]{1,0:T(8,128)(2,1)S(1)} %get-tuple-element.33), channel_id=1, source_target_pairs={{0,256},{1,0},{256,257},{257,1},{2,258},{3,2},{258,259},{259,3},{4... | collective-permute-start | bytes 196616 | tf_op jit(solution)/shard_map/ppermute | solution.py:134
  19.0 1.9 %collective-permute-done.2 = bf16[64,512]{1,0:T(8,128)(2,1)S(1)} collective-permute-done((bf16[64,512]{1,0:T(8,128)(2,1)S(1)}, bf16[64,512]{1,0:T(8,128)(2,1)S(1)}, u32[]{:S(2)}, u32[]{:S(2)}) %collective-permute-start.2) | collective-permute-done | bytes 65568 | tf_op jit(solution)/shard_map/ppermute | solution.py:134
  23.4 4.3 %collective-permute-start.3 = (bf16[64,256]{1,0:T(8,128)(2,1)S(1)}, bf16[64,256]{1,0:T(8,128)(2,1)S(1)}, u32[]{:S(2)}, u32[]{:S(2)}) collective-permute-start(bf16[64,256]{1,0:T(8,128)(2,1)S(1)} %fusion.13), channel_id=1, source_target_pairs={{0,256},{256,0},{1,257},{257,1},{2,258},{258,2},{3,259},{259,3},{4... | collective-permute-start | bytes 98312 | tf_op jit(solution)/shard_map/ppermute | solution.py:42
  27.8 1.9 %collective-permute-start.4 = (bf16[512,256]{1,0:T(8,128)(2,1)S(1)}, bf16[512,256]{1,0:T(8,128)(2,1)S(1)}, u32[]{:S(2)}, u32[]{:S(2)}) collective-permute-start(bf16[512,256]{1,0:T(8,128)(2,1)S(1)} %get-tuple-element.29), channel_id=1, source_target_pairs={{0,256},{256,0},{1,257},{257,1},{2,258},{258,2},{3,259},{259,3},{4... | collective-permute-start | bytes 786440 | tf_op jit(solution)/shard_map/ppermute | solution.py:42
  29.8 27.9 %all_gather.17 = bf16[512,256]{1,0:T(8,128)(2,1)S(1)} all-gather(bf16[128,256]{1,0:T(8,128)(2,1)S(1)} %pad_maximum_fusion.2), channel_id=1, replica_groups=mesh['yl'=2,'zh'=4,'zl'=4,'yh'=2,'x'=4,'c'=2] {'zh'}, dimensions={0}, use_global_device_ids=true | all-gather | bytes 327680 | tf_op jit(solution)/shard_map/all_gather | solution.py:149
  58.7 31.4 %all_to_all.15 = bf16[8,512,256]{2,1,0:T(8,128)(2,1)S(1)} all-to-all(bf16[8,512,256]{2,1,0:T(8,128)(2,1)S(1)} %broadcast_in_dim.14), channel_id=1, replica_groups=mesh['yl'=2,'zh'=4,'zl'=4,'yh'=2,'x'=4,'c'=2] {'yh','x'}, dimensions={0} | all-to-all | bytes 4194304 | tf_op jit(solution)/shard_map/all_to_all | solution.py:154
  90.1 1.3 copy.6
  92.0 1.9 %collective-permute-start.5 = (bf16[512,2048]{1,0:T(8,128)(2,1)S(1)}, bf16[512,2048]{1,0:T(8,128)(2,1)}, u32[]{:S(2)}, u32[]{:S(2)}) collective-permute-start(bf16[512,2048]{1,0:T(8,128)(2,1)S(1)} %bitcast.49), channel_id=1, source_target_pairs={{0,1},{1,0},{2,3},{3,2},{4,5},{5,4},{6,7},{7,6},{8,9},{9,8},{10,11... | collective-permute-start | bytes 6291464 | tf_op jit(solution)/shard_map/ppermute | solution.py:42
  94.0 2.4 %collective-permute-start.6 = (bf16[512,512]{1,0:T(8,128)(2,1)}, bf16[512,512]{1,0:T(8,128)(2,1)}, u32[]{:S(2)}, u32[]{:S(2)}) collective-permute-start(bf16[512,512]{1,0:T(8,128)(2,1)} %pad_maximum_fusion), channel_id=1, source_target_pairs={{0,1},{1,0},{2,3},{3,2},{4,5},{5,4},{6,7},{7,6},{8,9},{9,8},{10,11... | collective-permute-start | bytes 1572872 | tf_op jit(solution)/shard_map/ppermute | solution.py:42
  96.4 2.8 %collective-permute-done.6 = bf16[512,512]{1,0:T(8,128)(2,1)} collective-permute-done((bf16[512,512]{1,0:T(8,128)(2,1)}, bf16[512,512]{1,0:T(8,128)(2,1)}, u32[]{:S(2)}, u32[]{:S(2)}) %collective-permute-start.6) | collective-permute-done | bytes 524320 | tf_op jit(solution)/shard_map/ppermute | solution.py:42
  99.2 2.3 %broadcast_select_fusion.2 = (bf16[512,512]{1,0:T(8,128)(2,1)}, bf16[512,512]{1,0:T(8,128)(2,1)}) fusion(bf16[512,512]{1,0:T(8,128)(2,1)} %collective-permute-done.6, bf16[512,512]{1,0:T(8,128)(2,1)} %pad_maximum_fusion, pred[]{:T(512)S(6)} %eq.16), kind=kLoop, calls=%fused_computation.18 | loop fusion | flops 524288 | bytes 2097153 | tf_op jit(solution)/shard_map/jit(_where)/select_n | solution.py:162
  101.4 4.0 %broadcast_select_fusion = (bf16[512,2048]{1,0:T(8,128)(2,1)}, bf16[512,2048]{1,0:T(8,128)(2,1)}) fusion(bf16[512,2048]{1,0:T(8,128)(2,1)} %collective-permute-done.5, bf16[512,2048]{1,0:T(8,128)(2,1)S(1)} %bitcast.50, pred[]{:T(512)S(6)} %eq.16), kind=kLoop, calls=%fused_computation.1 | loop fusion | flops 2097152 | bytes 8388609 | tf_op jit(solution)/shard_map/jit(_where)/select_n | solution.py:160
  105.4 3.4 %all-gather.5.cloned.1.call-done = bf16[4096,512]{1,0:T(8,128)(2,1)} async-done(((bf16[256,512]{1,0:T(8,128)(2,1)}), bf16[4096,512]{1,0:T(8,128)(2,1)}) %all-gather.5.cloned.1.call-update) | async-done | bytes 4194320 | tf_op jit(solution)/shard_map/all_gather | solution.py:139
  108.9 6.2 %shard_map.56 = (bf16[4,4,64,512]{3,2,1,0:T(8,128)(2,1)S(1)}, bf16[512,256]{1,0:T(8,128)(2,1)}) custom-call(bf16[16,256,512]{2,1,0:T(8,128)(2,1)} %bitcast.53, bf16[512,2048]{1,0:T(8,128)(2,1)} %get-tuple-element.23.rows, bf16[512,2048]{1,0:T(8,128)(2,1)} %get-tuple-element.22.rows_peer, bf16[512,512]{1,0:T(8,128)(2,1)} %get-tuple-element.27.basis, ...), custom_call_target="tpu_custom_call" | custom-call | flops 2147483648 | bytes 10747904 | tf_op jit(solution)/shard_map/pallas_call | solution.py:83
  115.1 18.0 %conditional.1 = (bf16[8,128,512]{2,1,0:T(8,128)(2,1)S(1)}) conditional(s32[]{:T(128)} %convert_element_type.19, bf16[8,128,512]{2,1,0:T(8,128)(2,1)S(1)} %bitcast.51, bf16[8,128,512]{2,1,0:T(8,128)(2,1)S(1)} %bitcast.52), branch_computations={%region_0.1_spmd, %region_1.2_spmd} | conditional | bytes 4194312 | solution.py:166
  115.1 17.9 %all_to_all.14 = bf16[8,128,512]{2,1,0:T(8,128)(2,1)S(1)} all-to-all(bf16[8,128,512]{2,1,0:T(8,128)(2,1)S(1)} %copy.10), channel_id=1, replica_groups=mesh['yl'=2,'zh'=4,'zl'=4,'yh'=2,'x'=4,'c'=2] {'yh','x'}, dimensions={0} | all-to-all | bytes 2097152 | tf_op jit(solution)/shard_map/cond/branch_1_fun/all_to_all | solution.py:168
  133.3 15.5 %all_to_all.16 = bf16[8,128,512]{2,1,0:T(8,128)(2,1)S(1)} all-to-all(bf16[8,128,512]{2,1,0:T(8,128)(2,1)S(1)} %broadcast_in_dim.15), channel_id=1, replica_groups=mesh['yl'=2,'zh'=4,'zl'=4,'yh'=2,'x'=4,'c'=2] {'yh','x'}, dimensions={0} | all-to-all | bytes 2097152 | tf_op jit(solution)/shard_map/all_to_all | solution.py:174
  148.9 1.9 %collective-permute-start.7 = (bf16[1024,512]{1,0:T(8,128)(2,1)S(1)}, bf16[1024,512]{1,0:T(8,128)(2,1)S(1)}, u32[]{:S(2)}, u32[]{:S(2)}) collective-permute-start(bf16[1024,512]{1,0:T(8,128)(2,1)S(1)} %bitcast.54), channel_id=1, source_target_pairs={{0,1},{1,0},{2,3},{3,2},{4,5},{5,4},{6,7},{7,6},{8,9},{9,8},{10,11... | collective-permute-start | bytes 3145736 | tf_op jit(solution)/shard_map/ppermute | solution.py:42
  150.8 1.3 constant_dynamic-slice_fusion
  153.8 2.7 %collective-permute-start.8 = (f32[256,256]{1,0:T(8,128)S(1)}, f32[256,256]{1,0:T(8,128)S(1)}, u32[]{:S(2)}, u32[]{:S(2)}) collective-permute-start(f32[256,256]{1,0:T(8,128)S(1)} %fusion.1), channel_id=1, source_target_pairs={{0,256},{256,0},{1,257},{257,1},{2,258},{258,2},{3,259},{259,3},{4... | collective-permute-start | bytes 786440 | tf_op jit(solution)/shard_map/ppermute | solution.py:42
  156.8 7.2 %collective-permute-done.8 = f32[256,256]{1,0:T(8,128)S(1)} collective-permute-done((f32[256,256]{1,0:T(8,128)S(1)}, f32[256,256]{1,0:T(8,128)S(1)}, u32[]{:S(2)}, u32[]{:S(2)}) %collective-permute-start.8) | collective-permute-done | bytes 262176 | tf_op jit(solution)/shard_map/ppermute | solution.py:42
  (37 shorter events, 9.0 us)
Async XLA Ops:
  6.5 15.1 %copy-start = (bf16[128,4096]{1,0:T(8,128)(2,1)S(1)}, bf16[128,4096]{1,0:T(8,128)(2,1)}, u32[]{:S(2)}) copy-start(bf16[128,4096]{1,0:T(8,128)(2,1)} %param.7) | copy-start | bytes 3145732
  6.5 21.2 %copy-start.1 = (bf16[2,512,256]{2,1,0:T(8,128)(2,1)S(1)}, bf16[2,512,256]{2,1,0:T(8,128)(2,1)}, u32[]{:S(2)}) copy-start(bf16[2,512,256]{2,1,0:T(8,128)(2,1)} %param.9) | copy-start | bytes 1572868
  6.5 102.3 %all-gather.5.cloned.1.call-start = ((), (), s32[]{:S(2)}) async-start(), calls=%async_computation.3 | async-start | bytes 4456448 | tf_op jit(solution)/shard_map/all_gather | solution.py:139
  7.5 11.4 %collective-permute-start = (bf16[128,256]{1,0:T(8,128)(2,1)S(1)}, bf16[128,256]{1,0:T(8,128)(2,1)S(1)}, u32[]{:S(2)}, u32[]{:S(2)}) collective-permute-start(bf16[128,256]{1,0:T(8,128)(2,1)S(1)} %get-tuple-element.31), channel_id=1, source_target_pairs={{0,256},{256,0},{1,257},{257,1},{2,258},{258,2},{3,259},{259,3},{4... | collective-permute-start | bytes 196616 | tf_op jit(solution)/shard_map/ppermute | solution.py:42
  14.0 5.0 %collective-permute-start.1 = (bf16[64,512]{1,0:T(8,128)(2,1)S(1)}, bf16[64,512]{1,0:T(8,128)(2,1)S(1)}, u32[]{:S(2)}, u32[]{:S(2)}) collective-permute-start(bf16[64,512]{1,0:T(8,128)(2,1)S(1)} %get-tuple-element.32), channel_id=1, source_target_pairs={{0,0},{1,256},{256,1},{257,257},{2,2},{3,258},{258,3},{259,259},{4... | collective-permute-start | bytes 196616 | tf_op jit(solution)/shard_map/ppermute | solution.py:131
  14.6 6.2 %collective-permute-start.2 = (bf16[64,512]{1,0:T(8,128)(2,1)S(1)}, bf16[64,512]{1,0:T(8,128)(2,1)S(1)}, u32[]{:S(2)}, u32[]{:S(2)}) collective-permute-start(bf16[64,512]{1,0:T(8,128)(2,1)S(1)} %get-tuple-element.33), channel_id=1, source_target_pairs={{0,256},{1,0},{256,257},{257,1},{2,258},{3,2},{258,259},{259,3},{4... | collective-permute-start | bytes 196616 | tf_op jit(solution)/shard_map/ppermute | solution.py:134
  21.6 129.2 %all-gather.7.cloned.1.call-start = ((), (), s32[]{:S(2)}) async-start(), calls=%async_computation.4 | async-start | bytes 1310720 | tf_op jit(solution)/shard_map/all_gather | solution.py:164
  23.4 6.3 %collective-permute-start.3 = (bf16[64,256]{1,0:T(8,128)(2,1)S(1)}, bf16[64,256]{1,0:T(8,128)(2,1)S(1)}, u32[]{:S(2)}, u32[]{:S(2)}) collective-permute-start(bf16[64,256]{1,0:T(8,128)(2,1)S(1)} %fusion.13), channel_id=1, source_target_pairs={{0,256},{256,0},{1,257},{257,1},{2,258},{258,2},{3,259},{259,3},{4... | collective-permute-start | bytes 98312 | tf_op jit(solution)/shard_map/ppermute | solution.py:42
  27.8 29.9 %collective-permute-start.4 = (bf16[512,256]{1,0:T(8,128)(2,1)S(1)}, bf16[512,256]{1,0:T(8,128)(2,1)S(1)}, u32[]{:S(2)}, u32[]{:S(2)}) collective-permute-start(bf16[512,256]{1,0:T(8,128)(2,1)S(1)} %get-tuple-element.29), channel_id=1, source_target_pairs={{0,256},{256,0},{1,257},{257,1},{2,258},{258,2},{3,259},{259,3},{4... | collective-permute-start | bytes 786440 | tf_op jit(solution)/shard_map/ppermute | solution.py:42
  92.0 9.4 %collective-permute-start.5 = (bf16[512,2048]{1,0:T(8,128)(2,1)S(1)}, bf16[512,2048]{1,0:T(8,128)(2,1)}, u32[]{:S(2)}, u32[]{:S(2)}) collective-permute-start(bf16[512,2048]{1,0:T(8,128)(2,1)S(1)} %bitcast.49), channel_id=1, source_target_pairs={{0,1},{1,0},{2,3},{3,2},{4,5},{5,4},{6,7},{7,6},{8,9},{9,8},{10,11... | collective-permute-start | bytes 6291464 | tf_op jit(solution)/shard_map/ppermute | solution.py:42
  94.0 5.2 %collective-permute-start.6 = (bf16[512,512]{1,0:T(8,128)(2,1)}, bf16[512,512]{1,0:T(8,128)(2,1)}, u32[]{:S(2)}, u32[]{:S(2)}) collective-permute-start(bf16[512,512]{1,0:T(8,128)(2,1)} %pad_maximum_fusion), channel_id=1, source_target_pairs={{0,1},{1,0},{2,3},{3,2},{4,5},{5,4},{6,7},{7,6},{8,9},{9,8},{10,11... | collective-permute-start | bytes 1572872 | tf_op jit(solution)/shard_map/ppermute | solution.py:42
  148.9 4.5 %collective-permute-start.7 = (bf16[1024,512]{1,0:T(8,128)(2,1)S(1)}, bf16[1024,512]{1,0:T(8,128)(2,1)S(1)}, u32[]{:S(2)}, u32[]{:S(2)}) collective-permute-start(bf16[1024,512]{1,0:T(8,128)(2,1)S(1)} %bitcast.54), channel_id=1, source_target_pairs={{0,1},{1,0},{2,3},{3,2},{4,5},{5,4},{6,7},{7,6},{8,9},{9,8},{10,11... | collective-permute-start | bytes 3145736 | tf_op jit(solution)/shard_map/ppermute | solution.py:42
  153.8 10.2 %collective-permute-start.8 = (f32[256,256]{1,0:T(8,128)S(1)}, f32[256,256]{1,0:T(8,128)S(1)}, u32[]{:S(2)}, u32[]{:S(2)}) collective-permute-start(f32[256,256]{1,0:T(8,128)S(1)} %fusion.1), channel_id=1, source_target_pairs={{0,256},{256,0},{1,257},{257,1},{2,258},{258,2},{3,259},{259,3},{4... | collective-permute-start | bytes 786440 | tf_op jit(solution)/shard_map/ppermute | solution.py:42
Sparse Core Ops, SparseCore 0:
  21.7 87.0 all-gather.4
  115.2 34.4 all-gather.6

commit v10 on v9

--- a/solution.py
+++ b/solution.py
@@ -7,7 +7,7 @@
 
 F32, BF16 = jnp.float32, jnp.bfloat16
 PLANE = ("yh", "x")
-VMEM_GRANT = 56
+VMEM_GRANT = 46
 
 
 def pick_kernel(ids, grads, picked, chooser):

time: 174 us -> 180 us (1.034)
  local copies, waits for them, and re-layouts: 5.46 us -> 10.3 us
    unnamed x5 -> x13, local copies, waits for them, and re-layouts: 0.69 us -> 4.36 us
  transfers between devices with their start and end apart: 11 -> 11, of which waited for: 5 -> 5; matrix products, arithmetic and copies ran while one was open for 8% -> 9% of each run, Pallas kernels for 1% -> 1%
where the time goes in v10:
time: 180 us; the launch traced here: 177 us
  blocking collectives  92.9 us (52%)
  starting transfers between devices  23.7 us (13%)
  waiting for transfers between devices  16 us (9%)
  between operations  13.7 us (8%)
  local copies, waits for them, and re-layouts  10.3 us (6%)
  other arithmetic  10.1 us (6%)
  Pallas kernels  7.12 us (4%)
  matrix products  3.06 us (2%)
    all_to_all x1, blocking collectives, per_device(): rows = lax.all_to_all(copies, PLANE, 0, 0, tiled=True)  31.4 us
    all_gather x1, blocking collectives, per_device(): rows = lax.all_gather(rows, 'zh', axis=0, tiled=True)  27.9 us
    ppermute x7, starting transfers between devices, swap(): return lax.ppermute(x, axis, [(0, 1), (1, 0)])  18.6 us
    all_to_all x1, blocking collectives, per_device(): lax.all_to_all(x, PLANE, 0, 0, tiled=True)  18 us
    all_to_all x1, blocking collectives, per_device(): lax.all_to_all(copies, PLANE, 0, 0, tiled=True).reshape(nz * capacity, -1)  15.5 us
    ppermute x7, waiting for transfers between devices, swap(): return lax.ppermute(x, axis, [(0, 1), (1, 0)])  10.6 us
    pallas_call x1, Pallas kernels, project(): pl.pallas_call(project_kernel, grid=(nz // step,), in_specs=[pl.BlockSpec...  5.08 us
    unnamed x13, local copies, waits for them, and re-layouts  4.36 us
  transfers between devices with their start and end apart: 11, of which 5 were waited for; matrix products, arithmetic and copies ran while one was open for 9% of the time, Pallas kernels for 1%

profile of v10, /device:TPU:6, one launch (start us, length us, event | category | flops | bytes accessed | tf_op | source)
XLA Modules:
  0.0 176.8 jit_solution(7624321008263139040)
XLA Ops:
  7.5 3.5 %collective-permute-start = (bf16[128,256]{1,0:T(8,128)(2,1)S(1)}, bf16[128,256]{1,0:T(8,128)(2,1)S(1)}, u32[]{:S(2)}, u32[]{:S(2)}) collective-permute-start(bf16[128,256]{1,0:T(8,128)(2,1)S(1)} %get-tuple-element.31), channel_id=1, source_target_pairs={{0,256},{256,0},{1,257},{257,1},{2,258},{258,2},{3,259},{259,3},{4... | collective-permute-start | bytes 196616 | tf_op jit(solution)/shard_map/ppermute | solution.py:42
  11.0 2.0 %shard_map.55 = (bf16[2,64,512]{2,1,0:T(8,128)(2,1)}, bf16[2,64,128]{2,1,0:T(8,128)(2,1)}) custom-call(s32[2,128]{1,0:T(2,128)} %bitcast.62, bf16[2,128,512]{2,1,0:T(8,128)(2,1)} %grads.1), custom_call_target="tpu_custom_call" | custom-call | tf_op jit(solution)/shard_map/pallas_call | solution.py:32
  14.6 4.3 %collective-permute-start.2 = (bf16[64,512]{1,0:T(8,128)(2,1)S(1)}, bf16[64,512]{1,0:T(8,128)(2,1)S(1)}, u32[]{:S(2)}, u32[]{:S(2)}) collective-permute-start(bf16[64,512]{1,0:T(8,128)(2,1)S(1)} %get-tuple-element.33), channel_id=1, source_target_pairs={{0,256},{1,0},{256,257},{257,1},{2,258},{3,2},{258,259},{259,3},{4... | collective-permute-start | bytes 196616 | tf_op jit(solution)/shard_map/ppermute | solution.py:134
  19.0 1.9 %collective-permute-done.2 = bf16[64,512]{1,0:T(8,128)(2,1)S(1)} collective-permute-done((bf16[64,512]{1,0:T(8,128)(2,1)S(1)}, bf16[64,512]{1,0:T(8,128)(2,1)S(1)}, u32[]{:S(2)}, u32[]{:S(2)}) %collective-permute-start.2) | collective-permute-done | bytes 65568 | tf_op jit(solution)/shard_map/ppermute | solution.py:134
  23.4 4.3 %collective-permute-start.3 = (bf16[64,256]{1,0:T(8,128)(2,1)S(1)}, bf16[64,256]{1,0:T(8,128)(2,1)S(1)}, u32[]{:S(2)}, u32[]{:S(2)}) collective-permute-start(bf16[64,256]{1,0:T(8,128)(2,1)S(1)} %fusion.13), channel_id=1, source_target_pairs={{0,256},{256,0},{1,257},{257,1},{2,258},{258,2},{3,259},{259,3},{4... | collective-permute-start | bytes 98312 | tf_op jit(solution)/shard_map/ppermute | solution.py:42
  27.8 1.9 %collective-permute-start.4 = (bf16[512,256]{1,0:T(8,128)(2,1)S(1)}, bf16[512,256]{1,0:T(8,128)(2,1)S(1)}, u32[]{:S(2)}, u32[]{:S(2)}) collective-permute-start(bf16[512,256]{1,0:T(8,128)(2,1)S(1)} %get-tuple-element.29), channel_id=1, source_target_pairs={{0,256},{256,0},{1,257},{257,1},{2,258},{258,2},{3,259},{259,3},{4... | collective-permute-start | bytes 786440 | tf_op jit(solution)/shard_map/ppermute | solution.py:42
  29.8 27.9 %all_gather.17 = bf16[512,256]{1,0:T(8,128)(2,1)S(1)} all-gather(bf16[128,256]{1,0:T(8,128)(2,1)S(1)} %pad_maximum_fusion.2), channel_id=1, replica_groups=mesh['yl'=2,'zh'=4,'zl'=4,'yh'=2,'x'=4,'c'=2] {'zh'}, dimensions={0}, use_global_device_ids=true | all-gather | bytes 327680 | tf_op jit(solution)/shard_map/all_gather | solution.py:149
  58.7 31.4 %all_to_all.15 = bf16[8,512,256]{2,1,0:T(8,128)(2,1)S(1)} all-to-all(bf16[8,512,256]{2,1,0:T(8,128)(2,1)S(1)} %broadcast_in_dim.14), channel_id=1, replica_groups=mesh['yl'=2,'zh'=4,'zl'=4,'yh'=2,'x'=4,'c'=2] {'yh','x'}, dimensions={0} | all-to-all | bytes 4194304 | tf_op jit(solution)/shard_map/all_to_all | solution.py:154
  90.0 1.3 copy.6
  92.0 1.9 %collective-permute-start.5 = (bf16[512,2048]{1,0:T(8,128)(2,1)S(1)}, bf16[512,2048]{1,0:T(8,128)(2,1)}, u32[]{:S(2)}, u32[]{:S(2)}) collective-permute-start(bf16[512,2048]{1,0:T(8,128)(2,1)S(1)} %bitcast.49), channel_id=1, source_target_pairs={{0,1},{1,0},{2,3},{3,2},{4,5},{5,4},{6,7},{7,6},{8,9},{9,8},{10,11... | collective-permute-start | bytes 6291464 | tf_op jit(solution)/shard_map/ppermute | solution.py:42
  94.0 2.4 %collective-permute-start.6 = (bf16[512,512]{1,0:T(8,128)(2,1)}, bf16[512,512]{1,0:T(8,128)(2,1)}, u32[]{:S(2)}, u32[]{:S(2)}) collective-permute-start(bf16[512,512]{1,0:T(8,128)(2,1)} %pad_maximum_fusion), channel_id=1, source_target_pairs={{0,1},{1,0},{2,3},{3,2},{4,5},{5,4},{6,7},{7,6},{8,9},{9,8},{10,11... | collective-permute-start | bytes 1572872 | tf_op jit(solution)/shard_map/ppermute | solution.py:42
  96.4 2.8 %collective-permute-done.6 = bf16[512,512]{1,0:T(8,128)(2,1)} collective-permute-done((bf16[512,512]{1,0:T(8,128)(2,1)}, bf16[512,512]{1,0:T(8,128)(2,1)}, u32[]{:S(2)}, u32[]{:S(2)}) %collective-permute-start.6) | collective-permute-done | bytes 524320 | tf_op jit(solution)/shard_map/ppermute | solution.py:42
  99.2 2.3 %broadcast_select_fusion.2 = (bf16[512,512]{1,0:T(8,128)(2,1)}, bf16[512,512]{1,0:T(8,128)(2,1)}) fusion(bf16[512,512]{1,0:T(8,128)(2,1)} %collective-permute-done.6, bf16[512,512]{1,0:T(8,128)(2,1)} %pad_maximum_fusion, pred[]{:T(512)S(6)} %eq.16), kind=kLoop, calls=%fused_computation.18 | loop fusion | flops 524288 | bytes 2097153 | tf_op jit(solution)/shard_map/jit(_where)/select_n | solution.py:162
  101.5 3.9 %broadcast_select_fusion = (bf16[512,2048]{1,0:T(8,128)(2,1)S(1)}, bf16[512,2048]{1,0:T(8,128)(2,1)}) fusion(bf16[512,2048]{1,0:T(8,128)(2,1)} %collective-permute-done.5, bf16[512,2048]{1,0:T(8,128)(2,1)} %bitcast.50, pred[]{:T(512)S(6)} %eq.16), kind=kLoop, calls=%fused_computation.1 | loop fusion | flops 2097152 | bytes 8388609 | tf_op jit(solution)/shard_map/jit(_where)/select_n | solution.py:160
  105.4 3.5 %all-gather.5.cloned.1.call-done = bf16[4096,512]{1,0:T(8,128)(2,1)} async-done(((bf16[256,512]{1,0:T(8,128)(2,1)}), bf16[4096,512]{1,0:T(8,128)(2,1)}) %all-gather.5.cloned.1.call-update) | async-done | bytes 4194320 | tf_op jit(solution)/shard_map/all_gather | solution.py:139
  108.9 1.6 copy-done.1
  112.5 5.1 %shard_map.56 = (bf16[4,4,64,512]{3,2,1,0:T(8,128)(2,1)}, bf16[512,256]{1,0:T(8,128)(2,1)}) custom-call(bf16[16,256,512]{2,1,0:T(8,128)(2,1)} %bitcast.53, bf16[512,2048]{1,0:T(8,128)(2,1)S(1)} %copy-done.1, bf16[512,2048]{1,0:T(8,128)(2,1)S(1)} %get-tuple-element.22.rows_peer, bf16[512,512]{1,0:T(8,128)(2,1)S(1)} %copy-done.3, bf16[512,512]{1,0:T(8,128)(2,1)S(1)} %copy-done.2), custom_call_target="tpu_custom_call" | custom-call | flops 2147483648 | bytes 10747904 | tf_op jit(solution)/shard_map/pallas_call | solution.py:83
  117.6 19.3 %conditional.1 = (bf16[8,128,512]{2,1,0:T(8,128)(2,1)}) conditional(s32[]{:T(128)} %convert_element_type.19, bf16[8,128,512]{2,1,0:T(8,128)(2,1)} %bitcast.51, bf16[8,128,512]{2,1,0:T(8,128)(2,1)} %bitcast.52), branch_computations={%region_0.1_spmd, %region_1.2_spmd} | conditional | bytes 6291492 | solution.py:166
  118.9 18.0 %all_to_all.14 = bf16[8,128,512]{2,1,0:T(8,128)(2,1)} all-to-all(bf16[8,128,512]{2,1,0:T(8,128)(2,1)S(1)} %copy-done.5), channel_id=1, replica_groups=mesh['yl'=2,'zh'=4,'zl'=4,'yh'=2,'x'=4,'c'=2] {'yh','x'}, dimensions={0} | all-to-all | bytes 2097152 | tf_op jit(solution)/shard_map/cond/branch_1_fun/all_to_all | solution.py:168
  136.9 1.4 convert_reduce_fusion
  138.4 15.5 %all_to_all.16 = bf16[8,128,512]{2,1,0:T(8,128)(2,1)S(1)} all-to-all(bf16[8,128,512]{2,1,0:T(8,128)(2,1)S(1)} %broadcast_in_dim.15), channel_id=1, replica_groups=mesh['yl'=2,'zh'=4,'zl'=4,'yh'=2,'x'=4,'c'=2] {'yh','x'}, dimensions={0} | all-to-all | bytes 2097152 | tf_op jit(solution)/shard_map/all_to_all | solution.py:174
  153.9 1.9 %collective-permute-start.7 = (bf16[1024,512]{1,0:T(8,128)(2,1)S(1)}, bf16[1024,512]{1,0:T(8,128)(2,1)S(1)}, u32[]{:S(2)}, u32[]{:S(2)}) collective-permute-start(bf16[1024,512]{1,0:T(8,128)(2,1)S(1)} %bitcast.54), channel_id=1, source_target_pairs={{0,1},{1,0},{2,3},{3,2},{4,5},{5,4},{6,7},{7,6},{8,9},{9,8},{10,11... | collective-permute-start | bytes 3145736 | tf_op jit(solution)/shard_map/ppermute | solution.py:42
  158.8 2.7 %collective-permute-start.8 = (f32[256,256]{1,0:T(8,128)S(1)}, f32[256,256]{1,0:T(8,128)S(1)}, u32[]{:S(2)}, u32[]{:S(2)}) collective-permute-start(f32[256,256]{1,0:T(8,128)S(1)} %fusion.1), channel_id=1, source_target_pairs={{0,256},{256,0},{1,257},{257,1},{2,258},{258,2},{3,259},{259,3},{4... | collective-permute-start | bytes 786440 | tf_op jit(solution)/shard_map/ppermute | solution.py:42
  161.9 7.2 %collective-permute-done.8 = f32[256,256]{1,0:T(8,128)S(1)} collective-permute-done((f32[256,256]{1,0:T(8,128)S(1)}, f32[256,256]{1,0:T(8,128)S(1)}, u32[]{:S(2)}, u32[]{:S(2)}) %collective-permute-start.8) | collective-permute-done | bytes 262176 | tf_op jit(solution)/shard_map/ppermute | solution.py:42
  (46 shorter events, 14.4 us)
Async XLA Ops:
  6.5 15.1 %copy-start = (bf16[128,4096]{1,0:T(8,128)(2,1)S(1)}, bf16[128,4096]{1,0:T(8,128)(2,1)}, u32[]{:S(2)}) copy-start(bf16[128,4096]{1,0:T(8,128)(2,1)} %param.7) | copy-start | bytes 3145732
  6.5 21.2 %copy-start.6 = (bf16[2,512,256]{2,1,0:T(8,128)(2,1)S(1)}, bf16[2,512,256]{2,1,0:T(8,128)(2,1)}, u32[]{:S(2)}) copy-start(bf16[2,512,256]{2,1,0:T(8,128)(2,1)} %param.9) | copy-start | bytes 1572868
  6.5 102.3 %all-gather.5.cloned.1.call-start = ((), (), s32[]{:S(2)}) async-start(), calls=%async_computation.3 | async-start | bytes 4456448 | tf_op jit(solution)/shard_map/all_gather | solution.py:139
  7.5 11.4 %collective-permute-start = (bf16[128,256]{1,0:T(8,128)(2,1)S(1)}, bf16[128,256]{1,0:T(8,128)(2,1)S(1)}, u32[]{:S(2)}, u32[]{:S(2)}) collective-permute-start(bf16[128,256]{1,0:T(8,128)(2,1)S(1)} %get-tuple-element.31), channel_id=1, source_target_pairs={{0,256},{256,0},{1,257},{257,1},{2,258},{258,2},{3,259},{259,3},{4... | collective-permute-start | bytes 196616 | tf_op jit(solution)/shard_map/ppermute | solution.py:42
  14.0 5.0 %collective-permute-start.1 = (bf16[64,512]{1,0:T(8,128)(2,1)S(1)}, bf16[64,512]{1,0:T(8,128)(2,1)S(1)}, u32[]{:S(2)}, u32[]{:S(2)}) collective-permute-start(bf16[64,512]{1,0:T(8,128)(2,1)S(1)} %get-tuple-element.32), channel_id=1, source_target_pairs={{0,0},{1,256},{256,1},{257,257},{2,2},{3,258},{258,3},{259,259},{4... | collective-permute-start | bytes 196616 | tf_op jit(solution)/shard_map/ppermute | solution.py:131
  14.6 6.2 %collective-permute-start.2 = (bf16[64,512]{1,0:T(8,128)(2,1)S(1)}, bf16[64,512]{1,0:T(8,128)(2,1)S(1)}, u32[]{:S(2)}, u32[]{:S(2)}) collective-permute-start(bf16[64,512]{1,0:T(8,128)(2,1)S(1)} %get-tuple-element.33), channel_id=1, source_target_pairs={{0,256},{1,0},{256,257},{257,1},{2,258},{3,2},{258,259},{259,3},{4... | collective-permute-start | bytes 196616 | tf_op jit(solution)/shard_map/ppermute | solution.py:134
  21.6 134.3 %all-gather.7.cloned.1.call-start = ((), (), s32[]{:S(2)}) async-start(), calls=%async_computation.4 | async-start | bytes 1310720 | tf_op jit(solution)/shard_map/all_gather | solution.py:164
  23.4 6.3 %collective-permute-start.3 = (bf16[64,256]{1,0:T(8,128)(2,1)S(1)}, bf16[64,256]{1,0:T(8,128)(2,1)S(1)}, u32[]{:S(2)}, u32[]{:S(2)}) collective-permute-start(bf16[64,256]{1,0:T(8,128)(2,1)S(1)} %fusion.13), channel_id=1, source_target_pairs={{0,256},{256,0},{1,257},{257,1},{2,258},{258,2},{3,259},{259,3},{4... | collective-permute-start | bytes 98312 | tf_op jit(solution)/shard_map/ppermute | solution.py:42
  27.8 29.9 %collective-permute-start.4 = (bf16[512,256]{1,0:T(8,128)(2,1)S(1)}, bf16[512,256]{1,0:T(8,128)(2,1)S(1)}, u32[]{:S(2)}, u32[]{:S(2)}) collective-permute-start(bf16[512,256]{1,0:T(8,128)(2,1)S(1)} %get-tuple-element.29), channel_id=1, source_target_pairs={{0,256},{256,0},{1,257},{257,1},{2,258},{258,2},{3,259},{259,3},{4... | collective-permute-start | bytes 786440 | tf_op jit(solution)/shard_map/ppermute | solution.py:42
  92.0 9.4 %copy-start.4 = (bf16[64,8,8,256]{3,1,2,0:T(8,128)(2,1)}, bf16[64,8,8,256]{3,1,2,0:T(8,128)(2,1)S(1)}, u32[]{:S(2)}) copy-start(bf16[64,8,8,256]{3,1,2,0:T(8,128)(2,1)S(1)} %copy.7) | copy-start | bytes 6291460
  92.0 9.4 %collective-permute-start.5 = (bf16[512,2048]{1,0:T(8,128)(2,1)S(1)}, bf16[512,2048]{1,0:T(8,128)(2,1)}, u32[]{:S(2)}, u32[]{:S(2)}) collective-permute-start(bf16[512,2048]{1,0:T(8,128)(2,1)S(1)} %bitcast.49), channel_id=1, source_target_pairs={{0,1},{1,0},{2,3},{3,2},{4,5},{5,4},{6,7},{7,6},{8,9},{9,8},{10,11... | collective-permute-start | bytes 6291464 | tf_op jit(solution)/shard_map/ppermute | solution.py:42
  94.0 5.2 %collective-permute-start.6 = (bf16[512,512]{1,0:T(8,128)(2,1)}, bf16[512,512]{1,0:T(8,128)(2,1)}, u32[]{:S(2)}, u32[]{:S(2)}) collective-permute-start(bf16[512,512]{1,0:T(8,128)(2,1)} %pad_maximum_fusion), channel_id=1, source_target_pairs={{0,1},{1,0},{2,3},{3,2},{4,5},{5,4},{6,7},{7,6},{8,9},{9,8},{10,11... | collective-permute-start | bytes 1572872 | tf_op jit(solution)/shard_map/ppermute | solution.py:42
  108.8 1.6 copy-start.1
  110.4 1.0 copy-start.2
  111.5 1.0 copy-start.3
  117.6 1.2 copy-start.5
  153.9 4.5 %collective-permute-start.7 = (bf16[1024,512]{1,0:T(8,128)(2,1)S(1)}, bf16[1024,512]{1,0:T(8,128)(2,1)S(1)}, u32[]{:S(2)}, u32[]{:S(2)}) collective-permute-start(bf16[1024,512]{1,0:T(8,128)(2,1)S(1)} %bitcast.54), channel_id=1, source_target_pairs={{0,1},{1,0},{2,3},{3,2},{4,5},{5,4},{6,7},{7,6},{8,9},{9,8},{10,11... | collective-permute-start | bytes 3145736 | tf_op jit(solution)/shard_map/ppermute | solution.py:42
  158.8 10.2 %collective-permute-start.8 = (f32[256,256]{1,0:T(8,128)S(1)}, f32[256,256]{1,0:T(8,128)S(1)}, u32[]{:S(2)}, u32[]{:S(2)}) collective-permute-start(f32[256,256]{1,0:T(8,128)S(1)} %fusion.1), channel_id=1, source_target_pairs={{0,256},{256,0},{1,257},{257,1},{2,258},{258,2},{3,259},{259,3},{4... | collective-permute-start | bytes 786440 | tf_op jit(solution)/shard_map/ppermute | solution.py:42
Sparse Core Ops, SparseCore 0:
  21.7 87.0 all-gather.4
  117.8 34.4 all-gather.6

commit v11 on v10

--- a/solution.py
+++ b/solution.py
@@ -7,7 +7,7 @@
 
 F32, BF16 = jnp.float32, jnp.bfloat16
 PLANE = ("yh", "x")
-VMEM_GRANT = 46
+VMEM_GRANT = 52
 
 
 def pick_kernel(ids, grads, picked, chooser):

time: 180 us -> 174 us (0.967)
  other arithmetic: 10.1 us -> 6.51 us
  local copies, waits for them, and re-layouts: 10.3 us -> 6.81 us
    unnamed x13 -> x5, local copies, waits for them, and re-layouts: 4.36 us -> 2.03 us
    select_n x1, other arithmetic: 2.28 us -> 0.07 us  [per_device(): basis_b = jnp.where(same, basis_peer, basis_half)]
  transfers between devices with their start and end apart: 11 -> 11, of which waited for: 5 -> 5; matrix products, arithmetic and copies ran while one was open for 9% -> 8% of each run, Pallas kernels for 1% -> 1%
where the time goes in v11:
time: 174 us; the launch traced here: 171 us
  blocking collectives  92.8 us (53%)
  starting transfers between devices  23.7 us (14%)
  waiting for transfers between devices  17 us (10%)
  between operations  13.7 us (8%)
  Pallas kernels  7.6 us (4%)
  local copies, waits for them, and re-layouts  6.81 us (4%)
  other arithmetic  6.51 us (4%)
  matrix products  3.06 us (2%)
    all_to_all x1, blocking collectives, per_device(): rows = lax.all_to_all(copies, PLANE, 0, 0, tiled=True)  31.4 us
    all_gather x1, blocking collectives, per_device(): rows = lax.all_gather(rows, 'zh', axis=0, tiled=True)  27.9 us
    ppermute x7, starting transfers between devices, swap(): return lax.ppermute(x, axis, [(0, 1), (1, 0)])  18.7 us
    all_to_all x1, blocking collectives, per_device(): lax.all_to_all(x, PLANE, 0, 0, tiled=True)  17.9 us
    all_to_all x1, blocking collectives, per_device(): lax.all_to_all(copies, PLANE, 0, 0, tiled=True).reshape(nz * capacity, -1)  15.6 us
    ppermute x7, waiting for transfers between devices, swap(): return lax.ppermute(x, axis, [(0, 1), (1, 0)])  10.2 us
    pallas_call x1, Pallas kernels, project(): pl.pallas_call(project_kernel, grid=(nz // step,), in_specs=[pl.BlockSpec...  5.56 us
    all_gather x1, waiting for transfers between devices, per_device(): gathered = lax.all_gather(payload, ('zh', 'zl'), axis=0, tiled=False)  4.86 us
  transfers between devices with their start and end apart: 11, of which 5 were waited for; matrix products, arithmetic and copies ran while one was open for 8% of the time, Pallas kernels for 1%

profile of v11, /device:TPU:6, one launch (start us, length us, event | category | flops | bytes accessed | tf_op | source)
XLA Modules:
  0.0 171.1 jit_solution(17243199885225347058)
XLA Ops:
  6.5 1.0 dynamic-slice_bitcast_fusion.5
  7.5 3.5 %collective-permute-start = (bf16[128,256]{1,0:T(8,128)(2,1)S(1)}, bf16[128,256]{1,0:T(8,128)(2,1)S(1)}, u32[]{:S(2)}, u32[]{:S(2)}) collective-permute-start(bf16[128,256]{1,0:T(8,128)(2,1)S(1)} %get-tuple-element.31), channel_id=1, source_target_pairs={{0,256},{256,0},{1,257},{257,1},{2,258},{258,2},{3,259},{259,3},{4... | collective-permute-start | bytes 196616 | tf_op jit(solution)/shard_map/ppermute | solution.py:42
  11.0 2.0 %shard_map.55 = (bf16[2,64,512]{2,1,0:T(8,128)(2,1)}, bf16[2,64,128]{2,1,0:T(8,128)(2,1)}) custom-call(s32[2,128]{1,0:T(2,128)} %bitcast.60, bf16[2,128,512]{2,1,0:T(8,128)(2,1)} %grads.1), custom_call_target="tpu_custom_call" | custom-call | tf_op jit(solution)/shard_map/pallas_call | solution.py:32
  14.6 4.3 %collective-permute-start.2 = (bf16[64,512]{1,0:T(8,128)(2,1)S(1)}, bf16[64,512]{1,0:T(8,128)(2,1)S(1)}, u32[]{:S(2)}, u32[]{:S(2)}) collective-permute-start(bf16[64,512]{1,0:T(8,128)(2,1)S(1)} %get-tuple-element.33), channel_id=1, source_target_pairs={{0,256},{1,0},{256,257},{257,1},{2,258},{3,2},{258,259},{259,3},{4... | collective-permute-start | bytes 196616 | tf_op jit(solution)/shard_map/ppermute | solution.py:134
  19.0 1.9 %collective-permute-done.2 = bf16[64,512]{1,0:T(8,128)(2,1)S(1)} collective-permute-done((bf16[64,512]{1,0:T(8,128)(2,1)S(1)}, bf16[64,512]{1,0:T(8,128)(2,1)S(1)}, u32[]{:S(2)}, u32[]{:S(2)}) %collective-permute-start.2) | collective-permute-done | bytes 65568 | tf_op jit(solution)/shard_map/ppermute | solution.py:134
  23.4 4.3 %collective-permute-start.3 = (bf16[64,256]{1,0:T(8,128)(2,1)S(1)}, bf16[64,256]{1,0:T(8,128)(2,1)S(1)}, u32[]{:S(2)}, u32[]{:S(2)}) collective-permute-start(bf16[64,256]{1,0:T(8,128)(2,1)S(1)} %fusion.13), channel_id=1, source_target_pairs={{0,256},{256,0},{1,257},{257,1},{2,258},{258,2},{3,259},{259,3},{4... | collective-permute-start | bytes 98312 | tf_op jit(solution)/shard_map/ppermute | solution.py:42
  27.8 1.9 %collective-permute-start.4 = (bf16[512,256]{1,0:T(8,128)(2,1)S(1)}, bf16[512,256]{1,0:T(8,128)(2,1)S(1)}, u32[]{:S(2)}, u32[]{:S(2)}) collective-permute-start(bf16[512,256]{1,0:T(8,128)(2,1)S(1)} %get-tuple-element.29), channel_id=1, source_target_pairs={{0,256},{256,0},{1,257},{257,1},{2,258},{258,2},{3,259},{259,3},{4... | collective-permute-start | bytes 786440 | tf_op jit(solution)/shard_map/ppermute | solution.py:42
  29.8 27.9 %all_gather.17 = bf16[512,256]{1,0:T(8,128)(2,1)S(1)} all-gather(bf16[128,256]{1,0:T(8,128)(2,1)S(1)} %pad_maximum_fusion.2), channel_id=1, replica_groups=mesh['yl'=2,'zh'=4,'zl'=4,'yh'=2,'x'=4,'c'=2] {'zh'}, dimensions={0}, use_global_device_ids=true | all-gather | bytes 327680 | tf_op jit(solution)/shard_map/all_gather | solution.py:149
  57.9 31.4 %all_to_all.15 = bf16[8,512,256]{2,1,0:T(8,128)(2,1)S(1)} all-to-all(bf16[8,512,256]{2,1,0:T(8,128)(2,1)S(1)} %broadcast_in_dim.14), channel_id=1, replica_groups=mesh['yl'=2,'zh'=4,'zl'=4,'yh'=2,'x'=4,'c'=2] {'yh','x'}, dimensions={0} | all-to-all | bytes 4194304 | tf_op jit(solution)/shard_map/all_to_all | solution.py:154
  89.3 1.3 copy.6
  90.6 2.0 %copy.7 = bf16[64,8,8,256]{3,1,2,0:T(8,128)(2,1)} copy(bf16[64,8,8,256]{3,2,1,0:T(8,128)(2,1)S(1)} %bitcast.48) | data formatting | bytes 4194304
  92.6 1.9 %collective-permute-start.5 = (bf16[512,2048]{1,0:T(8,128)(2,1)}, bf16[512,2048]{1,0:T(8,128)(2,1)}, u32[]{:S(2)}, u32[]{:S(2)}) collective-permute-start(bf16[512,2048]{1,0:T(8,128)(2,1)} %bitcast.24), channel_id=1, source_target_pairs={{0,1},{1,0},{2,3},{3,2},{4,5},{5,4},{6,7},{7,6},{8,9},{9,8},{10,11... | collective-permute-start | bytes 6291464 | tf_op jit(solution)/shard_map/ppermute | solution.py:42
  94.5 2.4 %collective-permute-start.6 = (bf16[512,512]{1,0:T(8,128)(2,1)S(1)}, bf16[512,512]{1,0:T(8,128)(2,1)S(1)}, u32[]{:S(2)}, u32[]{:S(2)}) collective-permute-start(bf16[512,512]{1,0:T(8,128)(2,1)S(1)} %pad_maximum_fusion), channel_id=1, source_target_pairs={{0,1},{1,0},{2,3},{3,2},{4,5},{5,4},{6,7},{7,6},{8,9},{9,8},{10,11... | collective-permute-start | bytes 1572872 | tf_op jit(solution)/shard_map/ppermute | solution.py:42
  96.9 2.5 %collective-permute-done.6 = bf16[512,512]{1,0:T(8,128)(2,1)S(1)} collective-permute-done((bf16[512,512]{1,0:T(8,128)(2,1)S(1)}, bf16[512,512]{1,0:T(8,128)(2,1)S(1)}, u32[]{:S(2)}, u32[]{:S(2)}) %collective-permute-start.6) | collective-permute-done | bytes 524320 | tf_op jit(solution)/shard_map/ppermute | solution.py:42
  99.5 4.5 %broadcast_select_fusion = (bf16[512,2048]{1,0:T(8,128)(2,1)}, bf16[512,2048]{1,0:T(8,128)(2,1)}) fusion(bf16[512,2048]{1,0:T(8,128)(2,1)} %collective-permute-done.5, bf16[512,2048]{1,0:T(8,128)(2,1)} %bitcast.24, pred[]{:T(512)S(6)} %eq.16), kind=kLoop, calls=%fused_computation.1 | loop fusion | flops 2097152 | bytes 8388609 | tf_op jit(solution)/shard_map/jit(_where)/select_n | solution.py:160
  104.0 4.9 %all-gather.5.cloned.1.call-done = bf16[4096,512]{1,0:T(8,128)(2,1)} async-done(((bf16[256,512]{1,0:T(8,128)(2,1)}), bf16[4096,512]{1,0:T(8,128)(2,1)}) %all-gather.5.cloned.1.call-update) | async-done | bytes 4194320 | tf_op jit(solution)/shard_map/all_gather | solution.py:139
  108.9 5.6 %shard_map.56 = (bf16[4,4,64,512]{3,2,1,0:T(8,128)(2,1)S(1)}, bf16[512,256]{1,0:T(8,128)(2,1)}) custom-call(bf16[16,256,512]{2,1,0:T(8,128)(2,1)} %bitcast.51, bf16[512,2048]{1,0:T(8,128)(2,1)} %get-tuple-element.23.rows, bf16[512,2048]{1,0:T(8,128)(2,1)} %get-tuple-element.22.rows_peer, bf16[512,512]{1,0:T(8,128)(2,1)S(1)} %get-tuple-element.27.basis, ...), custom_call_target="tpu_custom_call" | custom-call | flops 2147483648 | bytes 10747904 | tf_op jit(solution)/shard_map/pallas_call | solution.py:83
  114.4 17.9 %conditional.1 = (bf16[8,128,512]{2,1,0:T(8,128)(2,1)S(1)}) conditional(s32[]{:T(128)} %convert_element_type.19, bf16[8,128,512]{2,1,0:T(8,128)(2,1)S(1)} %bitcast.49, bf16[8,128,512]{2,1,0:T(8,128)(2,1)S(1)} %bitcast.50), branch_computations={%region_0.1_spmd, %region_1.2_spmd} | conditional | bytes 4194312 | solution.py:166
  114.5 17.9 %all_to_all.14 = bf16[8,128,512]{2,1,0:T(8,128)(2,1)S(1)} all-to-all(bf16[8,128,512]{2,1,0:T(8,128)(2,1)S(1)} %copy.10), channel_id=1, replica_groups=mesh['yl'=2,'zh'=4,'zl'=4,'yh'=2,'x'=4,'c'=2] {'yh','x'}, dimensions={0} | all-to-all | bytes 2097152 | tf_op jit(solution)/shard_map/cond/branch_1_fun/all_to_all | solution.py:168
  132.7 15.6 %all_to_all.16 = bf16[8,128,512]{2,1,0:T(8,128)(2,1)S(1)} all-to-all(bf16[8,128,512]{2,1,0:T(8,128)(2,1)S(1)} %broadcast_in_dim.15), channel_id=1, replica_groups=mesh['yl'=2,'zh'=4,'zl'=4,'yh'=2,'x'=4,'c'=2] {'yh','x'}, dimensions={0} | all-to-all | bytes 2097152 | tf_op jit(solution)/shard_map/all_to_all | solution.py:174
  148.3 1.9 %collective-permute-start.7 = (bf16[1024,512]{1,0:T(8,128)(2,1)S(1)}, bf16[1024,512]{1,0:T(8,128)(2,1)S(1)}, u32[]{:S(2)}, u32[]{:S(2)}) collective-permute-start(bf16[1024,512]{1,0:T(8,128)(2,1)S(1)} %bitcast.52), channel_id=1, source_target_pairs={{0,1},{1,0},{2,3},{3,2},{4,5},{5,4},{6,7},{7,6},{8,9},{9,8},{10,11... | collective-permute-start | bytes 3145736 | tf_op jit(solution)/shard_map/ppermute | solution.py:42
  150.2 1.3 constant_dynamic-slice_fusion
  153.2 2.8 %collective-permute-start.8 = (f32[256,256]{1,0:T(8,128)S(1)}, f32[256,256]{1,0:T(8,128)S(1)}, u32[]{:S(2)}, u32[]{:S(2)}) collective-permute-start(f32[256,256]{1,0:T(8,128)S(1)} %fusion.1), channel_id=1, source_target_pairs={{0,256},{256,0},{1,257},{257,1},{2,258},{258,2},{3,259},{259,3},{4... | collective-permute-start | bytes 786440 | tf_op jit(solution)/shard_map/ppermute | solution.py:42
  156.3 7.1 %collective-permute-done.8 = f32[256,256]{1,0:T(8,128)S(1)} collective-permute-done((f32[256,256]{1,0:T(8,128)S(1)}, f32[256,256]{1,0:T(8,128)S(1)}, u32[]{:S(2)}, u32[]{:S(2)}) %collective-permute-start.8) | collective-permute-done | bytes 262176 | tf_op jit(solution)/shard_map/ppermute | solution.py:42
  (37 shorter events, 7.6 us)
Async XLA Ops:
  6.5 15.1 %copy-start = (bf16[128,4096]{1,0:T(8,128)(2,1)S(1)}, bf16[128,4096]{1,0:T(8,128)(2,1)}, u32[]{:S(2)}) copy-start(bf16[128,4096]{1,0:T(8,128)(2,1)} %param.7) | copy-start | bytes 3145732
  6.5 21.2 %copy-start.1 = (bf16[2,512,256]{2,1,0:T(8,128)(2,1)S(1)}, bf16[2,512,256]{2,1,0:T(8,128)(2,1)}, u32[]{:S(2)}) copy-start(bf16[2,512,256]{2,1,0:T(8,128)(2,1)} %param.9) | copy-start | bytes 1572868
  6.5 102.3 %all-gather.5.cloned.1.call-start = ((), (), s32[]{:S(2)}) async-start(), calls=%async_computation.3 | async-start | bytes 4456448 | tf_op jit(solution)/shard_map/all_gather | solution.py:139
  7.5 11.4 %collective-permute-start = (bf16[128,256]{1,0:T(8,128)(2,1)S(1)}, bf16[128,256]{1,0:T(8,128)(2,1)S(1)}, u32[]{:S(2)}, u32[]{:S(2)}) collective-permute-start(bf16[128,256]{1,0:T(8,128)(2,1)S(1)} %get-tuple-element.31), channel_id=1, source_target_pairs={{0,256},{256,0},{1,257},{257,1},{2,258},{258,2},{3,259},{259,3},{4... | collective-permute-start | bytes 196616 | tf_op jit(solution)/shard_map/ppermute | solution.py:42
  14.0 5.0 %collective-permute-start.1 = (bf16[64,512]{1,0:T(8,128)(2,1)S(1)}, bf16[64,512]{1,0:T(8,128)(2,1)S(1)}, u32[]{:S(2)}, u32[]{:S(2)}) collective-permute-start(bf16[64,512]{1,0:T(8,128)(2,1)S(1)} %get-tuple-element.32), channel_id=1, source_target_pairs={{0,0},{1,256},{256,1},{257,257},{2,2},{3,258},{258,3},{259,259},{4... | collective-permute-start | bytes 196616 | tf_op jit(solution)/shard_map/ppermute | solution.py:131
  14.6 6.2 %collective-permute-start.2 = (bf16[64,512]{1,0:T(8,128)(2,1)S(1)}, bf16[64,512]{1,0:T(8,128)(2,1)S(1)}, u32[]{:S(2)}, u32[]{:S(2)}) collective-permute-start(bf16[64,512]{1,0:T(8,128)(2,1)S(1)} %get-tuple-element.33), channel_id=1, source_target_pairs={{0,256},{1,0},{256,257},{257,1},{2,258},{3,2},{258,259},{259,3},{4... | collective-permute-start | bytes 196616 | tf_op jit(solution)/shard_map/ppermute | solution.py:134
  21.6 128.6 %all-gather.7.cloned.1.call-start = ((), (), s32[]{:S(2)}) async-start(), calls=%async_computation.4 | async-start | bytes 1310720 | tf_op jit(solution)/shard_map/all_gather | solution.py:164
  23.4 6.3 %collective-permute-start.3 = (bf16[64,256]{1,0:T(8,128)(2,1)S(1)}, bf16[64,256]{1,0:T(8,128)(2,1)S(1)}, u32[]{:S(2)}, u32[]{:S(2)}) collective-permute-start(bf16[64,256]{1,0:T(8,128)(2,1)S(1)} %fusion.13), channel_id=1, source_target_pairs={{0,256},{256,0},{1,257},{257,1},{2,258},{258,2},{3,259},{259,3},{4... | collective-permute-start | bytes 98312 | tf_op jit(solution)/shard_map/ppermute | solution.py:42
  27.8 29.9 %collective-permute-start.4 = (bf16[512,256]{1,0:T(8,128)(2,1)S(1)}, bf16[512,256]{1,0:T(8,128)(2,1)S(1)}, u32[]{:S(2)}, u32[]{:S(2)}) collective-permute-start(bf16[512,256]{1,0:T(8,128)(2,1)S(1)} %get-tuple-element.29), channel_id=1, source_target_pairs={{0,256},{256,0},{1,257},{257,1},{2,258},{258,2},{3,259},{259,3},{4... | collective-permute-start | bytes 786440 | tf_op jit(solution)/shard_map/ppermute | solution.py:42
  92.6 6.9 %collective-permute-start.5 = (bf16[512,2048]{1,0:T(8,128)(2,1)}, bf16[512,2048]{1,0:T(8,128)(2,1)}, u32[]{:S(2)}, u32[]{:S(2)}) collective-permute-start(bf16[512,2048]{1,0:T(8,128)(2,1)} %bitcast.24), channel_id=1, source_target_pairs={{0,1},{1,0},{2,3},{3,2},{4,5},{5,4},{6,7},{7,6},{8,9},{9,8},{10,11... | collective-permute-start | bytes 6291464 | tf_op jit(solution)/shard_map/ppermute | solution.py:42
  94.5 4.9 %collective-permute-start.6 = (bf16[512,512]{1,0:T(8,128)(2,1)S(1)}, bf16[512,512]{1,0:T(8,128)(2,1)S(1)}, u32[]{:S(2)}, u32[]{:S(2)}) collective-permute-start(bf16[512,512]{1,0:T(8,128)(2,1)S(1)} %pad_maximum_fusion), channel_id=1, source_target_pairs={{0,1},{1,0},{2,3},{3,2},{4,5},{5,4},{6,7},{7,6},{8,9},{9,8},{10,11... | collective-permute-start | bytes 1572872 | tf_op jit(solution)/shard_map/ppermute | solution.py:42
  148.3 4.5 %collective-permute-start.7 = (bf16[1024,512]{1,0:T(8,128)(2,1)S(1)}, bf16[1024,512]{1,0:T(8,128)(2,1)S(1)}, u32[]{:S(2)}, u32[]{:S(2)}) collective-permute-start(bf16[1024,512]{1,0:T(8,128)(2,1)S(1)} %bitcast.52), channel_id=1, source_target_pairs={{0,1},{1,0},{2,3},{3,2},{4,5},{5,4},{6,7},{7,6},{8,9},{9,8},{10,11... | collective-permute-start | bytes 3145736 | tf_op jit(solution)/shard_map/ppermute | solution.py:42
  153.2 10.2 %collective-permute-start.8 = (f32[256,256]{1,0:T(8,128)S(1)}, f32[256,256]{1,0:T(8,128)S(1)}, u32[]{:S(2)}, u32[]{:S(2)}) collective-permute-start(f32[256,256]{1,0:T(8,128)S(1)} %fusion.1), channel_id=1, source_target_pairs={{0,256},{256,0},{1,257},{257,1},{2,258},{258,2},{3,259},{259,3},{4... | collective-permute-start | bytes 786440 | tf_op jit(solution)/shard_map/ppermute | solution.py:42
Sparse Core Ops, SparseCore 0:
  21.7 87.0 all-gather.4
  114.6 34.3 all-gather.6

commit v12 on v11

--- a/solution.py
+++ b/solution.py
@@ -172,7 +172,6 @@
     grad_sq = jnp.square(jnp.sum(parts.astype(F32), axis=0)).astype(BF16)
     copies = jnp.broadcast_to(grad_sq[None], (planes,) + grad_sq.shape)
     grad_sq = lax.all_to_all(copies, PLANE, 0, 0, tiled=True).reshape(nz * capacity, -1)
-    grad_sq_other = swap(grad_sq, "c")
 
     act_sq = act_sq.reshape(nl, 2, nz // nl * capacity, cols)
 
@@ -185,7 +184,8 @@
         return lax.dot_general(g, a, (((0,), (0,)), ((), ())), preferred_element_type=F32)
 
     def block(lo, hi):
-        own, other = grad_sq[:, lo:hi], grad_sq_other[:, lo:hi]
+        own = grad_sq[:, lo:hi]
+        other = swap(own, "c")
         return (outer(own, act_first) + outer(other, act_second)) / token_total
 
     keys = grad_sq.shape[1]

time: 174 us -> 176 us (1.011)
  starting transfers between devices: 23.7 us -> 26.2 us
    ppermute x7 -> x8, starting transfers between devices: 18.7 us -> 21.2 us  [swap(): return lax.ppermute(x, axis, [(0, 1), (1, 0)])]
    ppermute x7 -> x8, waiting for transfers between devices: 10.2 us -> 9.02 us  [swap(): return lax.ppermute(x, axis, [(0, 1), (1, 0)])]
  transfers between devices with their start and end apart: 11 -> 12, of which waited for: 5 -> 4; matrix products, arithmetic and copies ran while one was open for 8% -> 9% of each run, Pallas kernels for 1% -> 1%
where the time goes in v12:
time: 176 us; the launch traced here: 173 us
  blocking collectives  92.7 us (53%)
  starting transfers between devices  26.2 us (15%)
  waiting for transfers between devices  15.7 us (9%)
  between operations  13.7 us (8%)
  local copies, waits for them, and re-layouts  7.94 us (5%)
  Pallas kernels  7.6 us (4%)
  other arithmetic  6.54 us (4%)
  matrix products  3.06 us (2%)
    all_to_all x1, blocking collectives, per_device(): rows = lax.all_to_all(copies, PLANE, 0, 0, tiled=True)  31.4 us
    all_gather x1, blocking collectives, per_device(): rows = lax.all_gather(rows, 'zh', axis=0, tiled=True)  27.9 us
    ppermute x8, starting transfers between devices, swap(): return lax.ppermute(x, axis, [(0, 1), (1, 0)])  21.2 us
    all_to_all x1, blocking collectives, per_device(): lax.all_to_all(x, PLANE, 0, 0, tiled=True)  17.9 us
    all_to_all x1, blocking collectives, per_device(): lax.all_to_all(copies, PLANE, 0, 0, tiled=True).reshape(nz * capacity, -1)  15.5 us
    ppermute x8, waiting for transfers between devices, swap(): return lax.ppermute(x, axis, [(0, 1), (1, 0)])  9.02 us
    pallas_call x1, Pallas kernels, project(): pl.pallas_call(project_kernel, grid=(nz // step,), in_specs=[pl.BlockSpec...  5.56 us
    all_gather x1, waiting for transfers between devices, per_device(): gathered = lax.all_gather(payload, ('zh', 'zl'), axis=0, tiled=False)  4.76 us
  transfers between devices with their start and end apart: 12, of which 4 were waited for; matrix products, arithmetic and copies ran while one was open for 9% of the time, Pallas kernels for 1%

profile of v12, /device:TPU:6, one launch (start us, length us, event | category | flops | bytes accessed | tf_op | source)
XLA Modules:
  0.0 173.5 jit_solution(54334332996387592)
XLA Ops:
  7.5 3.5 %collective-permute-start = (bf16[128,256]{1,0:T(8,128)(2,1)S(1)}, bf16[128,256]{1,0:T(8,128)(2,1)S(1)}, u32[]{:S(2)}, u32[]{:S(2)}) collective-permute-start(bf16[128,256]{1,0:T(8,128)(2,1)S(1)} %get-tuple-element.33), channel_id=1, source_target_pairs={{0,256},{256,0},{1,257},{257,1},{2,258},{258,2},{3,259},{259,3},{4... | collective-permute-start | bytes 196616 | tf_op jit(solution)/shard_map/ppermute | solution.py:42
  11.0 2.0 %shard_map.55 = (bf16[2,64,512]{2,1,0:T(8,128)(2,1)}, bf16[2,64,128]{2,1,0:T(8,128)(2,1)}) custom-call(s32[2,128]{1,0:T(2,128)} %bitcast.62, bf16[2,128,512]{2,1,0:T(8,128)(2,1)} %grads.1), custom_call_target="tpu_custom_call" | custom-call | tf_op jit(solution)/shard_map/pallas_call | solution.py:32
  14.6 4.3 %collective-permute-start.2 = (bf16[64,512]{1,0:T(8,128)(2,1)S(1)}, bf16[64,512]{1,0:T(8,128)(2,1)S(1)}, u32[]{:S(2)}, u32[]{:S(2)}) collective-permute-start(bf16[64,512]{1,0:T(8,128)(2,1)S(1)} %get-tuple-element.35), channel_id=1, source_target_pairs={{0,256},{1,0},{256,257},{257,1},{2,258},{3,2},{258,259},{259,3},{4... | collective-permute-start | bytes 196616 | tf_op jit(solution)/shard_map/ppermute | solution.py:134
  19.0 1.9 %collective-permute-done.2 = bf16[64,512]{1,0:T(8,128)(2,1)S(1)} collective-permute-done((bf16[64,512]{1,0:T(8,128)(2,1)S(1)}, bf16[64,512]{1,0:T(8,128)(2,1)S(1)}, u32[]{:S(2)}, u32[]{:S(2)}) %collective-permute-start.2) | collective-permute-done | bytes 65568 | tf_op jit(solution)/shard_map/ppermute | solution.py:134
  23.4 4.3 %collective-permute-start.3 = (bf16[64,256]{1,0:T(8,128)(2,1)S(1)}, bf16[64,256]{1,0:T(8,128)(2,1)S(1)}, u32[]{:S(2)}, u32[]{:S(2)}) collective-permute-start(bf16[64,256]{1,0:T(8,128)(2,1)S(1)} %fusion.7), channel_id=1, source_target_pairs={{0,256},{256,0},{1,257},{257,1},{2,258},{258,2},{3,259},{259,3},{4... | collective-permute-start | bytes 98312 | tf_op jit(solution)/shard_map/ppermute | solution.py:42
  27.8 1.9 %collective-permute-start.4 = (bf16[512,256]{1,0:T(8,128)(2,1)S(1)}, bf16[512,256]{1,0:T(8,128)(2,1)S(1)}, u32[]{:S(2)}, u32[]{:S(2)}) collective-permute-start(bf16[512,256]{1,0:T(8,128)(2,1)S(1)} %get-tuple-element.31), channel_id=1, source_target_pairs={{0,256},{256,0},{1,257},{257,1},{2,258},{258,2},{3,259},{259,3},{4... | collective-permute-start | bytes 786440 | tf_op jit(solution)/shard_map/ppermute | solution.py:42
  29.8 27.9 %all_gather.17 = bf16[512,256]{1,0:T(8,128)(2,1)S(1)} all-gather(bf16[128,256]{1,0:T(8,128)(2,1)S(1)} %pad_maximum_fusion.2), channel_id=1, replica_groups=mesh['yl'=2,'zh'=4,'zl'=4,'yh'=2,'x'=4,'c'=2] {'zh'}, dimensions={0}, use_global_device_ids=true | all-gather | bytes 327680 | tf_op jit(solution)/shard_map/all_gather | solution.py:149
  57.9 31.4 %all_to_all.15 = bf16[8,512,256]{2,1,0:T(8,128)(2,1)S(1)} all-to-all(bf16[8,512,256]{2,1,0:T(8,128)(2,1)S(1)} %broadcast_in_dim.14), channel_id=1, replica_groups=mesh['yl'=2,'zh'=4,'zl'=4,'yh'=2,'x'=4,'c'=2] {'yh','x'}, dimensions={0} | all-to-all | bytes 4194304 | tf_op jit(solution)/shard_map/all_to_all | solution.py:154
  89.3 1.3 copy.6
  90.6 2.1 %copy.7 = bf16[64,8,8,256]{3,1,2,0:T(8,128)(2,1)} copy(bf16[64,8,8,256]{3,2,1,0:T(8,128)(2,1)S(1)} %bitcast.50) | data formatting | bytes 4194304
  92.6 1.9 %collective-permute-start.5 = (bf16[512,2048]{1,0:T(8,128)(2,1)}, bf16[512,2048]{1,0:T(8,128)(2,1)}, u32[]{:S(2)}, u32[]{:S(2)}) collective-permute-start(bf16[512,2048]{1,0:T(8,128)(2,1)} %bitcast.24), channel_id=1, source_target_pairs={{0,1},{1,0},{2,3},{3,2},{4,5},{5,4},{6,7},{7,6},{8,9},{9,8},{10,11... | collective-permute-start | bytes 6291464 | tf_op jit(solution)/shard_map/ppermute | solution.py:42
  94.6 2.4 %collective-permute-start.6 = (bf16[512,512]{1,0:T(8,128)(2,1)S(1)}, bf16[512,512]{1,0:T(8,128)(2,1)S(1)}, u32[]{:S(2)}, u32[]{:S(2)}) collective-permute-start(bf16[512,512]{1,0:T(8,128)(2,1)S(1)} %pad_maximum_fusion), channel_id=1, source_target_pairs={{0,1},{1,0},{2,3},{3,2},{4,5},{5,4},{6,7},{7,6},{8,9},{9,8},{10,11... | collective-permute-start | bytes 1572872 | tf_op jit(solution)/shard_map/ppermute | solution.py:42
  97.0 2.5 %collective-permute-done.6 = bf16[512,512]{1,0:T(8,128)(2,1)S(1)} collective-permute-done((bf16[512,512]{1,0:T(8,128)(2,1)S(1)}, bf16[512,512]{1,0:T(8,128)(2,1)S(1)}, u32[]{:S(2)}, u32[]{:S(2)}) %collective-permute-start.6) | collective-permute-done | bytes 524320 | tf_op jit(solution)/shard_map/ppermute | solution.py:42
  99.5 4.6 %broadcast_select_fusion = (bf16[512,2048]{1,0:T(8,128)(2,1)}, bf16[512,2048]{1,0:T(8,128)(2,1)}) fusion(bf16[512,2048]{1,0:T(8,128)(2,1)} %collective-permute-done.5, bf16[512,2048]{1,0:T(8,128)(2,1)} %bitcast.24, pred[]{:T(512)S(6)} %eq.16), kind=kLoop, calls=%fused_computation.1 | loop fusion | flops 2097152 | bytes 8388609 | tf_op jit(solution)/shard_map/jit(_where)/select_n | solution.py:160
  104.1 4.8 %all-gather.5.cloned.1.call-done = bf16[4096,512]{1,0:T(8,128)(2,1)} async-done(((bf16[256,512]{1,0:T(8,128)(2,1)}), bf16[4096,512]{1,0:T(8,128)(2,1)}) %all-gather.5.cloned.1.call-update) | async-done | bytes 4194320 | tf_op jit(solution)/shard_map/all_gather | solution.py:139
  108.9 5.6 %shard_map.56 = (bf16[4,4,64,512]{3,2,1,0:T(8,128)(2,1)S(1)}, bf16[512,256]{1,0:T(8,128)(2,1)}) custom-call(bf16[16,256,512]{2,1,0:T(8,128)(2,1)} %bitcast.55, bf16[512,2048]{1,0:T(8,128)(2,1)} %get-tuple-element.23.rows, bf16[512,2048]{1,0:T(8,128)(2,1)} %get-tuple-element.22.rows_peer, bf16[512,512]{1,0:T(8,128)(2,1)S(1)} %get-tuple-element.29.basis, ...), custom_call_target="tpu_custom_call" | custom-call | flops 2147483648 | bytes 10747904 | tf_op jit(solution)/shard_map/pallas_call | solution.py:83
  114.4 17.9 %conditional.1 = (bf16[8,128,512]{2,1,0:T(8,128)(2,1)S(1)}) conditional(s32[]{:T(128)} %convert_element_type.19, bf16[8,128,512]{2,1,0:T(8,128)(2,1)S(1)} %bitcast.53, bf16[8,128,512]{2,1,0:T(8,128)(2,1)S(1)} %bitcast.54), branch_computations={%region_0.1_spmd, %region_1.2_spmd} | conditional | bytes 4194312 | solution.py:166
  114.5 17.9 %all_to_all.14 = bf16[8,128,512]{2,1,0:T(8,128)(2,1)S(1)} all-to-all(bf16[8,128,512]{2,1,0:T(8,128)(2,1)S(1)} %copy.10), channel_id=1, replica_groups=mesh['yl'=2,'zh'=4,'zl'=4,'yh'=2,'x'=4,'c'=2] {'yh','x'}, dimensions={0} | all-to-all | bytes 2097152 | tf_op jit(solution)/shard_map/cond/branch_1_fun/all_to_all | solution.py:168
  132.7 15.5 %all_to_all.16 = bf16[8,128,512]{2,1,0:T(8,128)(2,1)S(1)} all-to-all(bf16[8,128,512]{2,1,0:T(8,128)(2,1)S(1)} %broadcast_in_dim.15), channel_id=1, replica_groups=mesh['yl'=2,'zh'=4,'zl'=4,'yh'=2,'x'=4,'c'=2] {'yh','x'}, dimensions={0} | all-to-all | bytes 2097152 | tf_op jit(solution)/shard_map/all_to_all | solution.py:174
  149.3 1.9 %collective-permute-start.8 = (bf16[1024,256]{1,0:T(8,128)(2,1)}, bf16[1024,256]{1,0:T(8,128)(2,1)S(1)}, u32[]{:S(2)}, u32[]{:S(2)}) collective-permute-start(bf16[1024,256]{1,0:T(8,128)(2,1)} %get-tuple-element.25), channel_id=1, source_target_pairs={{0,1},{1,0},{2,3},{3,2},{4,5},{5,4},{6,7},{7,6},{8,9},{9,8},{10,11... | collective-permute-start | bytes 1572872 | tf_op jit(solution)/shard_map/ppermute | solution.py:42
  151.2 2.4 %collective-permute-start.7 = (bf16[1024,256]{1,0:T(8,128)(2,1)}, bf16[1024,256]{1,0:T(8,128)(2,1)S(1)}, u32[]{:S(2)}, u32[]{:S(2)}) collective-permute-start(bf16[1024,256]{1,0:T(8,128)(2,1)} %get-tuple-element.24), channel_id=1, source_target_pairs={{0,1},{1,0},{2,3},{3,2},{4,5},{5,4},{6,7},{7,6},{8,9},{9,8},{10,11... | collective-permute-start | bytes 1572872 | tf_op jit(solution)/shard_map/ppermute | solution.py:42
  153.6 1.3 constant_dynamic-slice_fusion
  155.6 2.9 %collective-permute-start.9 = (f32[256,256]{1,0:T(8,128)S(1)}, f32[256,256]{1,0:T(8,128)S(1)}, u32[]{:S(2)}, u32[]{:S(2)}) collective-permute-start(f32[256,256]{1,0:T(8,128)S(1)} %fusion.1), channel_id=1, source_target_pairs={{0,256},{256,0},{1,257},{257,1},{2,258},{258,2},{3,259},{259,3},{4... | collective-permute-start | bytes 786440 | tf_op jit(solution)/shard_map/ppermute | solution.py:42
  159.2 6.5 %collective-permute-done.9 = f32[256,256]{1,0:T(8,128)S(1)} collective-permute-done((f32[256,256]{1,0:T(8,128)S(1)}, f32[256,256]{1,0:T(8,128)S(1)}, u32[]{:S(2)}, u32[]{:S(2)}) %collective-permute-start.9) | collective-permute-done | bytes 262176 | tf_op jit(solution)/shard_map/ppermute | solution.py:42
  (40 shorter events, 9.1 us)
Async XLA Ops:
  6.5 15.1 %copy-start = (bf16[128,4096]{1,0:T(8,128)(2,1)S(1)}, bf16[128,4096]{1,0:T(8,128)(2,1)}, u32[]{:S(2)}) copy-start(bf16[128,4096]{1,0:T(8,128)(2,1)} %param.7) | copy-start | bytes 3145732
  6.5 21.2 %copy-start.1 = (bf16[2,512,256]{2,1,0:T(8,128)(2,1)S(1)}, bf16[2,512,256]{2,1,0:T(8,128)(2,1)}, u32[]{:S(2)}) copy-start(bf16[2,512,256]{2,1,0:T(8,128)(2,1)} %param.9) | copy-start | bytes 1572868
  6.5 102.3 %all-gather.5.cloned.1.call-start = ((), (), s32[]{:S(2)}) async-start(), calls=%async_computation.3 | async-start | bytes 4456448 | tf_op jit(solution)/shard_map/all_gather | solution.py:139
  7.5 11.4 %collective-permute-start = (bf16[128,256]{1,0:T(8,128)(2,1)S(1)}, bf16[128,256]{1,0:T(8,128)(2,1)S(1)}, u32[]{:S(2)}, u32[]{:S(2)}) collective-permute-start(bf16[128,256]{1,0:T(8,128)(2,1)S(1)} %get-tuple-element.33), channel_id=1, source_target_pairs={{0,256},{256,0},{1,257},{257,1},{2,258},{258,2},{3,259},{259,3},{4... | collective-permute-start | bytes 196616 | tf_op jit(solution)/shard_map/ppermute | solution.py:42
  14.0 5.0 %collective-permute-start.1 = (bf16[64,512]{1,0:T(8,128)(2,1)S(1)}, bf16[64,512]{1,0:T(8,128)(2,1)S(1)}, u32[]{:S(2)}, u32[]{:S(2)}) collective-permute-start(bf16[64,512]{1,0:T(8,128)(2,1)S(1)} %get-tuple-element.34), channel_id=1, source_target_pairs={{0,0},{1,256},{256,1},{257,257},{2,2},{3,258},{258,3},{259,259},{4... | collective-permute-start | bytes 196616 | tf_op jit(solution)/shard_map/ppermute | solution.py:131
  14.6 6.2 %collective-permute-start.2 = (bf16[64,512]{1,0:T(8,128)(2,1)S(1)}, bf16[64,512]{1,0:T(8,128)(2,1)S(1)}, u32[]{:S(2)}, u32[]{:S(2)}) collective-permute-start(bf16[64,512]{1,0:T(8,128)(2,1)S(1)} %get-tuple-element.35), channel_id=1, source_target_pairs={{0,256},{1,0},{256,257},{257,1},{2,258},{3,2},{258,259},{259,3},{4... | collective-permute-start | bytes 196616 | tf_op jit(solution)/shard_map/ppermute | solution.py:134
  21.6 132.0 %all-gather.7.cloned.1.call-start = ((), (), s32[]{:S(2)}) async-start(), calls=%async_computation.4 | async-start | bytes 1310720 | tf_op jit(solution)/shard_map/all_gather | solution.py:164
  23.4 6.3 %collective-permute-start.3 = (bf16[64,256]{1,0:T(8,128)(2,1)S(1)}, bf16[64,256]{1,0:T(8,128)(2,1)S(1)}, u32[]{:S(2)}, u32[]{:S(2)}) collective-permute-start(bf16[64,256]{1,0:T(8,128)(2,1)S(1)} %fusion.7), channel_id=1, source_target_pairs={{0,256},{256,0},{1,257},{257,1},{2,258},{258,2},{3,259},{259,3},{4... | collective-permute-start | bytes 98312 | tf_op jit(solution)/shard_map/ppermute | solution.py:42
  27.8 29.9 %collective-permute-start.4 = (bf16[512,256]{1,0:T(8,128)(2,1)S(1)}, bf16[512,256]{1,0:T(8,128)(2,1)S(1)}, u32[]{:S(2)}, u32[]{:S(2)}) collective-permute-start(bf16[512,256]{1,0:T(8,128)(2,1)S(1)} %get-tuple-element.31), channel_id=1, source_target_pairs={{0,256},{256,0},{1,257},{257,1},{2,258},{258,2},{3,259},{259,3},{4... | collective-permute-start | bytes 786440 | tf_op jit(solution)/shard_map/ppermute | solution.py:42
  92.6 6.9 %collective-permute-start.5 = (bf16[512,2048]{1,0:T(8,128)(2,1)}, bf16[512,2048]{1,0:T(8,128)(2,1)}, u32[]{:S(2)}, u32[]{:S(2)}) collective-permute-start(bf16[512,2048]{1,0:T(8,128)(2,1)} %bitcast.24), channel_id=1, source_target_pairs={{0,1},{1,0},{2,3},{3,2},{4,5},{5,4},{6,7},{7,6},{8,9},{9,8},{10,11... | collective-permute-start | bytes 6291464 | tf_op jit(solution)/shard_map/ppermute | solution.py:42
  94.6 4.9 %collective-permute-start.6 = (bf16[512,512]{1,0:T(8,128)(2,1)S(1)}, bf16[512,512]{1,0:T(8,128)(2,1)S(1)}, u32[]{:S(2)}, u32[]{:S(2)}) collective-permute-start(bf16[512,512]{1,0:T(8,128)(2,1)S(1)} %pad_maximum_fusion), channel_id=1, source_target_pairs={{0,1},{1,0},{2,3},{3,2},{4,5},{5,4},{6,7},{7,6},{8,9},{9,8},{10,11... | collective-permute-start | bytes 1572872 | tf_op jit(solution)/shard_map/ppermute | solution.py:42
  149.3 6.0 %collective-permute-start.8 = (bf16[1024,256]{1,0:T(8,128)(2,1)}, bf16[1024,256]{1,0:T(8,128)(2,1)S(1)}, u32[]{:S(2)}, u32[]{:S(2)}) collective-permute-start(bf16[1024,256]{1,0:T(8,128)(2,1)} %get-tuple-element.25), channel_id=1, source_target_pairs={{0,1},{1,0},{2,3},{3,2},{4,5},{5,4},{6,7},{7,6},{8,9},{9,8},{10,11... | collective-permute-start | bytes 1572872 | tf_op jit(solution)/shard_map/ppermute | solution.py:42
  151.2 7.6 %collective-permute-start.7 = (bf16[1024,256]{1,0:T(8,128)(2,1)}, bf16[1024,256]{1,0:T(8,128)(2,1)S(1)}, u32[]{:S(2)}, u32[]{:S(2)}) collective-permute-start(bf16[1024,256]{1,0:T(8,128)(2,1)} %get-tuple-element.24), channel_id=1, source_target_pairs={{0,1},{1,0},{2,3},{3,2},{4,5},{5,4},{6,7},{7,6},{8,9},{9,8},{10,11... | collective-permute-start | bytes 1572872 | tf_op jit(solution)/shard_map/ppermute | solution.py:42
  155.6 10.1 %collective-permute-start.9 = (f32[256,256]{1,0:T(8,128)S(1)}, f32[256,256]{1,0:T(8,128)S(1)}, u32[]{:S(2)}, u32[]{:S(2)}) collective-permute-start(f32[256,256]{1,0:T(8,128)S(1)} %fusion.1), channel_id=1, source_target_pairs={{0,256},{256,0},{1,257},{257,1},{2,258},{258,2},{3,259},{259,3},{4... | collective-permute-start | bytes 786440 | tf_op jit(solution)/shard_map/ppermute | solution.py:42
Sparse Core Ops, SparseCore 0:
  21.7 87.0 all-gather.4
  114.6 34.3 all-gather.6
